TPU v7x, 32 devices: a whole 2x2x4 slice. The times are simulated.
32 devices in a mesh: dom: 16 (over z, y, x), hid: 2 (over core).
Axes of the slice: x: 2, y: 2, z: 4, core: 2. Of those that a mesh axis runs over, the one named last changes fastest.
Arguments:
- features: bfloat16 [16384, 512], P('dom', 'hid'), may hold values from -6 to 6
- history: bfloat16 [16384, 512], P('dom', 'hid'), may hold values from -6 to 6
- remote_tiles: bfloat16 [16, 16, 128, 128], P('dom'), may hold values from -0.21875 to 0.21875
- remote_dst: int32 [16, 16], P('dom'), may hold values from 0 to 7
- serve_block: int32 [16, 16], P('dom'), may hold values from 0 to 7
- push_flag: int32 [16, 16], P('dom'), may hold values 0 or 1
- local_tiles: bfloat16 [16, 32, 128, 128], P('dom'), may hold values from -0.21875 to 0.21875
- local_src: int32 [16, 32], P('dom'), may hold values from 0 to 7
- local_dst: int32 [16, 32], P('dom'), may hold values from 0 to 7
- weight_in: bfloat16 [512, 512], P('hid'), may hold values from -0.25 to 0.25
- weight_out: bfloat16 [512, 512], P('hid'), may hold values from -0.25 to 0.25
- cotangent: bfloat16 [16384, 512], P('dom', 'hid'), may hold values from -6 to 6
Outputs:
- out: bfloat16 [16384, 512], P('dom', 'hid')
- grad_hidden: bfloat16 [16384, 512], P('dom', 'hid')
- grad_weight_in: float32 [512, 512], P('hid')
- grad_weight_out: float32 [512, 512], P('hid')
Inputs may be any that keep to these rules, and one draw needn't show every extreme that they name: `remote_dst`: local block indices. `serve_block`: local block indices. `local_src`: local block indices. `local_dst`: local block indices.
All inputs are finite; a program needn't handle non-finite values. No bound on the sum of `push_flag` on one device may be relied on, other than what follows from the above.
Results may differ from a plain program's by a relative error of at most 0.007.
Values may be sent and summed in bfloat16 or wider, within the bound.
No kernel may reach another device: no remote copies, remote signals or barrier semaphores. Data moves between devices by JAX's collectives and lax.ppermute only.
A program may use at most 128 MiB of HBM per device.

v0:
```python
import jax
import jax.numpy as jnp
from jax import lax
from jax.sharding import PartitionSpec as P


def one_hot(indices, count, kind):
    return (indices[..., None] == jnp.arange(count, dtype=jnp.int32)).astype(kind)


def local_forward(tiles, sources, targets, node_blocks):
    rows = jnp.take(node_blocks, sources, axis=0)
    inner = jnp.einsum("kij,kjf->kif", tiles, rows, preferred_element_type=jnp.float32)
    return jnp.einsum(
        "kb,kif->bif",
        one_hot(targets, node_blocks.shape[0], jnp.float32),
        inner,
        precision=lax.Precision.HIGHEST,
    )


def remote_forward(tiles, targets, received, count):
    peers, tile = (tiles.shape[0], tiles.shape[1])
    width = received.shape[2]
    group = min(16, peers)
    steps_count = peers // group

    def step(accum, items):
        tile_group, recv_group, target_group = items
        outer = jnp.einsum(
            "qij,qjf->qif", tile_group, recv_group, preferred_element_type=jnp.float32
        )
        hot = one_hot(target_group, count, jnp.float32)
        return (
            accum + jnp.einsum("qb,qif->bif", hot, outer, precision=lax.Precision.HIGHEST),
            None,
        )

    start = jnp.zeros((count, tile, width), jnp.float32)
    items = (
        tiles.reshape(steps_count, group, tile, tile),
        received.reshape(steps_count, group, tile, width),
        targets.reshape(steps_count, group),
    )
    total, _ = lax.scan(step, start, items)
    return total


def supply_rows(sending):
    return lax.all_to_all(sending, "dom", split_axis=0, concat_axis=0, tiled=True)


def project(values, weight):
    partial_sums = jnp.dot(values, weight, preferred_element_type=jnp.float32)
    return lax.psum_scatter(partial_sums, "hid", scatter_dimension=1, tiled=True)


def widen(values):
    return lax.all_gather(values, "hid", axis=1, tiled=True)


def per_device(
    features,
    history,
    remote_tiles,
    remote_dst,
    serve_block,
    push_flag,
    local_tiles,
    local_src,
    local_dst,
    weight_in,
    weight_out,
    cotangent,
):
    tile = remote_tiles.shape[-1]
    rows, width = features.shape
    count = rows // tile
    peers = remote_tiles.shape[1]
    tiles_remote = remote_tiles[0]
    targets_remote = remote_dst[0]
    served_ids = serve_block[0]
    flags = push_flag[0]
    tiles_local = local_tiles[0]
    sources_local = local_src[0]
    targets_local = local_dst[0]

    def aggregate(node_blocks, received):
        total = local_forward(tiles_local, sources_local, targets_local, node_blocks)
        total = total + remote_forward(tiles_remote, targets_remote, received, count)
        return total.reshape(rows, width).astype(jnp.bfloat16)

    feat_blocks = features.reshape(count, tile, width)
    z_first = aggregate(feat_blocks, supply_rows(jnp.take(feat_blocks, served_ids, axis=0)))
    pre_first = project(z_first, weight_in)
    hidden = jax.nn.silu(pre_first).astype(jnp.bfloat16)
    hidden_blocks = hidden.reshape(count, tile, width)
    hist_blocks = history.reshape(count, tile, width)
    fresh = (flags == 1)[:, None, None]
    sending = jnp.where(
        fresh,
        jnp.take(hidden_blocks, served_ids, axis=0),
        jnp.take(hist_blocks, served_ids, axis=0),
    )
    z_second = aggregate(hidden_blocks, supply_rows(sending))
    out = project(z_second, weight_out).astype(jnp.bfloat16)
    grad_full = widen(cotangent)
    grad_z = jnp.einsum(
        "rf,kf->rk", grad_full, weight_out, preferred_element_type=jnp.float32
    ).astype(jnp.bfloat16)
    grad_out_w = jnp.einsum("rk,rf->kf", z_second, grad_full, preferred_element_type=jnp.float32)
    grad_blocks = grad_z.reshape(count, tile, width)
    inner = jnp.einsum(
        "kji,kjf->kif",
        tiles_local,
        jnp.take(grad_blocks, targets_local, axis=0),
        preferred_element_type=jnp.float32,
    )
    grad_acc = jnp.einsum(
        "kb,kif->bif",
        one_hot(sources_local, count, jnp.float32),
        inner,
        precision=lax.Precision.HIGHEST,
    )
    outer = jnp.einsum(
        "qji,qjf->qif",
        tiles_remote,
        jnp.take(grad_blocks, targets_remote, axis=0),
        preferred_element_type=jnp.float32,
    ).astype(jnp.bfloat16)
    returned = lax.all_to_all(outer, "dom", split_axis=0, concat_axis=0, tiled=True)
    owner_hot = one_hot(served_ids, count, jnp.bfloat16) * flags.astype(jnp.bfloat16)[:, None]
    grad_acc = grad_acc + jnp.einsum(
        "qb,qif->bif", owner_hot, returned, preferred_element_type=jnp.float32
    )
    grad_acc = grad_acc.reshape(rows, width)
    sig = jax.nn.sigmoid(pre_first)
    grad_pre = (grad_acc * sig * (1.0 + pre_first * (1.0 - sig))).astype(jnp.bfloat16)
    grad_pre_full = widen(grad_pre)
    grad_in_w = jnp.einsum("rk,rf->kf", z_first, grad_pre_full, preferred_element_type=jnp.float32)
    summed_in, summed_out = lax.psum((grad_in_w, grad_out_w), "dom")
    scale = float(rows * peers) ** (-0.5)
    return (out, grad_acc.astype(jnp.bfloat16), summed_in * scale, summed_out * scale)


def solution(mesh):
    return jax.shard_map(
        per_device,
        mesh=mesh,
        in_specs=(
            P("dom", "hid"),
            P("dom", "hid"),
            P("dom", None, None, None),
            P("dom", None),
            P("dom", None),
            P("dom", None),
            P("dom", None, None, None),
            P("dom", None),
            P("dom", None),
            P("hid", None),
            P("hid", None),
            P("dom", "hid"),
        ),
        out_specs=(P("dom", "hid"), P("dom", "hid"), P("hid", None), P("hid", None)),
        check_vma=False,
    )
```

profile of v0, /device:TPU:0, one launch (start us, length us, event | category | flops | bytes accessed | tf_op | source)
XLA Modules:
  0.0 274.7 jit_solution(13679635931278011998)
XLA Ops:
  7.2 0.7 compare_select_fusion.3
  7.9 0.7 compare_and_fusion.3
  8.6 2.6 gather_fusion.1
  11.2 1.6 copy.32
  12.9 1.2 broadcast_select_fusion
  14.0 8.4 %all-to-all-start = ((bf16[16,128,256]{1,2,0:T(8,128)(2,1)}), bf16[16,128,256]{1,2,0:T(8,128)(2,1)}, u32[]{:S(2)}, u32[]{:S(2)}) async-start(bf16[16,128,256]{1,2,0:T(8,128)(2,1)} %broadcast_select_fusion), calls=%async_computation | async-start | bytes 2097152 | tf_op jit(solution)/shard_map/all_to_all | solution.py:50
  22.4 0.0 all-gather.3.cloned.1.call-start
  22.5 0.7 all-gather.3.cloned.1.call-update
  23.2 0.0 reduce-scatter.3.cloned.1.call-start
  23.2 2.0 gather_fusion
  25.3 4.4 %convolution_bitcast_fusion.2 = f32[32,128,256]{1,2,0:T(8,128)} fusion(bf16[32,128,256]{2,1,0:T(8,128)(2,1)} %gather_fusion, pred[32]{0:T(512)(128)(4,1)S(1)} %compare_and_fusion.2, bf16[1,32,128,128]{3,2,1,0:T(8,128)(2,1)S(1)} %copy-done), kind=kOutput, calls=%fused_computation.9 | convolution fusion | flops 269484032 | bytes 7340064 | tf_op jit(solution)/shard_map/kij,kjf->kif/dot_general | solution.py:13
  29.7 5.6 %copy.31 = f32[32,128,256]{2,0,1:T(8,128)} copy(f32[32,128,256]{1,2,0:T(8,128)} %convolution_bitcast_fusion.2) | data formatting | bytes 8388608 | tf_op jit(solution)/shard_map/kij,kjf->kif/dot_general | solution.py:13
  35.3 4.6 %fusion.27 = f32[8,128,256]{2,0,1:T(8,128)} fusion(f32[32,128,256]{2,0,1:T(8,128)} %copy.31, s32[32]{0:T(128)S(1)} %bitcast.101), kind=kOutput, calls=%fused_computation.59 | convolution fusion | flops 100663552 | bytes 5243008 | tf_op jit(solution)/shard_map/kb,kif->bif/dot_general | solution.py:14
  39.8 7.1 %all-to-all-done = bf16[16,128,256]{1,2,0:T(8,128)(2,1)} async-done(((bf16[16,128,256]{1,2,0:T(8,128)(2,1)}), bf16[16,128,256]{1,2,0:T(8,128)(2,1)}, u32[]{:S(2)}, u32[]{:S(2)}) %all-to-all-start) | async-done | bytes 1048608 | tf_op jit(solution)/shard_map/all_to_all | solution.py:50
  46.9 1.8 convolution_bitcast_fusion.4
  48.7 2.1 copy.33
  50.8 2.7 fusion.7
  53.5 0.1 copy.34
  53.7 0.8 copy-done.3
  54.5 1.8 fusion.51
  56.3 0.0 all-gather.3.cloned.1.call-done
  56.4 1.7 convolution_convert_fusion.1
  58.1 0.6 gather_fusion.6
  58.7 1.6 fusion.6
  60.3 2.3 copy.44
  62.6 5.9 %all-to-all-start.2 = ((bf16[16,128,256]{2,1,0:T(8,128)(2,1)}), bf16[16,128,256]{2,1,0:T(8,128)(2,1)}, u32[]{:S(2)}, u32[]{:S(2)}) async-start(bf16[16,128,256]{2,1,0:T(8,128)(2,1)} %copy.44), calls=%async_computation.4 | async-start | bytes 2097152 | tf_op jit(solution)/shard_map/all_to_all | solution.py:131
  68.5 1.7 gather_fusion.4
  70.2 1.3 copy.38
  71.5 2.0 gather_fusion.5
  73.6 4.4 %convolution_bitcast_fusion = f32[32,128,256]{1,2,0:T(8,128)} fusion(bf16[32,128,256]{2,1,0:T(8,128)(2,1)} %gather_fusion.5, pred[32]{0:T(512)(128)(4,1)S(1)} %compare_and_fusion.1, bf16[1,32,128,128]{3,2,1,0:T(8,128)(2,1)S(1)} %copy-done), kind=kOutput, calls=%fused_computation.7 | convolution fusion | flops 269484032 | bytes 7340064 | tf_op jit(solution)/shard_map/kji,kjf->kif/dot_general | solution.py:113
  77.9 5.5 %copy.42 = f32[32,128,256]{2,0,1:T(8,128)} copy(f32[32,128,256]{1,2,0:T(8,128)} %convolution_bitcast_fusion) | data formatting | bytes 8388608 | tf_op jit(solution)/shard_map/kji,kjf->kif/dot_general | solution.py:113
  83.4 3.6 %fusion.33 = f32[8,128,256]{2,0,1:T(8,128)S(1)} fusion(f32[32,128,256]{2,0,1:T(8,128)} %copy.42, s32[32]{0:T(128)S(1)} %bitcast.106), kind=kOutput, calls=%fused_computation.62 | convolution fusion | flops 100663552 | bytes 5243008 | tf_op jit(solution)/shard_map/kb,kif->bif/dot_general | solution.py:119
  87.1 4.4 %all-to-all-done.2 = bf16[16,128,256]{2,1,0:T(8,128)(2,1)} async-done(((bf16[16,128,256]{2,1,0:T(8,128)(2,1)}), bf16[16,128,256]{2,1,0:T(8,128)(2,1)}, u32[]{:S(2)}, u32[]{:S(2)}) %all-to-all-start.2) | async-done | bytes 1048608 | tf_op jit(solution)/shard_map/all_to_all | solution.py:131
  91.5 1.9 convolution_add_fusion
  93.4 0.3 copy.46
  93.7 0.0 reduce-scatter.3.cloned.1.call-done
  93.8 2.5 fusion.10
  96.3 1.6 gather_fusion.3
  97.9 2.3 copy.37
  100.2 2.8 %select_select_fusion = bf16[16,128,256]{1,2,0:T(8,128)(2,1)} fusion(bf16[16,128,256]{1,2,0:T(8,128)(2,1)} %copy.38, bf16[16,128,256]{1,2,0:T(8,128)(2,1)} %copy.37, pred[16]{0:T(512)(128)(4,1)S(1)} %compare_and_fusion.3, pred[16]{0:T(512)(128)(4,1)S(1)} %compare_bitcast_fusion), kind=kLoop, calls=%fused_computation.35 | loop fusion | flops 1572864 | bytes 3145760 | tf_op jit(solution)/shard_map/jit(_where)/select_n | solution.py:100
  103.0 6.2 %all-to-all-start.1 = ((bf16[16,128,256]{1,2,0:T(8,128)(2,1)}), bf16[16,128,256]{1,2,0:T(8,128)(2,1)}, u32[]{:S(2)}, u32[]{:S(2)}) async-start(bf16[16,128,256]{1,2,0:T(8,128)(2,1)} %select_select_fusion), calls=%async_computation.2 | async-start | bytes 2097152 | tf_op jit(solution)/shard_map/all_to_all | solution.py:50
  109.2 0.0 all-gather.5.cloned.1.call-start
  109.2 0.7 all-gather.5.cloned.1.call-update
  109.9 0.0 all-reduce.3.cloned.1.call-start
  110.0 2.0 gather_fusion.2
  112.0 4.4 %convolution_bitcast_fusion.1 = f32[32,128,256]{1,2,0:T(8,128)} fusion(bf16[32,128,256]{2,1,0:T(8,128)(2,1)} %gather_fusion.2, pred[32]{0:T(512)(128)(4,1)S(1)} %compare_and_fusion.2, bf16[1,32,128,128]{3,2,1,0:T(8,128)(2,1)S(1)} %copy-done), kind=kOutput, calls=%fused_computation.8 | convolution fusion | flops 269484032 | bytes 7340064 | tf_op jit(solution)/shard_map/kij,kjf->kif/dot_general | solution.py:13
  116.4 5.5 %copy.36 = f32[32,128,256]{2,0,1:T(8,128)} copy(f32[32,128,256]{1,2,0:T(8,128)} %convolution_bitcast_fusion.1) | data formatting | bytes 8388608 | tf_op jit(solution)/shard_map/kij,kjf->kif/dot_general | solution.py:13
  121.9 4.7 %fusion.25 = f32[8,128,256]{2,0,1:T(8,128)} fusion(f32[32,128,256]{2,0,1:T(8,128)} %copy.36, s32[32]{0:T(128)S(1)} %bitcast.102), kind=kOutput, calls=%fused_computation.58 | convolution fusion | flops 100663552 | bytes 5243008 | tf_op jit(solution)/shard_map/kb,kif->bif/dot_general | solution.py:14
  126.6 2.5 fusion.53
  129.1 3.8 %all-to-all-done.1 = bf16[16,128,256]{1,2,0:T(8,128)(2,1)} async-done(((bf16[16,128,256]{1,2,0:T(8,128)(2,1)}), bf16[16,128,256]{1,2,0:T(8,128)(2,1)}, u32[]{:S(2)}, u32[]{:S(2)}) %all-to-all-start.1) | async-done | bytes 1048608 | tf_op jit(solution)/shard_map/all_to_all | solution.py:50
  132.8 3.0 %convolution_bitcast_fusion.3 = f32[16,128,256]{1,2,0:T(8,128)} fusion(bf16[16,128,256]{1,2,0:T(8,128)(2,1)} %all-to-all-done.1, bf16[1,16,128,128]{3,2,1,0:T(8,128)(2,1)S(1)} %copy-done.2), kind=kOutput, calls=%fused_computation.16 | convolution fusion | flops 134217728 | bytes 3670016 | tf_op jit(solution)/shard_map/while/body/eval_jaxpr/qij,qjf->qif/dot_general | solution.py:30
  135.8 3.1 %copy.39 = f32[16,128,256]{2,0,1:T(8,128)} copy(f32[16,128,256]{1,2,0:T(8,128)} %convolution_bitcast_fusion.3) | data formatting | bytes 4194304 | tf_op jit(solution)/shard_map/while/body/eval_jaxpr/qij,qjf->qif/dot_general | solution.py:30
  138.9 2.8 %fusion.8 = bf16[8,128,256]{2,0,1:T(8,128)(2,1)S(1)} fusion(f32[8,128,256]{2,0,1:T(8,128)} %fusion.25, f32[16,128,256]{2,0,1:T(8,128)} %copy.39, s32[16]{0:T(128)S(1)} %bitcast.104), kind=kOutput, calls=%fused_computation.24 | convolution fusion | flops 50856064 | bytes 3670080 | tf_op jit(solution)/shard_map/while/body/eval_jaxpr/qb,qif->bif/dot_general | solution.py:35
  141.7 0.1 copy.40
  141.8 1.3 fusion.54
  143.0 0.0 all-reduce.3.cloned.1.call-update
  143.1 0.0 reduce-scatter.5.cloned.1.call-start
  143.1 1.8 fusion.52
  144.9 0.0 reduce-scatter.5.cloned.1.call-update
  144.9 0.8 bitcast_convert_fusion
  145.7 109.6 %all-reduce.3.cloned.1.call-done = (f32[256,512]{1,0:T(8,128)}, f32[256,512]{1,0:T(8,128)}) async-done(((f32[256,512]{1,0:T(8,128)}, f32[256,512]{1,0:T(8,128)}), (f32[256,512]{1,0:T(8,128)}, f32[256,512]{1,0:T(8,128)})) %all-reduce.3.cloned.1.call-update) | async-done | bytes 1048592 | tf_op jit(solution)/shard_map/psum | solution.py:141
  255.3 2.3 broadcast_multiply_fusion
  257.6 8.5 %reduce-scatter.5.cloned.1.call-done = f32[1024,256]{1,0:T(8,128)} async-done(((f32[1024,512]{1,0:T(8,128)}), f32[1024,256]{1,0:T(8,128)}) %reduce-scatter.5.cloned.1.call-update) | async-done | bytes 1048592 | tf_op jit(solution)/shard_map/reduce_scatter | solution.py:55
  266.1 2.1 convert_element_type.56
  (39 shorter events, 0.2 us)
Async XLA Ops:
  7.2 18.1 %copy-start = (bf16[1,32,128,128]{3,2,1,0:T(8,128)(2,1)S(1)}, bf16[1,32,128,128]{3,2,1,0:T(8,128)(2,1)}, u32[]{:S(2)}) copy-start(bf16[1,32,128,128]{3,2,1,0:T(8,128)(2,1)} %param.22) | copy-start | bytes 3145732
  12.9 10.3 %copy-start.11 = (s32[1,32]{1,0:T(1,128)S(1)}, s32[1,32]{1,0:T(1,128)}, u32[]{:S(2)}) copy-start(s32[1,32]{1,0:T(1,128)} %param.23) | copy-start | bytes 388
  12.9 10.4 %copy-start.1 = (bf16[1024,256]{1,0:T(8,128)(2,1)S(1)}, bf16[1024,256]{1,0:T(8,128)(2,1)}, u32[]{:S(2)}) copy-start(bf16[1024,256]{1,0:T(8,128)(2,1)} %param.16) | copy-start | bytes 1572868
  14.0 32.9 %all-to-all-start = ((bf16[16,128,256]{1,2,0:T(8,128)(2,1)}), bf16[16,128,256]{1,2,0:T(8,128)(2,1)}, u32[]{:S(2)}, u32[]{:S(2)}) async-start(bf16[16,128,256]{1,2,0:T(8,128)(2,1)} %broadcast_select_fusion), calls=%async_computation | async-start | bytes 2097152 | tf_op jit(solution)/shard_map/all_to_all | solution.py:50
  22.4 33.9 %all-gather.3.cloned.1.call-start = ((), (), s32[]{:S(2)}) async-start(), calls=%async_computation.7 | async-start | bytes 1572864 | tf_op jit(solution)/shard_map/all_gather | solution.py:59
  23.2 70.6 %reduce-scatter.3.cloned.1.call-start = ((), (), s32[]{:S(2)}) async-start(), calls=%async_computation.5 | async-start | bytes 3145728 | tf_op jit(solution)/shard_map/reduce_scatter | solution.py:55
  29.7 5.6 %copy-start.8 = (s32[1,32]{1,0:T(1,128)S(1)}, s32[1,32]{1,0:T(1,128)}, u32[]{:S(2)}) copy-start(s32[1,32]{1,0:T(1,128)} %param.24) | copy-start | bytes 388
  48.7 2.1 copy-start.9
  50.8 3.6 %copy-start.7 = (bf16[256,512]{1,0:T(8,128)(2,1)S(1)}, bf16[256,512]{1,0:T(8,128)(2,1)}, u32[]{:S(2)}) copy-start(bf16[256,512]{1,0:T(8,128)(2,1)} %param.25) | copy-start | bytes 786436
  53.7 0.8 copy-start.3
  54.5 1.9 copy-start.6
  56.3 2.5 copy-start.2
  62.6 28.9 %all-to-all-start.2 = ((bf16[16,128,256]{2,1,0:T(8,128)(2,1)}), bf16[16,128,256]{2,1,0:T(8,128)(2,1)}, u32[]{:S(2)}, u32[]{:S(2)}) async-start(bf16[16,128,256]{2,1,0:T(8,128)(2,1)} %copy.44), calls=%async_computation.4 | async-start | bytes 2097152 | tf_op jit(solution)/shard_map/all_to_all | solution.py:131
  68.5 3.0 %copy-start.12 = (s32[1,16]{1,0:T(1,128)S(1)}, s32[1,16]{1,0:T(1,128)}, u32[]{:S(2)}) copy-start(s32[1,16]{1,0:T(1,128)} %param.21) | copy-start | bytes 196
  83.4 8.1 %copy-start.10 = (s32[1,16]{1,0:T(1,128)S(1)}, s32[1,16]{1,0:T(1,128)}, u32[]{:S(2)}) copy-start(s32[1,16]{1,0:T(1,128)} %param.20) | copy-start | bytes 196
  103.0 29.8 %all-to-all-start.1 = ((bf16[16,128,256]{1,2,0:T(8,128)(2,1)}), bf16[16,128,256]{1,2,0:T(8,128)(2,1)}, u32[]{:S(2)}, u32[]{:S(2)}) async-start(bf16[16,128,256]{1,2,0:T(8,128)(2,1)} %select_select_fusion), calls=%async_computation.2 | async-start | bytes 2097152 | tf_op jit(solution)/shard_map/all_to_all | solution.py:50
  109.2 17.4 %all-gather.5.cloned.1.call-start = ((), (), s32[]{:S(2)}) async-start(), calls=%async_computation.8 | async-start | bytes 1572864 | tf_op jit(solution)/shard_map/all_gather | solution.py:59
  109.9 145.4 %all-reduce.3.cloned.1.call-start = ((), (), s32[]{:S(2)}) async-start(), calls=%async_computation.9 | async-start | bytes 2097152 | tf_op jit(solution)/shard_map/psum | solution.py:141
  121.9 4.7 %copy-start.4 = (bf16[8,128,256]{2,1,0:T(8,128)(2,1)S(1)}, bf16[8,128,256]{2,1,0:T(8,128)(2,1)}, u32[]{:S(2)}) copy-start(bf16[8,128,256]{2,1,0:T(8,128)(2,1)} %copy-done.3) | copy-start | bytes 1572868
  138.9 2.9 %copy-start.5 = (bf16[1024,512]{1,0:T(8,128)(2,1)S(1)}, bf16[1024,512]{1,0:T(8,128)(2,1)}, u32[]{:S(2)}) copy-start(bf16[1024,512]{1,0:T(8,128)(2,1)} %all-gather.3.cloned.1.call-done) | copy-start | bytes 3145732
  143.1 123.0 %reduce-scatter.5.cloned.1.call-start = ((), (), s32[]{:S(2)}) async-start(), calls=%async_computation.6 | async-start | bytes 3145728 | tf_op jit(solution)/shard_map/reduce_scatter | solution.py:55
Sparse Core Ops, SparseCore 0:
  24.8 10.2 all-gather.2
  56.4 9.7 reduce-scatter.2
  112.2 10.2 all-gather.4
  143.2 112.1 all-reduce.2
  257.5 8.5 reduce-scatter.4
where the time goes:
time: 276 us; the launch traced here: 275 us
  waiting for transfers between devices  135 us (49%)
  matrix products  48.8 us (18%)
  local copies, waits for them, and re-layouts  43.3 us (16%)
  starting transfers between devices  20.6 us (7%)
  between operations  14.1 us (5%)
  other arithmetic  13.1 us (5%)
    psum x1, waiting for transfers between devices, per_device(): summed_in, summed_out = lax.psum((grad_in_w, grad_out_w), 'dom')  110 us
    all_to_all x2, starting transfers between devices, supply_rows(): lax.all_to_all(sending, 'dom', split_axis=0, concat_axis=0, tiled=True)  14.6 us
    dot_general x2, local copies, waits for them, and re-layouts, local_forward(): jnp.einsum('kij,kjf->kif', tiles, rows, preferred_element_type=jnp.float32)  11.1 us
    all_to_all x2, waiting for transfers between devices, supply_rows(): lax.all_to_all(sending, 'dom', split_axis=0, concat_axis=0, tiled=True)  10.8 us
    dot_general x2, matrix products, local_forward(): jnp.einsum('kb,kif->bif', one_hot(targets, node_blocks.shape[0], jnp.floa...  9.25 us
    dot_general x2, matrix products, local_forward(): jnp.einsum('kij,kjf->kif', tiles, rows, preferred_element_type=jnp.float32)  8.76 us
    reduce_scatter x2, waiting for transfers between devices, project(): lax.psum_scatter(partial_sums, 'hid', scatter_dimension=1, tiled=True)  8.49 us
    all_to_all x1, starting transfers between devices, per_device(): lax.all_to_all(outer, 'dom', split_axis=0, concat_axis=0, tiled=True)  5.87 us
  transfers between devices with their start and end apart: 8, of which 5 were waited for; matrix products, arithmetic and copies ran while one was open for 28% of the time, Pallas kernels for 0%

commit v1 on v0

v1 whole, which is shorter than its diff:
```python
import functools

import jax
import jax.numpy as jnp
from jax import lax
from jax.experimental import pallas as pl
from jax.experimental.pallas import tpu as pltpu
from jax.sharding import PartitionSpec as P

BF16 = jnp.bfloat16
F32 = jnp.float32
VMEM_BYTES = 40 * 1024 * 1024
SWAP = ((0, 1), (1, 0))


def dot(a, b):
    return jnp.dot(a, b, preferred_element_type=F32)


def dot_t(a, b):
    return lax.dot_general(a, b, (((0,), (0,)), ((), ())), preferred_element_type=F32)


def dot_nt(a, b):
    return lax.dot_general(a, b, (((1,), (1,)), ((), ())), preferred_element_type=F32)


def call(body, scalars, arrays, grid, in_specs, out_specs, out_shape, scratch=(), flops=0, name=None):
    moved = sum(a.size * a.dtype.itemsize for a in arrays)
    moved += sum(s.size * s.dtype.itemsize for s in jax.tree.leaves(out_shape))
    return pl.pallas_call(
        body,
        grid_spec=pltpu.PrefetchScalarGridSpec(
            num_scalar_prefetch=len(scalars),
            grid=grid,
            in_specs=in_specs,
            out_specs=out_specs,
            scratch_shapes=list(scratch),
        ),
        out_shape=out_shape,
        compiler_params=pltpu.CompilerParams(vmem_limit_bytes=VMEM_BYTES),
        cost_estimate=pl.CostEstimate(flops=int(flops), bytes_accessed=int(moved), transcendentals=0),
        name=name,
    )(*scalars, *arrays)


def whole(shape):
    return pl.BlockSpec(shape, lambda i, *_: (0,) * len(shape))


def lead(shape):
    return pl.BlockSpec(shape, lambda i, *_: (i,) + (0,) * (len(shape) - 1))


def group_of(peers):
    return 8 if peers % 8 == 0 else 1


def pick_blocks(ids, node_blocks):
    peers = ids.shape[0]
    _, tile, width = node_blocks.shape
    group = group_of(peers)

    def body(ids_ref, nodes_ref, out_ref):
        step = pl.program_id(0)
        for j in range(group):
            out_ref[j] = nodes_ref[ids_ref[step * group + j]]

    return call(
        body, (ids,), (node_blocks,), (peers // group,),
        [whole(node_blocks.shape)], lead((group, tile, width)),
        jax.ShapeDtypeStruct((peers, tile, width), node_blocks.dtype), name="pick_blocks",
    )


def remote_back(targets, tiles, grads):
    peers, tile, _ = tiles.shape
    width = grads.shape[2]
    group = group_of(peers)

    def body(ids_ref, tiles_ref, grads_ref, out_ref):
        step = pl.program_id(0)
        for j in range(group):
            out_ref[j] = dot_t(tiles_ref[j], grads_ref[ids_ref[step * group + j]]).astype(BF16)

    return call(
        body, (targets,), (tiles, grads), (peers // group,),
        [lead((group, tile, tile)), whole(grads.shape)], lead((group, tile, width)),
        jax.ShapeDtypeStruct((peers, tile, width), BF16),
        flops=2 * peers * tile * tile * width, name="remote_back",
    )


def local_both(sources, targets, tiles, nodes, grads):
    many, tile, _ = tiles.shape
    group = group_of(many)

    def body(src_ref, dst_ref, tiles_ref, nodes_ref, grads_ref, fwd_ref, bwd_ref):
        step = pl.program_id(0)

        @pl.when(step == 0)
        def _():
            fwd_ref[...] = jnp.zeros_like(fwd_ref)
            bwd_ref[...] = jnp.zeros_like(bwd_ref)

        for j in range(group):
            src = src_ref[step * group + j]
            dst = dst_ref[step * group + j]
            fwd_ref[dst] += dot(tiles_ref[j], nodes_ref[src])
            bwd_ref[src] += dot_t(tiles_ref[j], grads_ref[dst])

    shape = jax.ShapeDtypeStruct(nodes.shape, F32)
    return call(
        body, (sources, targets), (tiles, nodes, grads), (many // group,),
        [lead((group, tile, tile)), whole(nodes.shape), whole(grads.shape)],
        [whole(nodes.shape)] * 2, [shape, shape],
        flops=4 * many * tile * tile * nodes.shape[2], name="local_both",
    )


def local_forward(sources, targets, tiles, nodes):
    many, tile, _ = tiles.shape
    group = group_of(many)

    def body(src_ref, dst_ref, tiles_ref, nodes_ref, fwd_ref):
        step = pl.program_id(0)

        @pl.when(step == 0)
        def _():
            fwd_ref[...] = jnp.zeros_like(fwd_ref)

        for j in range(group):
            src = src_ref[step * group + j]
            dst = dst_ref[step * group + j]
            fwd_ref[dst] += dot(tiles_ref[j], nodes_ref[src])

    return call(
        body, (sources, targets), (tiles, nodes), (many // group,),
        [lead((group, tile, tile)), whole(nodes.shape)],
        whole(nodes.shape), jax.ShapeDtypeStruct(nodes.shape, F32),
        flops=2 * many * tile * tile * nodes.shape[2], name="local_forward",
    )


def remote_forward(targets, tiles, received, base):
    peers, tile, _ = tiles.shape
    width = received.shape[2]
    group = group_of(peers)
    steps = peers // group

    def body(dst_ref, tiles_ref, recv_ref, base_ref, out_ref, acc_ref):
        step = pl.program_id(0)

        @pl.when(step == 0)
        def _():
            acc_ref[...] = base_ref[...]

        for j in range(group):
            acc_ref[dst_ref[step * group + j]] += dot(tiles_ref[j], recv_ref[j])

        @pl.when(step == steps - 1)
        def _():
            out_ref[...] = acc_ref[...].astype(BF16)

    return call(
        body, (targets,), (tiles, received, base), (steps,),
        [lead((group, tile, tile)), lead((group, tile, width)), whole(base.shape)],
        whole(base.shape), jax.ShapeDtypeStruct(base.shape, BF16),
        [pltpu.VMEM(base.shape, F32)],
        flops=2 * peers * tile * tile * width, name="remote_forward",
    )


def middle(ids, flags, z_mine, z_other, w_in, w_out, hist_out):
    rows, half = z_mine.shape
    peers = ids.shape[0]
    count, tile, _ = hist_out.shape
    per = 2 if count % 2 == 0 else 1
    steps = count // per
    span = per * tile

    def body(ids_ref, flag_ref, zm_ref, zo_ref, wi_ref, wo_ref, hw_ref, pre_ref, hid_ref, prod_ref, send_ref):
        step = pl.program_id(0)
        pre = dot(zm_ref[...], wi_ref[:half]) + dot(zo_ref[...], wi_ref[half:])
        pre_ref[...] = pre
        hidden = (pre * (1.0 / (1.0 + jnp.exp(-pre)))).astype(BF16)
        hid_ref[...] = hidden
        prod = dot(hidden, wo_ref[:, :half]).astype(BF16)
        for j in range(per):
            prod_ref[step * per + j] = prod[j * tile : (j + 1) * tile]

        @pl.when(step == steps - 1)
        def _():
            for p in range(peers):
                fresh = flag_ref[p] == 1
                block = ids_ref[p]

                @pl.when(fresh)
                def _():
                    send_ref[p] = prod_ref[block]

                @pl.when(jnp.logical_not(fresh))
                def _():
                    send_ref[p] = hw_ref[block]

    return call(
        body, (ids, flags), (z_mine, z_other, w_in, w_out, hist_out), (steps,),
        [lead((span, half)), lead((span, half)), whole(w_in.shape), whole(w_out.shape), whole(hist_out.shape)],
        [lead((span, 2 * half)), lead((span, 2 * half)), whole(hist_out.shape), whole((peers, tile, half))],
        [
            jax.ShapeDtypeStruct((rows, 2 * half), F32),
            jax.ShapeDtypeStruct((rows, 2 * half), BF16),
            jax.ShapeDtypeStruct(hist_out.shape, BF16),
            jax.ShapeDtypeStruct((peers, tile, half), BF16),
        ],
        flops=12 * rows * half * half, name="middle",
    )


def gather_grads(ids, flags, returned, base):
    peers, tile, width = returned.shape
    count = base.shape[0]
    group = group_of(peers)
    steps = peers // group

    def body(ids_ref, flag_ref, ret_ref, base_ref, out_ref, acc_ref):
        step = pl.program_id(0)

        @pl.when(step == 0)
        def _():
            acc_ref[0] = base_ref[...]
            acc_ref[1] = jnp.zeros_like(base_ref)

        for j in range(group):
            p = step * group + j
            side = jnp.where(flag_ref[p] == 1, 0, 1)
            acc_ref[side, ids_ref[p]] += ret_ref[j].astype(F32)

        @pl.when(step == steps - 1)
        def _():
            out_ref[...] = acc_ref[...].astype(BF16)

    both = (2,) + base.shape
    return call(
        body, (ids, flags), (returned, base), (steps,),
        [lead((group, tile, width)), whole(base.shape)],
        whole(both), jax.ShapeDtypeStruct(both, BF16),
        [pltpu.VMEM(both, F32)], name="gather_grads",
    )


def chunking(peers, total, width):
    row_chunks = min(peers, total // 16)
    col_chunks = peers // row_chunks
    return row_chunks, col_chunks, total // row_chunks, width // col_chunks


def backward(place, sums_mine, sums_other, hidden, history, z_mine, pre, w_out, peers):
    _, rows, half = sums_mine.shape
    step_rows = rows // 4
    row_chunks, col_chunks, chunk_rows, chunk_cols = chunking(peers, 2 * half, 2 * half)

    def body(place_ref, sm_ref, so_ref, hid_ref, hist_ref, z_ref, pre_ref, wo_ref, gh_ref, chunk_ref, acc_ref):
        step = pl.program_id(0)
        me, side = place_ref[0], place_ref[1]

        @pl.when(step == 0)
        def _():
            acc_ref[...] = jnp.zeros_like(acc_ref)

        dh = dot_nt(sm_ref[0], wo_ref[:, :half]) + dot_nt(so_ref[0], wo_ref[:, half:])
        gh_ref[...] = dh[:, :half].astype(BF16)
        pre = pre_ref[...]
        s = 1.0 / (1.0 + jnp.exp(-pre))
        dpre = (dh * s * (1.0 + pre * (1.0 - s))).astype(BF16)
        z = z_ref[...]
        own = pl.ds(pl.multiple_of(side * half, half), half)
        far = pl.ds(pl.multiple_of((1 - side) * half, half), half)
        acc_ref[:half, own] += dot_t(z, dpre[:, :half])
        acc_ref[:half, far] += dot_t(z, dpre[:, half:])
        hid, hist = hid_ref[...], hist_ref[...]
        acc_ref[half:, own] += dot_t(hid, sm_ref[0]) + dot_t(hist, sm_ref[1])
        acc_ref[half:, far] += dot_t(hid, so_ref[0]) + dot_t(hist, so_ref[1])

        @pl.when(step == 3)
        def _():
            for c in range(peers):
                r, k = c // col_chunks, c % col_chunks
                piece = acc_ref[r * chunk_rows : (r + 1) * chunk_rows, k * chunk_cols : (k + 1) * chunk_cols]
                chunk_ref[c ^ me] = piece.astype(BF16)

    sums_spec = pl.BlockSpec((2, step_rows, half), lambda i, *_: (0, i, 0))
    return call(
        body, (place,), (sums_mine, sums_other, hidden, history, z_mine, pre, w_out), (4,),
        [
            sums_spec, sums_spec, lead((step_rows, half)), lead((step_rows, half)),
            lead((step_rows, half)), lead((step_rows, 2 * half)), whole(w_out.shape),
        ],
        [lead((step_rows, half)), whole((peers, chunk_rows, chunk_cols))],
        [
            jax.ShapeDtypeStruct((rows, half), BF16),
            jax.ShapeDtypeStruct((peers, chunk_rows, chunk_cols), BF16),
        ],
        [pltpu.VMEM((2 * half, 2 * half), F32)],
        flops=20 * rows * half * half, name="backward",
    )


def finish_weights(place, chunks, half, scale):
    peers, chunk_rows, chunk_cols = chunks.shape
    _, col_chunks, _, _ = chunking(peers, 2 * half, 2 * half)

    def body(place_ref, chunk_ref, in_ref, out_ref):
        me = place_ref[0]
        for c in range(peers):
            r, k = (c // col_chunks) * chunk_rows, c % col_chunks
            piece = chunk_ref[c ^ me].astype(F32) * scale
            cols = slice(k * chunk_cols, (k + 1) * chunk_cols)
            if r < half:
                in_ref[r : r + chunk_rows, cols] = piece
            else:
                out_ref[r - half : r - half + chunk_rows, cols] = piece

    shape = jax.ShapeDtypeStruct((half, 2 * half), F32)
    return call(
        body, (place,), (chunks,), (1,), [whole(chunks.shape)],
        [whole(shape.shape)] * 2, [shape, shape], name="finish_weights",
    )


def stages(peers):
    found, stride = [], 1
    while stride < peers:
        radix = min(4, peers // stride)
        found.append((stride, radix))
        stride *= radix
    return found


def hop(value, peers, offset):
    return lax.ppermute(value, "dom", [(i, i ^ offset) for i in range(peers)])


def sum_over_dom(chunks):
    peers, chunk_rows, chunk_cols = chunks.shape
    plan = stages(peers)
    held = chunks
    for stride, radix in plan:
        parts = held.reshape(-1, radix, chunk_rows, chunk_cols)
        arrived = [hop(parts[:, t], peers, t * stride) for t in range(1, radix)]
        total = parts[:, 0].astype(F32)
        for piece in arrived:
            total = total + piece.astype(F32)
        held = total.astype(BF16)
    held = held.reshape(1, chunk_rows, chunk_cols)
    for stride, radix in reversed(plan):
        arrived = [held] + [hop(held, peers, t * stride) for t in range(1, radix)]
        held = jnp.stack(arrived, axis=1).reshape(-1, chunk_rows, chunk_cols)
    return held


def exchange(sending):
    return lax.all_to_all(sending, "dom", split_axis=0, concat_axis=0, tiled=True)


def swap(value):
    return lax.ppermute(value, "hid", SWAP)


def per_device(
    features,
    history,
    remote_tiles,
    remote_dst,
    serve_block,
    push_flag,
    local_tiles,
    local_src,
    local_dst,
    weight_in,
    weight_out,
    cotangent,
):
    tile = remote_tiles.shape[-1]
    rows, half = features.shape
    count = rows // tile
    peers = remote_tiles.shape[1]
    tiles_remote, tiles_local = remote_tiles[0], local_tiles[0]
    targets_remote, served_ids, flags = remote_dst[0], serve_block[0], push_flag[0]
    sources_local, targets_local = local_src[0], local_dst[0]
    side = lax.axis_index("hid")
    place = jnp.stack([lax.axis_index("dom"), side]).astype(jnp.int32)

    def blocks(values):
        return values.reshape(count, tile, half)

    def own_first(weight):
        joined = jnp.concatenate([weight, swap(weight)], axis=0)
        turned = jnp.concatenate([joined[:, half:], joined[:, :half]], axis=1)
        return jnp.where(side == 0, joined, turned)

    feat_blocks, grad_blocks = blocks(features), blocks(cotangent)
    received = exchange(pick_blocks(served_ids, feat_blocks))
    back = remote_back(targets_remote, tiles_remote, grad_blocks)
    base_forward, base_back = local_both(sources_local, targets_local, tiles_local, feat_blocks, grad_blocks)
    w_in, w_out = own_first(weight_in), own_first(weight_out)
    hist_out = dot(history, w_out[:half, :half]) + dot(swap(history), w_out[half:, :half])
    hist_out = blocks(hist_out.astype(BF16))

    returned = exchange(back)
    z_first = remote_forward(targets_remote, tiles_remote, received, base_forward).reshape(rows, half)
    pre, hidden, hidden_out, sending = middle(
        served_ids, flags, z_first, swap(z_first), w_in, w_out, hist_out
    )
    supplied = exchange(sending)

    base_out = local_forward(sources_local, targets_local, tiles_local, hidden_out)
    sums = gather_grads(served_ids, flags, returned, base_back).reshape(2, rows, half)
    grad_hidden, chunks = backward(
        place, sums, swap(sums), hidden, history, z_first, pre, w_out, peers
    )
    scale = float(rows * peers) ** (-0.5)
    grad_in, grad_out = finish_weights(place, sum_over_dom(chunks), half, scale)
    out = remote_forward(targets_remote, tiles_remote, supplied, base_out).reshape(rows, half)
    return (out, grad_hidden, grad_in, grad_out)


def solution(mesh):
    return jax.shard_map(
        per_device,
        mesh=mesh,
        in_specs=(
            P("dom", "hid"),
            P("dom", "hid"),
            P("dom", None, None, None),
            P("dom", None),
            P("dom", None),
            P("dom", None),
            P("dom", None, None, None),
            P("dom", None),
            P("dom", None),
            P("hid", None),
            P("hid", None),
            P("dom", "hid"),
        ),
        out_specs=(P("dom", "hid"), P("dom", "hid"), P("hid", None), P("hid", None)),
        check_vma=False,
    )
```

time: 276 us -> 145 us (0.53)
  waiting for transfers between devices: 135 us -> 52.5 us
  matrix products: 48.8 us -> 1.73 us
  Pallas kernels: 0 us -> 27 us
  local copies, waits for them, and re-layouts: 43.3 us -> 23.3 us
  starting transfers between devices: 20.6 us -> 37.5 us
  between operations: 14.1 us -> 0.95 us
  other arithmetic: 13.1 us -> 1.29 us
    psum x1 -> x0, waiting for transfers between devices: 110 us -> none  [per_device(): summed_in, summed_out = lax.psum((grad_in_w, grad_out_w), 'dom')]
    dot_general x17 -> x2, matrix products: 48.8 us -> 1.73 us  [dot(): return jnp.dot(a, b, preferred_element_type=F32)]
    pallas_call x0 -> x10, Pallas kernels: none -> 27 us  [call(): pl.pallas_call(body, grid_spec=pltpu.PrefetchScalarGridSpec(num_scalar_pr...]
    ppermute x0 -> x17, waiting for transfers between devices: none -> 22.2 us  [the longest x12 22.2 us: hop(): return lax.ppermute(value, 'dom', [(i, i ^ offset) for i in range(peers)])]
    dot_general x5 -> x0, local copies, waits for them, and re-layouts: 21.7 us -> none  [the longest x2 11.1 us: local_forward(): jnp.einsum('kij,kjf->kif', tiles, rows, preferred_element_type=jnp.float32)]
    gather x10 -> x0, local copies, waits for them, and re-layouts: 17.9 us -> none  [the longest x2 4.26 us: per_device(): jnp.take(feat_blocks, served_ids, axis=0)]
    unnamed x26 -> x64, local copies, waits for them, and re-layouts: 0.85 us -> 18.4 us
    ppermute x0 -> x17, starting transfers between devices: none -> 17.1 us  [the longest x12 16 us: hop(): return lax.ppermute(value, 'dom', [(i, i ^ offset) for i in range(peers)])]
  transfers between devices with their start and end apart: 8 -> 20, of which waited for: 5 -> 12; matrix products, arithmetic and copies ran while one was open for 28% -> 7% of each run, Pallas kernels for 0% -> 15%
where the time goes in v1:
time: 145 us; the launch traced here: 144 us
  waiting for transfers between devices  52.5 us (36%)
  starting transfers between devices  37.5 us (26%)
  Pallas kernels  27 us (19%)
  local copies, waits for them, and re-layouts  23.3 us (16%)
  matrix products  1.73 us (1%)
    all_to_all x3, waiting for transfers between devices, exchange(): lax.all_to_all(sending, 'dom', split_axis=0, concat_axis=0, tiled=True)  30.3 us
    pallas_call x10, Pallas kernels, call(): pl.pallas_call(body, grid_spec=pltpu.PrefetchScalarGridSpec(num_scalar_pr...  27 us
    ppermute x12, waiting for transfers between devices, hop(): return lax.ppermute(value, 'dom', [(i, i ^ offset) for i in range(peers)])  22.2 us
    all_to_all x3, starting transfers between devices, exchange(): lax.all_to_all(sending, 'dom', split_axis=0, concat_axis=0, tiled=True)  20.4 us
    unnamed x64, local copies, waits for them, and re-layouts  18.4 us
    ppermute x12, starting transfers between devices, hop(): return lax.ppermute(value, 'dom', [(i, i ^ offset) for i in range(peers)])  16 us
  transfers between devices with their start and end apart: 20, of which 12 were waited for; matrix products, arithmetic and copies ran while one was open for 7% of the time, Pallas kernels for 15%

profile of v1, /device:TPU:0, one launch (start us, length us, event | category | flops | bytes accessed | tf_op | source)
XLA Modules:
  0.0 144.2 jit_solution(9190563013980164832)
XLA Ops:
  0.6 1.0 copy-done
  1.7 1.0 copy-done.6
  2.7 0.7 copy-done.21
  3.4 2.0 %remote_back.1 = bf16[16,128,256]{2,1,0:T(8,128)(2,1)} custom-call(s32[16]{0:T(128)S(1)} %bitcast.83, bf16[16,128,128]{2,1,0:T(8,128)(2,1)S(1)} %bitcast.70, bf16[8,128,256]{2,1,0:T(8,128)(2,1)S(1)} %bitcast.75), custom_call_target="tpu_custom_call" | custom-call | flops 134217728 | bytes 2097152 | tf_op jit(solution)/shard_map/remote_back/pallas_call | solution.py:31
  5.4 8.5 %all-to-all-start.2 = ((bf16[16,128,256]{2,1,0:T(8,128)(2,1)}), bf16[16,128,256]{2,1,0:T(8,128)(2,1)}, u32[]{:S(2)}, u32[]{:S(2)}) async-start(bf16[16,128,256]{2,1,0:T(8,128)(2,1)} %remote_back.1), calls=%async_computation.2 | async-start | bytes 2097152 | tf_op jit(solution)/shard_map/all_to_all | solution.py:363
  14.0 0.7 pick_blocks.1
  14.7 1.0 copy-done.3
  15.7 22.7 %all-to-all-done.2.ret_ref = bf16[16,128,256]{2,1,0:T(8,128)(2,1)} async-done(((bf16[16,128,256]{2,1,0:T(8,128)(2,1)}), bf16[16,128,256]{2,1,0:T(8,128)(2,1)}, u32[]{:S(2)}, u32[]{:S(2)}) %all-to-all-start.2) | async-done | bytes 1048608 | tf_op jit(solution)/shard_map/all_to_all | solution.py:363
  38.4 5.8 %all-to-all-start = ((bf16[16,128,256]{2,1,0:T(8,128)(2,1)}), bf16[16,128,256]{2,1,0:T(8,128)(2,1)S(1)}, u32[]{:S(2)}, u32[]{:S(2)}) async-start(bf16[16,128,256]{2,1,0:T(8,128)(2,1)} %copy-done.3), calls=%async_computation | async-start | bytes 2097152 | tf_op jit(solution)/shard_map/all_to_all | solution.py:363
  44.3 0.5 collective-permute-start.2
  44.8 0.1 collective-permute-start.3
  44.9 0.7 constant_dynamic-update-slice_fusion.1
  45.7 2.5 %local_both.1 = (f32[8,128,256]{2,1,0:T(8,128)S(1)}, f32[8,128,256]{2,1,0:T(8,128)S(1)}) custom-call(s32[32]{0:T(128)S(1)} %bitcast.89, s32[32]{0:T(128)S(1)} %bitcast.91, bf16[32,128,128]{2,1,0:T(8,128)(2,1)S(1)} %bitcast.73, bf16[8,128,256]{2,1,0:T(8,128)(2,1)S(1)} %bitcast.79, bf16[8,128,256]{2,1,0:T(8,128)(2,1)S(1)} %bitcast.76), custom_call_target="tpu_custom_call" | custom-call | flops 536870912 | bytes 4194304 | tf_op jit(solution)/shard_map/local_both/pallas_call | solution.py:31
  48.2 1.0 copy-done.13
  49.2 1.0 copy-done.15
  50.2 1.0 constant_dynamic-update-slice_fusion.3
  51.1 1.7 %constant_dynamic-update-slice_fusion = bf16[512,512]{1,0:T(8,128)(2,1)} fusion(bf16[512,512]{1,0:T(8,128)(2,1)} %constant_dynamic-update-slice_fusion.1, bf16[256,512]{1,0:T(8,128)(2,1)} %collective-permute-done.1), kind=kLoop, calls=%fused_computation.29 | loop fusion | bytes 524288 | tf_op jit(solution)/shard_map/concatenate | solution.py:398
  52.8 1.1 constant_dynamic-update-slice_fusion.2
  53.9 1.1 fusion.15
  55.0 0.9 maximum_select_fusion.wi_ref
  56.0 3.0 %gather_grads.1 = bf16[2,8,128,256]{3,2,1,0:T(8,128)(2,1)} custom-call(s32[16]{0:T(128)S(1)} %bitcast.87, s32[16]{0:T(128)S(1)} %bitcast.93, bf16[16,128,256]{2,1,0:T(8,128)(2,1)} %all-to-all-done.2.ret_ref, f32[8,128,256]{2,1,0:T(8,128)S(1)} %copy-done.16), custom_call_target="tpu_custom_call" | custom-call | bytes 3145728 | tf_op jit(solution)/shard_map/gather_grads/pallas_call | solution.py:31
  59.0 0.4 collective-permute-start.4
  59.5 0.1 maximum_select_fusion.1.wo_ref
  59.6 7.6 %all-to-all-done.recv_ref = bf16[16,128,256]{2,1,0:T(8,128)(2,1)S(1)} async-done(((bf16[16,128,256]{2,1,0:T(8,128)(2,1)}), bf16[16,128,256]{2,1,0:T(8,128)(2,1)S(1)}, u32[]{:S(2)}, u32[]{:S(2)}) %all-to-all-start) | async-done | bytes 1048608 | tf_op jit(solution)/shard_map/all_to_all | solution.py:363
  67.2 1.2 copy-done.14
  68.4 2.1 %remote_forward.2 = bf16[8,128,256]{2,1,0:T(8,128)(2,1)} custom-call(s32[16]{0:T(128)S(1)} %bitcast.84, bf16[16,128,128]{2,1,0:T(8,128)(2,1)S(1)} %bitcast.71, bf16[16,128,256]{2,1,0:T(8,128)(2,1)S(1)} %all-to-all-done.recv_ref, f32[8,128,256]{2,1,0:T(8,128)S(1)} %copy-done.14), custom_call_target="tpu_custom_call" | custom-call | flops 134217728 | bytes 3145728 | tf_op jit(solution)/shard_map/remote_forward/pallas_call | solution.py:31
  70.5 1.4 fusion.6
  71.9 0.3 fusion.1
  72.3 1.0 copy.16
  73.3 0.8 copy-done.27
  74.1 1.0 copy-done.19
  75.1 1.0 copy-done.20
  76.2 1.0 copy-done.28
  77.2 4.2 %middle.1 = (f32[1024,512]{1,0:T(8,128)S(1)}, bf16[1024,512]{1,0:T(8,128)(2,1)S(1)}, bf16[8,128,256]{2,1,0:T(8,128)(2,1)S(1)}, bf16[16,128,256]{2,1,0:T(8,128)(2,1)S(1)}) custom-call(s32[16]{0:T(128)S(1)} %bitcast.88, s32[16]{0:T(128)S(1)} %bitcast.94, bf16[1024,256]{1,0:T(8,128)(2,1)} %bitcast.9.zm_ref.z_ref, bf16[1024,256]{1,0:T(8,128)(2,1)S(1)} %copy-done.28, ...), custom_call_target="tpu_custom_call" | custom-call | flops 805306368 | bytes 7340032 | tf_op jit(solution)/shard_map/middle/pallas_call | solution.py:31
  81.4 1.3 copy-done.4
  82.7 1.0 copy-done.12
  83.7 0.8 copy-done.17
  84.5 6.1 %all-to-all-start.1 = ((bf16[16,128,256]{2,1,0:T(8,128)(2,1)}), bf16[16,128,256]{2,1,0:T(8,128)(2,1)}, u32[]{:S(2)}, u32[]{:S(2)}) async-start(bf16[16,128,256]{2,1,0:T(8,128)(2,1)} %copy-done.12), calls=%async_computation.1 | async-start | bytes 2097152 | tf_op jit(solution)/shard_map/all_to_all | solution.py:363
  90.7 1.6 %copy-done.5 = f32[1024,512]{1,0:T(8,128)S(1)} copy-done((f32[1024,512]{1,0:T(8,128)S(1)}, f32[1024,512]{1,0:T(8,128)}, u32[]{:S(2)}) %copy-start.5) | copy-done | bytes 2097176
  92.3 1.0 copy-done.11
  93.3 5.9 %backward.1 = (bf16[1024,256]{1,0:T(8,128)(2,1)}, bf16[16,32,512]{2,1,0:T(8,128)(2,1)S(1)}) custom-call(s32[2]{0:T(128)S(1)} %pad_add_fusion.place_ref, bf16[2,1024,256]{2,1,0:T(8,128)(2,1)} %bitcast.15.sm_ref, bf16[2,1024,256]{2,1,0:T(8,128)(2,1)} %collective-permute-done.4.so_ref, bf16[1024,512]{1,0:T(8,128)(2,1)S(1)} %get-tuple-element.18.hid_ref, ...), custom_call_target="tpu_custom_call" | custom-call | flops 1342177280 | bytes 7864320 | tf_op jit(solution)/shard_map/backward/pallas_call | solution.py:31
  99.2 2.8 %collective-permute-start.7 = (bf16[4,32,512]{2,1,0:T(8,128)(2,1)S(1)}, bf16[4,32,512]{2,1,0:T(8,128)(2,1)S(1)}, u32[]{:S(2)}, u32[]{:S(2)}) collective-permute-start(bf16[4,32,512]{2,1,0:T(8,128)(2,1)S(1)} %get-tuple-element.26), channel_id=1, source_target_pairs={{0,6},{2,4},{4,2},{6,0},{8,14},{10,12},{12,10},{14,8},{16,22},{18,... | collective-permute-start | bytes 393224 | tf_op jit(solution)/shard_map/ppermute | solution.py:341
  102.1 0.6 collective-permute-start.6
  102.6 0.2 collective-permute-start.5
  102.8 8.0 %collective-permute-done.7 = bf16[4,32,512]{2,1,0:T(8,128)(2,1)S(1)} collective-permute-done((bf16[4,32,512]{2,1,0:T(8,128)(2,1)S(1)}, bf16[4,32,512]{2,1,0:T(8,128)(2,1)S(1)}, u32[]{:S(2)}, u32[]{:S(2)}) %collective-permute-start.7) | collective-permute-done | bytes 131104 | tf_op jit(solution)/shard_map/ppermute | solution.py:341
  110.8 5.3 %collective-permute-done.5 = bf16[4,32,512]{2,1,0:T(8,128)(2,1)S(1)} collective-permute-done((bf16[4,32,512]{2,1,0:T(8,128)(2,1)S(1)}, bf16[4,32,512]{2,1,0:T(8,128)(2,1)S(1)}, u32[]{:S(2)}, u32[]{:S(2)}) %collective-permute-start.5) | collective-permute-done | bytes 131104 | tf_op jit(solution)/shard_map/ppermute | solution.py:341
  116.3 3.5 %collective-permute-start.9 = (bf16[1,32,512]{2,1,0:T(8,128)(2,1)S(1)}, bf16[1,32,512]{2,1,0:T(8,128)(2,1)S(1)}, u32[]{:S(2)}, u32[]{:S(2)}) collective-permute-start(bf16[1,32,512]{2,1,0:T(8,128)(2,1)S(1)} %get-tuple-element.35), channel_id=1, source_target_pairs={{0,16},{2,18},{4,20},{6,22},{8,24},{10,26},{12,28},{14,30},{16,0},... | collective-permute-start | bytes 98312 | tf_op jit(solution)/shard_map/ppermute | solution.py:341
  119.8 0.9 collective-permute-start.8
  120.7 1.5 %collective-permute-done.10 = bf16[1,32,512]{2,1,0:T(8,128)(2,1)S(1)} collective-permute-done((bf16[1,32,512]{2,1,0:T(8,128)(2,1)S(1)}, bf16[1,32,512]{2,1,0:T(8,128)(2,1)S(1)}, u32[]{:S(2)}, u32[]{:S(2)}) %collective-permute-start.10) | collective-permute-done | bytes 32800 | tf_op jit(solution)/shard_map/ppermute | solution.py:341
  122.2 0.5 collective-permute-done.9
  122.6 1.0 collective-permute-done.8
  123.7 2.9 %collective-permute-start.13 = (bf16[1,32,512]{2,1,0:T(8,128)(2,1)S(1)}, bf16[1,32,512]{2,1,0:T(8,128)(2,1)S(1)}, u32[]{:S(2)}, u32[]{:S(2)}) collective-permute-start(bf16[1,32,512]{2,1,0:T(8,128)(2,1)S(1)} %fusion.11), channel_id=1, source_target_pairs={{0,24},{2,26},{4,28},{6,30},{8,16},{10,18},{12,20},{14,22},{16,8},... | collective-permute-start | bytes 98312 | tf_op jit(solution)/shard_map/ppermute | solution.py:341
  126.6 1.5 %collective-permute-start.11 = (bf16[1,32,512]{2,1,0:T(8,128)(2,1)S(1)}, bf16[1,32,512]{2,1,0:T(8,128)(2,1)S(1)}, u32[]{:S(2)}, u32[]{:S(2)}) collective-permute-start(bf16[1,32,512]{2,1,0:T(8,128)(2,1)S(1)} %fusion.11), channel_id=1, source_target_pairs={{0,8},{2,10},{4,12},{6,14},{8,0},{10,2},{12,4},{14,6},{16,24},{18,... | collective-permute-start | bytes 98312 | tf_op jit(solution)/shard_map/ppermute | solution.py:341
  128.2 1.3 collective-permute-done.13
  129.5 1.9 %collective-permute-done.12 = bf16[1,32,512]{2,1,0:T(8,128)(2,1)S(1)} collective-permute-done((bf16[1,32,512]{2,1,0:T(8,128)(2,1)S(1)}, bf16[1,32,512]{2,1,0:T(8,128)(2,1)S(1)}, u32[]{:S(2)}, u32[]{:S(2)}) %collective-permute-start.12) | collective-permute-done | bytes 32800 | tf_op jit(solution)/shard_map/ppermute | solution.py:341
  131.5 1.1 collective-permute-start.16
  132.6 1.9 %collective-permute-start.15 = (bf16[4,32,512]{2,1,0:T(8,128)(2,1)S(1)}, bf16[4,32,512]{2,1,0:T(8,128)(2,1)S(1)}, u32[]{:S(2)}, u32[]{:S(2)}) collective-permute-start(bf16[4,32,512]{2,1,0:T(8,128)(2,1)S(1)} %get-tuple-element.32), channel_id=1, source_target_pairs={{0,4},{2,6},{4,0},{6,2},{8,12},{10,14},{12,8},{14,10},{16,20},{18,... | collective-permute-start | bytes 393224 | tf_op jit(solution)/shard_map/ppermute | solution.py:341
  134.5 0.5 collective-permute-start.14
  135.0 1.9 %local_forward.1.base_ref = f32[8,128,256]{2,1,0:T(8,128)S(1)} custom-call(s32[32]{0:T(128)S(1)} %bitcast.90, s32[32]{0:T(128)S(1)} %bitcast.92, bf16[32,128,128]{2,1,0:T(8,128)(2,1)S(1)} %bitcast.74, bf16[8,128,256]{2,1,0:T(8,128)(2,1)S(1)} %copy-done.18), custom_call_target="tpu_custom_call" | custom-call | flops 268435456 | bytes 2621440 | tf_op jit(solution)/shard_map/local_forward/pallas_call | solution.py:31
  136.9 0.6 collective-permute-done.16
  137.5 1.3 collective-permute-done.15
  138.8 0.7 collective-permute-done.14
  139.5 1.5 %finish_weights.1 = (f32[256,512]{1,0:T(8,128)}, f32[256,512]{1,0:T(8,128)}) custom-call(s32[2]{0:T(128)S(1)} %pad_add_fusion.place_ref, bf16[16,32,512]{2,1,0:T(8,128)(2,1)S(1)} %bitcast.77), custom_call_target="tpu_custom_call" | custom-call | bytes 1572864 | tf_op jit(solution)/shard_map/finish_weights/pallas_call | solution.py:31
  141.1 3.1 %remote_forward.3 = bf16[8,128,256]{2,1,0:T(8,128)(2,1)} custom-call(s32[16]{0:T(128)S(1)} %bitcast.85, bf16[16,128,128]{2,1,0:T(8,128)(2,1)S(1)} %bitcast.72, bf16[16,128,256]{2,1,0:T(8,128)(2,1)} %all-to-all-done.1.recv_ref, f32[8,128,256]{2,1,0:T(8,128)S(1)} %local_forward.1.base_ref), custom_call_target="tpu_custom_call" | custom-call | flops 134217728 | bytes 3145728 | tf_op jit(solution)/shard_map/remote_forward/pallas_call | solution.py:31
  (66 shorter events, 0.6 us)
Async XLA Ops:
  0.6 1.0 copy-start
  1.7 1.0 copy-start.6
  2.7 0.7 copy-start.21
  3.4 10.6 %copy-start.23 = (s32[1,16]{1,0:T(1,128)S(1)}, s32[1,16]{1,0:T(1,128)}, u32[]{:S(2)}) copy-start(s32[1,16]{1,0:T(1,128)} %param.16) | copy-start | bytes 196
  5.4 8.5 %copy-start.8 = (bf16[1024,256]{1,0:T(8,128)(2,1)S(1)}, bf16[1024,256]{1,0:T(8,128)(2,1)}, u32[]{:S(2)}) copy-start(bf16[1024,256]{1,0:T(8,128)(2,1)} %param.12) | copy-start | bytes 1572868
  5.4 33.0 %all-to-all-start.2 = ((bf16[16,128,256]{2,1,0:T(8,128)(2,1)}), bf16[16,128,256]{2,1,0:T(8,128)(2,1)}, u32[]{:S(2)}, u32[]{:S(2)}) async-start(bf16[16,128,256]{2,1,0:T(8,128)(2,1)} %remote_back.1), calls=%async_computation.2 | async-start | bytes 2097152 | tf_op jit(solution)/shard_map/all_to_all | solution.py:363
  13.9 30.3 %copy-start.30 = (bf16[256,512]{1,0:T(8,128)(2,1)S(1)}, bf16[256,512]{1,0:T(8,128)(2,1)}, u32[]{:S(2)}) copy-start(bf16[256,512]{1,0:T(8,128)(2,1)} %param.21) | copy-start | bytes 786436
  14.0 31.7 %copy-start.2 = (bf16[1,32,128,128]{3,2,1,0:T(8,128)(2,1)S(1)}, bf16[1,32,128,128]{3,2,1,0:T(8,128)(2,1)}, u32[]{:S(2)}) copy-start(bf16[1,32,128,128]{3,2,1,0:T(8,128)(2,1)} %param.18) | copy-start | bytes 3145732
  14.0 31.7 %copy-start.7 = (bf16[1024,256]{1,0:T(8,128)(2,1)S(1)}, bf16[1024,256]{1,0:T(8,128)(2,1)}, u32[]{:S(2)}) copy-start(bf16[1024,256]{1,0:T(8,128)(2,1)} %param.23) | copy-start | bytes 1572868
  14.0 31.7 %copy-start.24 = (s32[1,32]{1,0:T(1,128)S(1)}, s32[1,32]{1,0:T(1,128)}, u32[]{:S(2)}) copy-start(s32[1,32]{1,0:T(1,128)} %param.19) | copy-start | bytes 388
  14.0 31.7 %copy-start.25 = (s32[1,32]{1,0:T(1,128)S(1)}, s32[1,32]{1,0:T(1,128)}, u32[]{:S(2)}) copy-start(s32[1,32]{1,0:T(1,128)} %param.20) | copy-start | bytes 388
  14.7 1.0 copy-start.3
  15.7 29.9 %copy-start.9 = (bf16[1024,256]{1,0:T(8,128)(2,1)S(1)}, bf16[1024,256]{1,0:T(8,128)(2,1)}, u32[]{:S(2)}) copy-start(bf16[1024,256]{1,0:T(8,128)(2,1)} %param.12) | copy-start | bytes 1572868
  38.4 28.8 %all-to-all-start = ((bf16[16,128,256]{2,1,0:T(8,128)(2,1)}), bf16[16,128,256]{2,1,0:T(8,128)(2,1)S(1)}, u32[]{:S(2)}, u32[]{:S(2)}) async-start(bf16[16,128,256]{2,1,0:T(8,128)(2,1)} %copy-done.3), calls=%async_computation | async-start | bytes 2097152 | tf_op jit(solution)/shard_map/all_to_all | solution.py:363
  44.3 6.9 %collective-permute-start.1 = (bf16[256,512]{1,0:T(8,128)(2,1)S(1)}, bf16[256,512]{1,0:T(8,128)(2,1)}, u32[]{:S(2)}, u32[]{:S(2)}) collective-permute-start(bf16[256,512]{1,0:T(8,128)(2,1)S(1)} %copy-done.30), channel_id=1, source_target_pairs={{0,1},{1,0},{2,3},{3,2},{4,5},{5,4},{6,7},{7,6},{8,9},{9,8},{10,11... | collective-permute-start | bytes 786440 | tf_op jit(solution)/shard_map/ppermute | solution.py:367
  44.3 8.5 %collective-permute-start.2 = (bf16[256,512]{1,0:T(8,128)(2,1)}, bf16[256,512]{1,0:T(8,128)(2,1)}, u32[]{:S(2)}, u32[]{:S(2)}) collective-permute-start(bf16[256,512]{1,0:T(8,128)(2,1)} %param.22), channel_id=1, source_target_pairs={{0,1},{1,0},{2,3},{3,2},{4,5},{5,4},{6,7},{7,6},{8,9},{9,8},{10,11... | collective-permute-start | bytes 786440 | tf_op jit(solution)/shard_map/ppermute | solution.py:367
  44.8 25.7 %collective-permute-start.3 = (bf16[1024,256]{1,0:T(8,128)(2,1)}, bf16[1024,256]{1,0:T(8,128)(2,1)}, u32[]{:S(2)}, u32[]{:S(2)}) collective-permute-start(bf16[1024,256]{1,0:T(8,128)(2,1)} %hist_ref.1), channel_id=1, source_target_pairs={{0,1},{1,0},{2,3},{3,2},{4,5},{5,4},{6,7},{7,6},{8,9},{9,8},{10,11... | collective-permute-start | bytes 1572872 | tf_op jit(solution)/shard_map/ppermute | solution.py:367
  48.2 1.0 copy-start.13
  49.2 1.0 copy-start.15
  52.8 2.2 %copy-start.29 = (bf16[512,512]{1,0:T(8,128)(2,1)S(1)}, bf16[512,512]{1,0:T(8,128)(2,1)}, u32[]{:S(2)}) copy-start(bf16[512,512]{1,0:T(8,128)(2,1)} %constant_dynamic-update-slice_fusion) | copy-start | bytes 1572868
  52.8 3.1 %copy-start.16 = (f32[8,128,256]{2,1,0:T(8,128)S(1)}, f32[8,128,256]{2,1,0:T(8,128)}, u32[]{:S(2)}) copy-start(f32[8,128,256]{2,1,0:T(8,128)} %copy-done.15) | copy-start | bytes 3145732
  52.8 3.1 %copy-start.26 = (s32[1,16]{1,0:T(1,128)S(1)}, s32[1,16]{1,0:T(1,128)}, u32[]{:S(2)}) copy-start(s32[1,16]{1,0:T(1,128)} %param.17) | copy-start | bytes 196
  56.0 11.2 %copy-start.1 = (bf16[1,16,128,128]{3,2,1,0:T(8,128)(2,1)S(1)}, bf16[1,16,128,128]{3,2,1,0:T(8,128)(2,1)}, u32[]{:S(2)}) copy-start(bf16[1,16,128,128]{3,2,1,0:T(8,128)(2,1)} %param.14) | copy-start | bytes 1572868
  56.0 11.2 %copy-start.22 = (s32[1,16]{1,0:T(1,128)S(1)}, s32[1,16]{1,0:T(1,128)}, u32[]{:S(2)}) copy-start(s32[1,16]{1,0:T(1,128)} %param.15) | copy-start | bytes 196
  59.0 31.6 %collective-permute-start.4 = (bf16[2,1024,256]{2,1,0:T(8,128)(2,1)}, bf16[2,1024,256]{2,1,0:T(8,128)(2,1)}, u32[]{:S(2)}, u32[]{:S(2)}) collective-permute-start(bf16[2,1024,256]{2,1,0:T(8,128)(2,1)} %bitcast.15.sm_ref), channel_id=1, source_target_pairs={{0,1},{1,0},{2,3},{3,2},{4,5},{5,4},{6,7},{7,6},{8,9},{9,8},{10,11... | collective-permute-start | bytes 3145736 | tf_op jit(solution)/shard_map/ppermute | solution.py:367
  67.2 1.2 copy-start.14
  68.4 3.5 %copy-start.10 = (bf16[1024,256]{1,0:T(8,128)(2,1)S(1)}, bf16[1024,256]{1,0:T(8,128)(2,1)}, u32[]{:S(2)}) copy-start(bf16[1024,256]{1,0:T(8,128)(2,1)} %hist_ref.1) | copy-start | bytes 1572868
  70.5 2.8 %collective-permute-start = (bf16[1024,256]{1,0:T(8,128)(2,1)}, bf16[1024,256]{1,0:T(8,128)(2,1)S(1)}, u32[]{:S(2)}, u32[]{:S(2)}) collective-permute-start(bf16[1024,256]{1,0:T(8,128)(2,1)} %bitcast.9.zm_ref.z_ref), channel_id=1, source_target_pairs={{0,1},{1,0},{2,3},{3,2},{4,5},{5,4},{6,7},{7,6},{8,9},{9,8},{10,11... | collective-permute-start | bytes 1572872 | tf_op jit(solution)/shard_map/ppermute | solution.py:367
  73.3 0.8 copy-start.27
  74.1 1.0 copy-start.19
  75.1 1.0 copy-start.20
  76.2 1.0 copy-start.28
  81.4 1.4 copy-start.4
  82.7 1.0 copy-start.12
  83.7 0.8 copy-start.17
  84.5 56.6 %all-to-all-start.1 = ((bf16[16,128,256]{2,1,0:T(8,128)(2,1)}), bf16[16,128,256]{2,1,0:T(8,128)(2,1)}, u32[]{:S(2)}, u32[]{:S(2)}) async-start(bf16[16,128,256]{2,1,0:T(8,128)(2,1)} %copy-done.12), calls=%async_computation.1 | async-start | bytes 2097152 | tf_op jit(solution)/shard_map/all_to_all | solution.py:363
  90.7 1.6 %copy-start.5 = (f32[1024,512]{1,0:T(8,128)S(1)}, f32[1024,512]{1,0:T(8,128)}, u32[]{:S(2)}) copy-start(f32[1024,512]{1,0:T(8,128)} %copy-done.4) | copy-start | bytes 6291460
  92.3 1.0 copy-start.11
  99.2 35.8 %copy-start.18 = (bf16[8,128,256]{2,1,0:T(8,128)(2,1)S(1)}, bf16[8,128,256]{2,1,0:T(8,128)(2,1)}, u32[]{:S(2)}) copy-start(bf16[8,128,256]{2,1,0:T(8,128)(2,1)} %copy-done.17) | copy-start | bytes 1572868
  99.2 11.5 %collective-permute-start.7 = (bf16[4,32,512]{2,1,0:T(8,128)(2,1)S(1)}, bf16[4,32,512]{2,1,0:T(8,128)(2,1)S(1)}, u32[]{:S(2)}, u32[]{:S(2)}) collective-permute-start(bf16[4,32,512]{2,1,0:T(8,128)(2,1)S(1)} %get-tuple-element.26), channel_id=1, source_target_pairs={{0,6},{2,4},{4,2},{6,0},{8,14},{10,12},{12,10},{14,8},{16,22},{18,... | collective-permute-start | bytes 393224 | tf_op jit(solution)/shard_map/ppermute | solution.py:341
  102.1 8.7 %collective-permute-start.6 = (bf16[4,32,512]{2,1,0:T(8,128)(2,1)S(1)}, bf16[4,32,512]{2,1,0:T(8,128)(2,1)S(1)}, u32[]{:S(2)}, u32[]{:S(2)}) collective-permute-start(bf16[4,32,512]{2,1,0:T(8,128)(2,1)S(1)} %get-tuple-element.25), channel_id=1, source_target_pairs={{0,4},{2,6},{4,0},{6,2},{8,12},{10,14},{12,8},{14,10},{16,20},{18,... | collective-permute-start | bytes 393224 | tf_op jit(solution)/shard_map/ppermute | solution.py:341
  102.6 13.5 %collective-permute-start.5 = (bf16[4,32,512]{2,1,0:T(8,128)(2,1)S(1)}, bf16[4,32,512]{2,1,0:T(8,128)(2,1)S(1)}, u32[]{:S(2)}, u32[]{:S(2)}) collective-permute-start(bf16[4,32,512]{2,1,0:T(8,128)(2,1)S(1)} %get-tuple-element.24), channel_id=1, source_target_pairs={{0,2},{2,0},{4,6},{6,4},{8,10},{10,8},{12,14},{14,12},{16,18},{18,... | collective-permute-start | bytes 393224 | tf_op jit(solution)/shard_map/ppermute | solution.py:341
  116.2 5.9 %collective-permute-start.10 = (bf16[1,32,512]{2,1,0:T(8,128)(2,1)S(1)}, bf16[1,32,512]{2,1,0:T(8,128)(2,1)S(1)}, u32[]{:S(2)}, u32[]{:S(2)}) collective-permute-start(bf16[1,32,512]{2,1,0:T(8,128)(2,1)S(1)} %get-tuple-element.34), channel_id=1, source_target_pairs={{0,24},{2,26},{4,28},{6,30},{8,16},{10,18},{12,20},{14,22},{16,8},... | collective-permute-start | bytes 98312 | tf_op jit(solution)/shard_map/ppermute | solution.py:341
  116.3 6.3 %collective-permute-start.9 = (bf16[1,32,512]{2,1,0:T(8,128)(2,1)S(1)}, bf16[1,32,512]{2,1,0:T(8,128)(2,1)S(1)}, u32[]{:S(2)}, u32[]{:S(2)}) collective-permute-start(bf16[1,32,512]{2,1,0:T(8,128)(2,1)S(1)} %get-tuple-element.35), channel_id=1, source_target_pairs={{0,16},{2,18},{4,20},{6,22},{8,24},{10,26},{12,28},{14,30},{16,0},... | collective-permute-start | bytes 98312 | tf_op jit(solution)/shard_map/ppermute | solution.py:341
  119.8 3.9 %collective-permute-start.8 = (bf16[1,32,512]{2,1,0:T(8,128)(2,1)S(1)}, bf16[1,32,512]{2,1,0:T(8,128)(2,1)S(1)}, u32[]{:S(2)}, u32[]{:S(2)}) collective-permute-start(bf16[1,32,512]{2,1,0:T(8,128)(2,1)S(1)} %get-tuple-element.33), channel_id=1, source_target_pairs={{0,8},{2,10},{4,12},{6,14},{8,0},{10,2},{12,4},{14,6},{16,24},{18,... | collective-permute-start | bytes 98312 | tf_op jit(solution)/shard_map/ppermute | solution.py:341
  123.7 5.8 %collective-permute-start.13 = (bf16[1,32,512]{2,1,0:T(8,128)(2,1)S(1)}, bf16[1,32,512]{2,1,0:T(8,128)(2,1)S(1)}, u32[]{:S(2)}, u32[]{:S(2)}) collective-permute-start(bf16[1,32,512]{2,1,0:T(8,128)(2,1)S(1)} %fusion.11), channel_id=1, source_target_pairs={{0,24},{2,26},{4,28},{6,30},{8,16},{10,18},{12,20},{14,22},{16,8},... | collective-permute-start | bytes 98312 | tf_op jit(solution)/shard_map/ppermute | solution.py:341
  126.6 4.8 %collective-permute-start.12 = (bf16[1,32,512]{2,1,0:T(8,128)(2,1)S(1)}, bf16[1,32,512]{2,1,0:T(8,128)(2,1)S(1)}, u32[]{:S(2)}, u32[]{:S(2)}) collective-permute-start(bf16[1,32,512]{2,1,0:T(8,128)(2,1)S(1)} %fusion.11), channel_id=1, source_target_pairs={{0,16},{2,18},{4,20},{6,22},{8,24},{10,26},{12,28},{14,30},{16,0},... | collective-permute-start | bytes 98312 | tf_op jit(solution)/shard_map/ppermute | solution.py:341
  126.6 4.8 %collective-permute-start.11 = (bf16[1,32,512]{2,1,0:T(8,128)(2,1)S(1)}, bf16[1,32,512]{2,1,0:T(8,128)(2,1)S(1)}, u32[]{:S(2)}, u32[]{:S(2)}) collective-permute-start(bf16[1,32,512]{2,1,0:T(8,128)(2,1)S(1)} %fusion.11), channel_id=1, source_target_pairs={{0,8},{2,10},{4,12},{6,14},{8,0},{10,2},{12,4},{14,6},{16,24},{18,... | collective-permute-start | bytes 98312 | tf_op jit(solution)/shard_map/ppermute | solution.py:341
  131.5 6.0 %collective-permute-start.16 = (bf16[4,32,512]{2,1,0:T(8,128)(2,1)S(1)}, bf16[4,32,512]{2,1,0:T(8,128)(2,1)S(1)}, u32[]{:S(2)}, u32[]{:S(2)}) collective-permute-start(bf16[4,32,512]{2,1,0:T(8,128)(2,1)S(1)} %get-tuple-element.32), channel_id=1, source_target_pairs={{0,6},{2,4},{4,2},{6,0},{8,14},{10,12},{12,10},{14,8},{16,22},{18,... | collective-permute-start | bytes 393224 | tf_op jit(solution)/shard_map/ppermute | solution.py:341
  132.6 6.2 %collective-permute-start.15 = (bf16[4,32,512]{2,1,0:T(8,128)(2,1)S(1)}, bf16[4,32,512]{2,1,0:T(8,128)(2,1)S(1)}, u32[]{:S(2)}, u32[]{:S(2)}) collective-permute-start(bf16[4,32,512]{2,1,0:T(8,128)(2,1)S(1)} %get-tuple-element.32), channel_id=1, source_target_pairs={{0,4},{2,6},{4,0},{6,2},{8,12},{10,14},{12,8},{14,10},{16,20},{18,... | collective-permute-start | bytes 393224 | tf_op jit(solution)/shard_map/ppermute | solution.py:341
  134.5 5.0 %collective-permute-start.14 = (bf16[4,32,512]{2,1,0:T(8,128)(2,1)S(1)}, bf16[4,32,512]{2,1,0:T(8,128)(2,1)S(1)}, u32[]{:S(2)}, u32[]{:S(2)}) collective-permute-start(bf16[4,32,512]{2,1,0:T(8,128)(2,1)S(1)} %get-tuple-element.32), channel_id=1, source_target_pairs={{0,2},{2,0},{4,6},{6,4},{8,10},{10,8},{12,14},{14,12},{16,18},{18,... | collective-permute-start | bytes 393224 | tf_op jit(solution)/shard_map/ppermute | solution.py:341

commit v2 on v1

--- a/solution.py
+++ b/solution.py
@@ -1,4 +1,4 @@
-import functools
+import math
 
 import jax
 import jax.numpy as jnp
@@ -9,7 +9,8 @@
 
 BF16 = jnp.bfloat16
 F32 = jnp.float32
-VMEM_BYTES = 40 * 1024 * 1024
+VMEM_SPARE = 6 * 1024 * 1024
+VMEM_MOST = 60 * 1024 * 1024
 SWAP = ((0, 1), (1, 0))
 
 
@@ -25,7 +26,14 @@
     return lax.dot_general(a, b, (((1,), (1,)), ((), ())), preferred_element_type=F32)
 
 
-def call(body, scalars, arrays, grid, in_specs, out_specs, out_shape, scratch=(), flops=0, name=None):
+def call(body, scalars, arrays, grid, in_specs, out_specs, out_shape, scratch=(), flops=0, name=None, vmem=None):
+    if vmem is None:
+        vmem = VMEM_SPARE + 2 * sum(math.prod(spec.block_shape) * a.dtype.itemsize for spec, a in zip(in_specs, arrays))
+        vmem += 2 * sum(
+            math.prod(spec.block_shape) * s.dtype.itemsize
+            for spec, s in zip(jax.tree.leaves(out_specs), jax.tree.leaves(out_shape))
+        )
+        vmem += sum(math.prod(s.shape) * jnp.dtype(s.dtype).itemsize for s in scratch)
     moved = sum(a.size * a.dtype.itemsize for a in arrays)
     moved += sum(s.size * s.dtype.itemsize for s in jax.tree.leaves(out_shape))
     return pl.pallas_call(
@@ -38,7 +46,7 @@
             scratch_shapes=list(scratch),
         ),
         out_shape=out_shape,
-        compiler_params=pltpu.CompilerParams(vmem_limit_bytes=VMEM_BYTES),
+        compiler_params=pltpu.CompilerParams(vmem_limit_bytes=vmem),
         cost_estimate=pl.CostEstimate(flops=int(flops), bytes_accessed=int(moved), transcendentals=0),
         name=name,
     )(*scalars, *arrays)
@@ -56,38 +64,22 @@
     return 8 if peers % 8 == 0 else 1
 
 
-def pick_blocks(ids, node_blocks):
-    peers = ids.shape[0]
-    _, tile, width = node_blocks.shape
+def prepare(ids, targets, tiles, nodes, grads):
+    peers, tile, _ = tiles.shape
+    width = nodes.shape[2]
     group = group_of(peers)
 
-    def body(ids_ref, nodes_ref, out_ref):
+    def body(ids_ref, dst_ref, tiles_ref, nodes_ref, grads_ref, out_ref):
         step = pl.program_id(0)
         for j in range(group):
-            out_ref[j] = nodes_ref[ids_ref[step * group + j]]
-
-    return call(
-        body, (ids,), (node_blocks,), (peers // group,),
-        [whole(node_blocks.shape)], lead((group, tile, width)),
-        jax.ShapeDtypeStruct((peers, tile, width), node_blocks.dtype), name="pick_blocks",
-    )
-
-
-def remote_back(targets, tiles, grads):
-    peers, tile, _ = tiles.shape
-    width = grads.shape[2]
-    group = group_of(peers)
-
-    def body(ids_ref, tiles_ref, grads_ref, out_ref):
-        step = pl.program_id(0)
-        for j in range(group):
-            out_ref[j] = dot_t(tiles_ref[j], grads_ref[ids_ref[step * group + j]]).astype(BF16)
-
-    return call(
-        body, (targets,), (tiles, grads), (peers // group,),
-        [lead((group, tile, tile)), whole(grads.shape)], lead((group, tile, width)),
-        jax.ShapeDtypeStruct((peers, tile, width), BF16),
-        flops=2 * peers * tile * tile * width, name="remote_back",
+            out_ref[j, :tile] = nodes_ref[ids_ref[step * group + j]]
+            out_ref[j, tile:] = dot_t(tiles_ref[j], grads_ref[dst_ref[step * group + j]]).astype(BF16)
+
+    return call(
+        body, (ids, targets), (tiles, nodes, grads), (peers // group,),
+        [lead((group, tile, tile)), whole(nodes.shape), whole(grads.shape)], lead((group, 2 * tile, width)),
+        jax.ShapeDtypeStruct((peers, 2 * tile, width), BF16),
+        flops=2 * peers * tile * tile * width, name="prepare", vmem=VMEM_MOST,
     )
 
 
@@ -169,6 +161,12 @@
         [pltpu.VMEM(base.shape, F32)],
         flops=2 * peers * tile * tile * width, name="remote_forward",
     )
+
+
+def silu_parts(z_mine, z_other, w_in):
+    half = z_mine.shape[1]
+    pre = dot(z_mine, w_in[:half]) + dot(z_other, w_in[half:])
+    return pre, 1.0 / (1.0 + jnp.exp(-pre))
 
 
 def middle(ids, flags, z_mine, z_other, w_in, w_out, hist_out):
@@ -179,13 +177,10 @@
     steps = count // per
     span = per * tile
 
-    def body(ids_ref, flag_ref, zm_ref, zo_ref, wi_ref, wo_ref, hw_ref, pre_ref, hid_ref, prod_ref, send_ref):
-        step = pl.program_id(0)
-        pre = dot(zm_ref[...], wi_ref[:half]) + dot(zo_ref[...], wi_ref[half:])
-        pre_ref[...] = pre
-        hidden = (pre * (1.0 / (1.0 + jnp.exp(-pre)))).astype(BF16)
-        hid_ref[...] = hidden
-        prod = dot(hidden, wo_ref[:, :half]).astype(BF16)
+    def body(ids_ref, flag_ref, zm_ref, zo_ref, wi_ref, wo_ref, hw_ref, prod_ref, send_ref):
+        step = pl.program_id(0)
+        pre, s = silu_parts(zm_ref[...], zo_ref[...], wi_ref[...])
+        prod = dot((pre * s).astype(BF16), wo_ref[:, :half]).astype(BF16)
         for j in range(per):
             prod_ref[step * per + j] = prod[j * tile : (j + 1) * tile]
 
@@ -206,10 +201,8 @@
     return call(
         body, (ids, flags), (z_mine, z_other, w_in, w_out, hist_out), (steps,),
         [lead((span, half)), lead((span, half)), whole(w_in.shape), whole(w_out.shape), whole(hist_out.shape)],
-        [lead((span, 2 * half)), lead((span, 2 * half)), whole(hist_out.shape), whole((peers, tile, half))],
+        [whole(hist_out.shape), whole((peers, tile, half))],
         [
-            jax.ShapeDtypeStruct((rows, 2 * half), F32),
-            jax.ShapeDtypeStruct((rows, 2 * half), BF16),
             jax.ShapeDtypeStruct(hist_out.shape, BF16),
             jax.ShapeDtypeStruct((peers, tile, half), BF16),
         ],
@@ -218,8 +211,8 @@
 
 
 def gather_grads(ids, flags, returned, base):
-    peers, tile, width = returned.shape
-    count = base.shape[0]
+    peers = returned.shape[0]
+    count, tile, width = base.shape
     group = group_of(peers)
     steps = peers // group
 
@@ -243,7 +236,7 @@
     both = (2,) + base.shape
     return call(
         body, (ids, flags), (returned, base), (steps,),
-        [lead((group, tile, width)), whole(base.shape)],
+        [pl.BlockSpec((group, tile, width), lambda i, *_: (i, 1, 0)), whole(base.shape)],
         whole(both), jax.ShapeDtypeStruct(both, BF16),
         [pltpu.VMEM(both, F32)], name="gather_grads",
     )
@@ -255,12 +248,12 @@
     return row_chunks, col_chunks, total // row_chunks, width // col_chunks
 
 
-def backward(place, sums_mine, sums_other, hidden, history, z_mine, pre, w_out, peers):
+def backward(place, sums_mine, sums_other, history, z_mine, z_other, w_in, w_out, peers):
     _, rows, half = sums_mine.shape
     step_rows = rows // 4
     row_chunks, col_chunks, chunk_rows, chunk_cols = chunking(peers, 2 * half, 2 * half)
 
-    def body(place_ref, sm_ref, so_ref, hid_ref, hist_ref, z_ref, pre_ref, wo_ref, gh_ref, chunk_ref, acc_ref):
+    def body(place_ref, sm_ref, so_ref, hist_ref, zm_ref, zo_ref, wi_ref, wo_ref, gh_ref, chunk_ref, acc_ref):
         step = pl.program_id(0)
         me, side = place_ref[0], place_ref[1]
 
@@ -268,17 +261,17 @@
         def _():
             acc_ref[...] = jnp.zeros_like(acc_ref)
 
+        z = zm_ref[...]
+        pre, s = silu_parts(z, zo_ref[...], wi_ref[...])
         dh = dot_nt(sm_ref[0], wo_ref[:, :half]) + dot_nt(so_ref[0], wo_ref[:, half:])
         gh_ref[...] = dh[:, :half].astype(BF16)
-        pre = pre_ref[...]
-        s = 1.0 / (1.0 + jnp.exp(-pre))
         dpre = (dh * s * (1.0 + pre * (1.0 - s))).astype(BF16)
-        z = z_ref[...]
+        hid = (pre[:, :half] * s[:, :half]).astype(BF16)
+        hist = hist_ref[...]
         own = pl.ds(pl.multiple_of(side * half, half), half)
         far = pl.ds(pl.multiple_of((1 - side) * half, half), half)
         acc_ref[:half, own] += dot_t(z, dpre[:, :half])
         acc_ref[:half, far] += dot_t(z, dpre[:, half:])
-        hid, hist = hid_ref[...], hist_ref[...]
         acc_ref[half:, own] += dot_t(hid, sm_ref[0]) + dot_t(hist, sm_ref[1])
         acc_ref[half:, far] += dot_t(hid, so_ref[0]) + dot_t(hist, so_ref[1])
 
@@ -290,19 +283,17 @@
                 chunk_ref[c ^ me] = piece.astype(BF16)
 
     sums_spec = pl.BlockSpec((2, step_rows, half), lambda i, *_: (0, i, 0))
-    return call(
-        body, (place,), (sums_mine, sums_other, hidden, history, z_mine, pre, w_out), (4,),
-        [
-            sums_spec, sums_spec, lead((step_rows, half)), lead((step_rows, half)),
-            lead((step_rows, half)), lead((step_rows, 2 * half)), whole(w_out.shape),
-        ],
-        [lead((step_rows, half)), whole((peers, chunk_rows, chunk_cols))],
+    some = lead((step_rows, half))
+    return call(
+        body, (place,), (sums_mine, sums_other, history, z_mine, z_other, w_in, w_out), (4,),
+        [sums_spec, sums_spec, some, some, some, whole(w_in.shape), whole(w_out.shape)],
+        [some, whole((peers, chunk_rows, chunk_cols))],
         [
             jax.ShapeDtypeStruct((rows, half), BF16),
             jax.ShapeDtypeStruct((peers, chunk_rows, chunk_cols), BF16),
         ],
         [pltpu.VMEM((2 * half, 2 * half), F32)],
-        flops=20 * rows * half * half, name="backward",
+        flops=28 * rows * half * half, name="backward",
     )
 
 
@@ -341,22 +332,25 @@
     return lax.ppermute(value, "dom", [(i, i ^ offset) for i in range(peers)])
 
 
-def sum_over_dom(chunks):
-    peers, chunk_rows, chunk_cols = chunks.shape
-    plan = stages(peers)
-    held = chunks
-    for stride, radix in plan:
-        parts = held.reshape(-1, radix, chunk_rows, chunk_cols)
-        arrived = [hop(parts[:, t], peers, t * stride) for t in range(1, radix)]
-        total = parts[:, 0].astype(F32)
-        for piece in arrived:
-            total = total + piece.astype(F32)
-        held = total.astype(BF16)
-    held = held.reshape(1, chunk_rows, chunk_cols)
-    for stride, radix in reversed(plan):
-        arrived = [held] + [hop(held, peers, t * stride) for t in range(1, radix)]
-        held = jnp.stack(arrived, axis=1).reshape(-1, chunk_rows, chunk_cols)
-    return held
+def scatter_stage(held, peers, stride, radix):
+    parts = held.reshape((-1, radix) + held.shape[1:])
+    return parts[:, 0], [hop(parts[:, t], peers, t * stride) for t in range(1, radix)]
+
+
+def add_pieces(kept, arrived):
+    total = kept.astype(F32)
+    for piece in arrived:
+        total = total + piece.astype(F32)
+    return total.astype(BF16)
+
+
+def gather_stage(held, peers, stride, radix):
+    arrived = [held] + [hop(held, peers, t * stride) for t in range(1, radix)]
+    return jnp.stack(arrived, axis=1).reshape((-1,) + held.shape[1:])
+
+
+def tie(values):
+    return lax.optimization_barrier(values)
 
 
 def exchange(sending):
@@ -400,28 +394,44 @@
         return jnp.where(side == 0, joined, turned)
 
     feat_blocks, grad_blocks = blocks(features), blocks(cotangent)
-    received = exchange(pick_blocks(served_ids, feat_blocks))
-    back = remote_back(targets_remote, tiles_remote, grad_blocks)
+    first = prepare(served_ids, targets_remote, tiles_remote, feat_blocks, grad_blocks)
+    received = exchange(first)
     base_forward, base_back = local_both(sources_local, targets_local, tiles_local, feat_blocks, grad_blocks)
     w_in, w_out = own_first(weight_in), own_first(weight_out)
     hist_out = dot(history, w_out[:half, :half]) + dot(swap(history), w_out[half:, :half])
     hist_out = blocks(hist_out.astype(BF16))
 
-    returned = exchange(back)
+    received, w_in, w_out, hist_out, base_forward, base_back = tie(
+        (received, w_in, w_out, hist_out, base_forward, base_back)
+    )
     z_first = remote_forward(targets_remote, tiles_remote, received, base_forward).reshape(rows, half)
-    pre, hidden, hidden_out, sending = middle(
-        served_ids, flags, z_first, swap(z_first), w_in, w_out, hist_out
-    )
+    z_first, received = tie((z_first, received))
+    z_other = swap(z_first)
+    sums = gather_grads(served_ids, flags, received, base_back).reshape(2, rows, half)
+    sums_other = swap(sums)
+    hidden_out, sending = middle(served_ids, flags, z_first, z_other, w_in, w_out, hist_out)
+    sending, sums, z_first, z_other = tie((sending, sums, z_first, z_other))
     supplied = exchange(sending)
-
+    grad_hidden, chunks = backward(
+        place, sums, sums_other, history, z_first, z_other, w_in, w_out, peers
+    )
+    plan = stages(peers)
+    kept, arrived = scatter_stage(chunks, peers, *plan[0])
+    kept, hidden_out = tie((kept, hidden_out))
     base_out = local_forward(sources_local, targets_local, tiles_local, hidden_out)
-    sums = gather_grads(served_ids, flags, returned, base_back).reshape(2, rows, half)
-    grad_hidden, chunks = backward(
-        place, sums, swap(sums), hidden, history, z_first, pre, w_out, peers
-    )
+    kept, base_out = tie((kept, base_out))
+    held = add_pieces(kept, arrived)
+    for stage in plan[1:]:
+        held = add_pieces(*scatter_stage(held, peers, *stage))
+    for stage in reversed(plan[1:]):
+        held = gather_stage(held, peers, *stage)
+    held, supplied = tie((held, supplied))
+    held = gather_stage(held, peers, *plan[0])
+    out = remote_forward(targets_remote, tiles_remote, supplied, base_out)
+    held, out = tie((held, out))
     scale = float(rows * peers) ** (-0.5)
-    grad_in, grad_out = finish_weights(place, sum_over_dom(chunks), half, scale)
-    out = remote_forward(targets_remote, tiles_remote, supplied, base_out).reshape(rows, half)
+    grad_in, grad_out = finish_weights(place, held, half, scale)
+    out = out.reshape(rows, half)
     return (out, grad_hidden, grad_in, grad_out)
 
 

time: 145 us -> 128 us (0.88)
  waiting for transfers between devices: 52.5 us -> 43.8 us
  local copies, waits for them, and re-layouts: 23.3 us -> 15.9 us
    unnamed x64 -> x56, local copies, waits for them, and re-layouts: 18.4 us -> 10 us
    all_to_all x3 -> x2, waiting for transfers between devices: 30.3 us -> 24.5 us  [exchange(): lax.all_to_all(sending, 'dom', split_axis=0, concat_axis=0, tiled=True)]
    ppermute x12, waiting for transfers between devices: 22.2 us -> 19.3 us  [hop(): return lax.ppermute(value, 'dom', [(i, i ^ offset) for i in range(peers)])]
    all_to_all x3 -> x2, starting transfers between devices: 20.4 us -> 18.6 us  [exchange(): lax.all_to_all(sending, 'dom', split_axis=0, concat_axis=0, tiled=True)]
    pallas_call x10 -> x9, Pallas kernels: 27 us -> 26.1 us  [call(): pl.pallas_call(body, grid_spec=pltpu.PrefetchScalarGridSpec(num_scalar_pr...]
  transfers between devices with their start and end apart: 20 -> 19, of which waited for: 12 -> 11; matrix products, arithmetic and copies ran while one was open for 7% -> 9% of each run, Pallas kernels for 15% -> 15%
where the time goes in v2:
time: 128 us
  waiting for transfers between devices  43.8 us (34%)
  starting transfers between devices  37.1 us (29%)
  Pallas kernels  26.1 us (20%)
  local copies, waits for them, and re-layouts  15.9 us (12%)
  matrix products  2.59 us (2%)
  other arithmetic  1.29 us (1%)
    pallas_call x9, Pallas kernels, call(): pl.pallas_call(body, grid_spec=pltpu.PrefetchScalarGridSpec(num_scalar_pr...  26.1 us
    all_to_all x2, waiting for transfers between devices, exchange(): lax.all_to_all(sending, 'dom', split_axis=0, concat_axis=0, tiled=True)  24.5 us
    ppermute x12, waiting for transfers between devices, hop(): return lax.ppermute(value, 'dom', [(i, i ^ offset) for i in range(peers)])  19.3 us
    all_to_all x2, starting transfers between devices, exchange(): lax.all_to_all(sending, 'dom', split_axis=0, concat_axis=0, tiled=True)  18.6 us
    ppermute x12, starting transfers between devices, hop(): return lax.ppermute(value, 'dom', [(i, i ^ offset) for i in range(peers)])  17.3 us
    unnamed x56, local copies, waits for them, and re-layouts  10 us
    concatenate x2, local copies, waits for them, and re-layouts, own_first(): joined = jnp.concatenate([weight, swap(weight)], axis=0)  2.7 us
    dot_general x2, matrix products, dot(): return jnp.dot(a, b, preferred_element_type=F32)  2.59 us
  transfers between devices with their start and end apart: 19, of which 11 were waited for; matrix products, arithmetic and copies ran while one was open for 9% of the time, Pallas kernels for 15%

profile of v2, /device:TPU:0, one launch (start us, length us, event | category | flops | bytes accessed | tf_op | source)
XLA Modules:
  0.0 127.7 jit_solution(3270331082201950732)
XLA Ops:
  0.6 3.6 %prepare.1 = bf16[16,256,256]{2,1,0:T(8,128)(2,1)} custom-call(s32[16]{0:T(128)} %bitcast.84, s32[16]{0:T(128)} %bitcast.81, bf16[16,128,128]{2,1,0:T(8,128)(2,1)} %bitcast.66, bf16[8,128,256]{2,1,0:T(8,128)(2,1)} %bitcast.72, bf16[8,128,256]{2,1,0:T(8,128)(2,1)} %bitcast.74), custom_call_target="tpu_custom_call" | custom-call | flops 134217728 | bytes 3670016 | tf_op jit(solution)/shard_map/prepare/pallas_call | solution.py:39
  4.3 0.0 copy-start.21
  4.3 8.5 %all-to-all-start = ((bf16[16,256,256]{2,1,0:T(8,128)(2,1)}), bf16[16,256,256]{2,1,0:T(8,128)(2,1)S(1)}, u32[]{:S(2)}, u32[]{:S(2)}) async-start(bf16[16,256,256]{2,1,0:T(8,128)(2,1)} %prepare.1), calls=%async_computation | async-start | bytes 4194304 | tf_op jit(solution)/shard_map/all_to_all | solution.py:357
  12.8 0.1 collective-permute-start
  12.8 0.5 collective-permute-start.1
  13.3 0.1 collective-permute-start.2
  13.4 0.7 constant_dynamic-update-slice_fusion.1
  14.2 1.0 copy-done.3
  15.2 1.0 copy-done.4
  16.2 2.6 %local_both.1 = (f32[8,128,256]{2,1,0:T(8,128)S(1)}, f32[8,128,256]{2,1,0:T(8,128)S(1)}) custom-call(s32[32]{0:T(128)S(1)} %bitcast.87, s32[32]{0:T(128)S(1)} %bitcast.89, bf16[32,128,128]{2,1,0:T(8,128)(2,1)S(1)} %bitcast.69, bf16[8,128,256]{2,1,0:T(8,128)(2,1)S(1)} %bitcast.73, bf16[8,128,256]{2,1,0:T(8,128)(2,1)S(1)} %bitcast.75), custom_call_target="tpu_custom_call" | custom-call | flops 536870912 | bytes 4194304 | tf_op jit(solution)/shard_map/local_both/pallas_call | solution.py:39
  18.9 1.0 copy-done.5
  19.8 1.0 copy-done.7
  20.8 1.0 constant_dynamic-update-slice_fusion.3
  21.8 1.7 %constant_dynamic-update-slice_fusion = bf16[512,512]{1,0:T(8,128)(2,1)} fusion(bf16[512,512]{1,0:T(8,128)(2,1)} %constant_dynamic-update-slice_fusion.1, bf16[256,512]{1,0:T(8,128)(2,1)} %collective-permute-done), kind=kLoop, calls=%fused_computation.24 | loop fusion | bytes 524288 | tf_op jit(solution)/shard_map/concatenate | solution.py:392
  23.5 1.0 constant_dynamic-update-slice_fusion.2
  24.5 1.1 fusion.10
  25.6 0.0 copy-start.9
  25.6 0.1 maximum_select_fusion.1.wo_ref
  25.8 0.9 maximum_select_fusion.wi_ref
  26.7 1.4 %fusion.3 = f32[256,1024]{1,0:T(8,128)S(1)} fusion(bf16[1024,256]{1,0:T(8,128)(2,1)} %collective-permute-done.2, bf16[512,512]{1,0:T(8,128)(2,1)S(1)} %maximum_select_fusion.1.wo_ref), kind=kOutput, calls=%fused_computation.12 | convolution fusion | flops 134217728 | bytes 1703936 | tf_op jit(solution)/shard_map/dot_general | solution.py:18
  28.2 1.1 fusion.1
  29.3 2.0 %copy.16 = bf16[1024,256]{1,0:T(8,128)(2,1)} copy(bf16[1024,256]{0,1:T(8,128)(2,1)} %fusion.1) | data formatting | bytes 1048576 | tf_op jit(solution)/shard_map/convert_element_type | solution.py:402
  31.3 24.5 %all-to-all-done.recv_ref.ret_ref = bf16[16,256,256]{2,1,0:T(8,128)(2,1)S(1)} async-done(((bf16[16,256,256]{2,1,0:T(8,128)(2,1)}), bf16[16,256,256]{2,1,0:T(8,128)(2,1)S(1)}, u32[]{:S(2)}, u32[]{:S(2)}) %all-to-all-start) | async-done | bytes 2097184 | tf_op jit(solution)/shard_map/all_to_all | solution.py:357
  55.8 1.2 copy-done.8
  57.1 1.4 %remote_forward.2 = bf16[8,128,256]{2,1,0:T(8,128)(2,1)S(1)} custom-call(s32[16]{0:T(128)S(1)} %bitcast.82, bf16[16,128,128]{2,1,0:T(8,128)(2,1)S(1)} %bitcast.67, bf16[16,256,256]{2,1,0:T(8,128)(2,1)S(1)} %all-to-all-done.recv_ref.ret_ref, f32[8,128,256]{2,1,0:T(8,128)S(1)} %copy-done.8), custom_call_target="tpu_custom_call" | custom-call | flops 134217728 | bytes 4194304 | tf_op jit(solution)/shard_map/remote_forward/pallas_call | solution.py:39
  58.5 0.0 copy-start.13
  58.5 0.1 collective-permute-start.3
  58.6 0.0 copy-start.15
  58.6 0.0 copy-start.17
  58.6 2.1 %gather_grads.1 = bf16[2,8,128,256]{3,2,1,0:T(8,128)(2,1)} custom-call(s32[16]{0:T(128)S(1)} %bitcast.85, s32[16]{0:T(128)S(1)} %bitcast.91, bf16[16,256,256]{2,1,0:T(8,128)(2,1)S(1)} %all-to-all-done.recv_ref.ret_ref, f32[8,128,256]{2,1,0:T(8,128)S(1)} %copy-done.6), custom_call_target="tpu_custom_call" | custom-call | bytes 4194304 | tf_op jit(solution)/shard_map/gather_grads/pallas_call | solution.py:39
  60.7 0.5 collective-permute-start.4
  61.2 0.0 copy-start.23
  61.2 3.8 %middle.1 = (bf16[8,128,256]{2,1,0:T(8,128)(2,1)S(1)}, bf16[16,128,256]{2,1,0:T(8,128)(2,1)}) custom-call(s32[16]{0:T(128)S(1)} %bitcast.86, s32[16]{0:T(128)S(1)} %bitcast.92, bf16[1024,256]{1,0:T(8,128)(2,1)S(1)} %bitcast.77, bf16[1024,256]{1,0:T(8,128)(2,1)S(1)} %collective-permute-done.3.zo_ref, bf16[512,512]{1,0:T(8,128)(2,1)S(1)} %copy-done.15, ...), custom_call_target="tpu_custom_call" | custom-call | flops 805306368 | bytes 4194304 | tf_op jit(solution)/shard_map/middle/pallas_call | solution.py:39
  65.0 0.8 copy-done.11
  65.8 10.1 %all-to-all-start.1 = ((bf16[16,128,256]{2,1,0:T(8,128)(2,1)}), bf16[16,128,256]{2,1,0:T(8,128)(2,1)}, u32[]{:S(2)}, u32[]{:S(2)}) async-start(bf16[16,128,256]{2,1,0:T(8,128)(2,1)} %get-tuple-element.51), calls=%async_computation.1 | async-start | bytes 2097152 | tf_op jit(solution)/shard_map/all_to_all | solution.py:357
  75.9 0.1 pad_add_fusion.place_ref
  76.1 1.1 copy-done.16
  77.2 1.0 copy-done.24
  78.2 6.1 %backward.1 = (bf16[1024,256]{1,0:T(8,128)(2,1)}, bf16[16,32,512]{2,1,0:T(8,128)(2,1)S(1)}) custom-call(s32[2]{0:T(128)S(1)} %pad_add_fusion.place_ref, bf16[2,1024,256]{2,1,0:T(8,128)(2,1)} %bitcast.14.sm_ref, bf16[2,1024,256]{2,1,0:T(8,128)(2,1)} %collective-permute-done.4.so_ref, bf16[1024,256]{1,0:T(8,128)(2,1)S(1)} %copy-done.10, ...), custom_call_target="tpu_custom_call" | custom-call | flops 1879048192 | bytes 5767168 | tf_op jit(solution)/shard_map/backward/pallas_call | solution.py:39
  84.4 1.9 %collective-permute-start.6 = (bf16[4,32,512]{2,1,0:T(8,128)(2,1)S(1)}, bf16[4,32,512]{2,1,0:T(8,128)(2,1)S(1)}, u32[]{:S(2)}, u32[]{:S(2)}) collective-permute-start(bf16[4,32,512]{2,1,0:T(8,128)(2,1)S(1)} %get-tuple-element.61), channel_id=1, source_target_pairs={{0,4},{2,6},{4,0},{6,2},{8,12},{10,14},{12,8},{14,10},{16,20},{18,... | collective-permute-start | bytes 393224 | tf_op jit(solution)/shard_map/ppermute | solution.py:332
  86.3 1.5 %collective-permute-start.5 = (bf16[4,32,512]{2,1,0:T(8,128)(2,1)S(1)}, bf16[4,32,512]{2,1,0:T(8,128)(2,1)S(1)}, u32[]{:S(2)}, u32[]{:S(2)}) collective-permute-start(bf16[4,32,512]{2,1,0:T(8,128)(2,1)S(1)} %get-tuple-element.62), channel_id=1, source_target_pairs={{0,2},{2,0},{4,6},{6,4},{8,10},{10,8},{12,14},{14,12},{16,18},{18,... | collective-permute-start | bytes 393224 | tf_op jit(solution)/shard_map/ppermute | solution.py:332
  87.8 0.2 collective-permute-start.7
  87.9 1.9 %local_forward.1.base_ref = f32[8,128,256]{2,1,0:T(8,128)S(1)} custom-call(s32[32]{0:T(128)S(1)} %bitcast.88, s32[32]{0:T(128)S(1)} %bitcast.90, bf16[32,128,128]{2,1,0:T(8,128)(2,1)S(1)} %bitcast.70, bf16[8,128,256]{2,1,0:T(8,128)(2,1)S(1)} %copy-done.12), custom_call_target="tpu_custom_call" | custom-call | flops 268435456 | bytes 2621440 | tf_op jit(solution)/shard_map/local_forward/pallas_call | solution.py:39
  89.8 1.9 %collective-permute-done.6 = bf16[4,32,512]{2,1,0:T(8,128)(2,1)S(1)} collective-permute-done((bf16[4,32,512]{2,1,0:T(8,128)(2,1)S(1)}, bf16[4,32,512]{2,1,0:T(8,128)(2,1)S(1)}, u32[]{:S(2)}, u32[]{:S(2)}) %collective-permute-start.6) | collective-permute-done | bytes 131104 | tf_op jit(solution)/shard_map/ppermute | solution.py:332
  91.8 4.2 %collective-permute-done.5 = bf16[4,32,512]{2,1,0:T(8,128)(2,1)S(1)} collective-permute-done((bf16[4,32,512]{2,1,0:T(8,128)(2,1)S(1)}, bf16[4,32,512]{2,1,0:T(8,128)(2,1)S(1)}, u32[]{:S(2)}, u32[]{:S(2)}) %collective-permute-start.5) | collective-permute-done | bytes 131104 | tf_op jit(solution)/shard_map/ppermute | solution.py:332
  96.0 5.0 %collective-permute-done.7 = bf16[4,32,512]{2,1,0:T(8,128)(2,1)S(1)} collective-permute-done((bf16[4,32,512]{2,1,0:T(8,128)(2,1)S(1)}, bf16[4,32,512]{2,1,0:T(8,128)(2,1)S(1)}, u32[]{:S(2)}, u32[]{:S(2)}) %collective-permute-start.7) | collective-permute-done | bytes 131104 | tf_op jit(solution)/shard_map/ppermute | solution.py:332
  101.0 0.1 fusion.2
  101.1 0.1 collective-permute-start.8
  101.2 5.6 %collective-permute-start.10 = (bf16[1,32,512]{2,1,0:T(8,128)(2,1)S(1)}, bf16[1,32,512]{2,1,0:T(8,128)(2,1)S(1)}, u32[]{:S(2)}, u32[]{:S(2)}) collective-permute-start(bf16[1,32,512]{2,1,0:T(8,128)(2,1)S(1)} %get-tuple-element.69), channel_id=1, source_target_pairs={{0,24},{2,26},{4,28},{6,30},{8,16},{10,18},{12,20},{14,22},{16,8},... | collective-permute-start | bytes 98312 | tf_op jit(solution)/shard_map/ppermute | solution.py:332
  106.8 2.2 %collective-permute-done.10 = bf16[1,32,512]{2,1,0:T(8,128)(2,1)S(1)} collective-permute-done((bf16[1,32,512]{2,1,0:T(8,128)(2,1)S(1)}, bf16[1,32,512]{2,1,0:T(8,128)(2,1)S(1)}, u32[]{:S(2)}, u32[]{:S(2)}) %collective-permute-start.10) | collective-permute-done | bytes 32800 | tf_op jit(solution)/shard_map/ppermute | solution.py:332
  109.1 2.6 %collective-permute-done.9 = bf16[1,32,512]{2,1,0:T(8,128)(2,1)S(1)} collective-permute-done((bf16[1,32,512]{2,1,0:T(8,128)(2,1)S(1)}, bf16[1,32,512]{2,1,0:T(8,128)(2,1)S(1)}, u32[]{:S(2)}, u32[]{:S(2)}) %collective-permute-start.9) | collective-permute-done | bytes 32800 | tf_op jit(solution)/shard_map/ppermute | solution.py:332
  111.6 1.0 collective-permute-start.13
  112.6 3.5 %collective-permute-start.11 = (bf16[1,32,512]{2,1,0:T(8,128)(2,1)S(1)}, bf16[1,32,512]{2,1,0:T(8,128)(2,1)S(1)}, u32[]{:S(2)}, u32[]{:S(2)}) collective-permute-start(bf16[1,32,512]{2,1,0:T(8,128)(2,1)S(1)} %fusion.8), channel_id=1, source_target_pairs={{0,8},{2,10},{4,12},{6,14},{8,0},{10,2},{12,4},{14,6},{16,24},{18,... | collective-permute-start | bytes 98312 | tf_op jit(solution)/shard_map/ppermute | solution.py:332
  116.1 1.4 %collective-permute-done.13 = bf16[1,32,512]{2,1,0:T(8,128)(2,1)S(1)} collective-permute-done((bf16[1,32,512]{2,1,0:T(8,128)(2,1)S(1)}, bf16[1,32,512]{2,1,0:T(8,128)(2,1)S(1)}, u32[]{:S(2)}, u32[]{:S(2)}) %collective-permute-start.13) | collective-permute-done | bytes 32800 | tf_op jit(solution)/shard_map/ppermute | solution.py:332
  117.5 0.8 collective-permute-done.12
  118.2 0.1 collective-permute-done.11
  118.3 1.3 collective-permute-start.16
  119.6 1.6 %collective-permute-start.15 = (bf16[4,32,512]{2,1,0:T(8,128)(2,1)S(1)}, bf16[4,32,512]{2,1,0:T(8,128)(2,1)S(1)}, u32[]{:S(2)}, u32[]{:S(2)}) collective-permute-start(bf16[4,32,512]{2,1,0:T(8,128)(2,1)S(1)} %maximum_bitcast_fusion), channel_id=1, source_target_pairs={{0,4},{2,6},{4,0},{6,2},{8,12},{10,14},{12,8},{14,10},{16,20},{18,... | collective-permute-start | bytes 393224 | tf_op jit(solution)/shard_map/ppermute | solution.py:332
  121.1 0.7 collective-permute-start.14
  121.9 3.1 %remote_forward.3 = bf16[8,128,256]{2,1,0:T(8,128)(2,1)} custom-call(s32[16]{0:T(128)S(1)} %bitcast.83, bf16[16,128,128]{2,1,0:T(8,128)(2,1)S(1)} %bitcast.68, bf16[16,128,256]{2,1,0:T(8,128)(2,1)} %all-to-all-done.1.recv_ref, f32[8,128,256]{2,1,0:T(8,128)S(1)} %local_forward.1.base_ref), custom_call_target="tpu_custom_call" | custom-call | flops 134217728 | bytes 3145728 | tf_op jit(solution)/shard_map/remote_forward/pallas_call | solution.py:39
  125.0 0.7 collective-permute-done.15
  125.7 0.5 collective-permute-done.14
  126.1 0.1 pad_maximum_fusion
  126.2 1.5 %finish_weights.1 = (f32[256,512]{1,0:T(8,128)}, f32[256,512]{1,0:T(8,128)}) custom-call(s32[2]{0:T(128)S(1)} %pad_add_fusion.place_ref, bf16[16,32,512]{2,1,0:T(8,128)(2,1)S(1)} %bitcast.71), custom_call_target="tpu_custom_call" | custom-call | bytes 1572864 | tf_op jit(solution)/shard_map/finish_weights/pallas_call | solution.py:39
  (55 shorter events, 0.2 us)
Async XLA Ops:
  4.3 8.5 %copy-start.26 = (bf16[256,512]{1,0:T(8,128)(2,1)S(1)}, bf16[256,512]{1,0:T(8,128)(2,1)}, u32[]{:S(2)}) copy-start(bf16[256,512]{1,0:T(8,128)(2,1)} %param.21) | copy-start | bytes 786436
  4.3 9.9 %copy-start.1 = (bf16[1,32,128,128]{3,2,1,0:T(8,128)(2,1)S(1)}, bf16[1,32,128,128]{3,2,1,0:T(8,128)(2,1)}, u32[]{:S(2)}) copy-start(bf16[1,32,128,128]{3,2,1,0:T(8,128)(2,1)} %param.18) | copy-start | bytes 3145732
  4.3 9.9 %copy-start.20 = (s32[1,32]{1,0:T(1,128)S(1)}, s32[1,32]{1,0:T(1,128)}, u32[]{:S(2)}) copy-start(s32[1,32]{1,0:T(1,128)} %param.19) | copy-start | bytes 388
  4.3 9.9 %copy-start.21 = (s32[1,32]{1,0:T(1,128)S(1)}, s32[1,32]{1,0:T(1,128)}, u32[]{:S(2)}) copy-start(s32[1,32]{1,0:T(1,128)} %param.20) | copy-start | bytes 388
  4.3 51.5 %all-to-all-start = ((bf16[16,256,256]{2,1,0:T(8,128)(2,1)}), bf16[16,256,256]{2,1,0:T(8,128)(2,1)S(1)}, u32[]{:S(2)}, u32[]{:S(2)}) async-start(bf16[16,256,256]{2,1,0:T(8,128)(2,1)} %prepare.1), calls=%async_computation | async-start | bytes 4194304 | tf_op jit(solution)/shard_map/all_to_all | solution.py:357
  12.8 9.0 %collective-permute-start = (bf16[256,512]{1,0:T(8,128)(2,1)S(1)}, bf16[256,512]{1,0:T(8,128)(2,1)}, u32[]{:S(2)}, u32[]{:S(2)}) collective-permute-start(bf16[256,512]{1,0:T(8,128)(2,1)S(1)} %copy-done.26), channel_id=1, source_target_pairs={{0,1},{1,0},{2,3},{3,2},{4,5},{5,4},{6,7},{7,6},{8,9},{9,8},{10,11... | collective-permute-start | bytes 786440 | tf_op jit(solution)/shard_map/ppermute | solution.py:361
  12.8 10.6 %collective-permute-start.1 = (bf16[256,512]{1,0:T(8,128)(2,1)}, bf16[256,512]{1,0:T(8,128)(2,1)}, u32[]{:S(2)}, u32[]{:S(2)}) collective-permute-start(bf16[256,512]{1,0:T(8,128)(2,1)} %param.22), channel_id=1, source_target_pairs={{0,1},{1,0},{2,3},{3,2},{4,5},{5,4},{6,7},{7,6},{8,9},{9,8},{10,11... | collective-permute-start | bytes 786440 | tf_op jit(solution)/shard_map/ppermute | solution.py:361
  13.3 13.4 %collective-permute-start.2 = (bf16[1024,256]{1,0:T(8,128)(2,1)}, bf16[1024,256]{1,0:T(8,128)(2,1)}, u32[]{:S(2)}, u32[]{:S(2)}) collective-permute-start(bf16[1024,256]{1,0:T(8,128)(2,1)} %hist_ref.1), channel_id=1, source_target_pairs={{0,1},{1,0},{2,3},{3,2},{4,5},{5,4},{6,7},{7,6},{8,9},{9,8},{10,11... | collective-permute-start | bytes 1572872 | tf_op jit(solution)/shard_map/ppermute | solution.py:361
  14.1 1.0 copy-start.3
  15.2 1.0 copy-start.4
  18.9 1.0 copy-start.5
  19.8 1.0 copy-start.7
  23.5 2.3 %copy-start.25 = (bf16[512,512]{1,0:T(8,128)(2,1)S(1)}, bf16[512,512]{1,0:T(8,128)(2,1)}, u32[]{:S(2)}) copy-start(bf16[512,512]{1,0:T(8,128)(2,1)} %constant_dynamic-update-slice_fusion) | copy-start | bytes 1572868
  25.6 2.5 %copy-start.9 = (bf16[1024,256]{1,0:T(8,128)(2,1)S(1)}, bf16[1024,256]{1,0:T(8,128)(2,1)}, u32[]{:S(2)}) copy-start(bf16[1024,256]{1,0:T(8,128)(2,1)} %hist_ref.1) | copy-start | bytes 1572868
  26.7 29.1 %copy-start = (bf16[1,16,128,128]{3,2,1,0:T(8,128)(2,1)S(1)}, bf16[1,16,128,128]{3,2,1,0:T(8,128)(2,1)}, u32[]{:S(2)}) copy-start(bf16[1,16,128,128]{3,2,1,0:T(8,128)(2,1)} %param.14) | copy-start | bytes 1572868
  26.7 29.1 %copy-start.18 = (s32[1,16]{1,0:T(1,128)S(1)}, s32[1,16]{1,0:T(1,128)}, u32[]{:S(2)}) copy-start(s32[1,16]{1,0:T(1,128)} %param.15) | copy-start | bytes 196
  55.8 1.2 copy-start.8
  57.1 1.5 %copy-start.6 = (f32[8,128,256]{2,1,0:T(8,128)S(1)}, f32[8,128,256]{2,1,0:T(8,128)}, u32[]{:S(2)}) copy-start(f32[8,128,256]{2,1,0:T(8,128)} %copy-done.5) | copy-start | bytes 3145732
  57.1 1.5 %copy-start.19 = (s32[1,16]{1,0:T(1,128)S(1)}, s32[1,16]{1,0:T(1,128)}, u32[]{:S(2)}) copy-start(s32[1,16]{1,0:T(1,128)} %param.16) | copy-start | bytes 196
  57.1 1.5 %copy-start.22 = (s32[1,16]{1,0:T(1,128)S(1)}, s32[1,16]{1,0:T(1,128)}, u32[]{:S(2)}) copy-start(s32[1,16]{1,0:T(1,128)} %param.17) | copy-start | bytes 196
  58.5 2.7 %copy-start.13 = (bf16[8,128,256]{2,1,0:T(8,128)(2,1)}, bf16[8,128,256]{2,1,0:T(8,128)(2,1)S(1)}, u32[]{:S(2)}) copy-start(bf16[8,128,256]{2,1,0:T(8,128)(2,1)S(1)} %remote_forward.2) | copy-start | bytes 1572868
  58.5 2.7 %collective-permute-start.3 = (bf16[1024,256]{1,0:T(8,128)(2,1)S(1)}, bf16[1024,256]{1,0:T(8,128)(2,1)S(1)}, u32[]{:S(2)}, u32[]{:S(2)}) collective-permute-start(bf16[1024,256]{1,0:T(8,128)(2,1)S(1)} %bitcast.76), channel_id=1, source_target_pairs={{0,1},{1,0},{2,3},{3,2},{4,5},{5,4},{6,7},{7,6},{8,9},{9,8},{10,11... | collective-permute-start | bytes 1572872 | tf_op jit(solution)/shard_map/ppermute | solution.py:361
  58.6 2.6 %copy-start.15 = (bf16[512,512]{1,0:T(8,128)(2,1)S(1)}, bf16[512,512]{1,0:T(8,128)(2,1)}, u32[]{:S(2)}) copy-start(bf16[512,512]{1,0:T(8,128)(2,1)} %maximum_select_fusion.wi_ref) | copy-start | bytes 1572868
  58.6 2.6 %copy-start.17 = (bf16[1024,256]{1,0:T(8,128)(2,1)S(1)}, bf16[1024,256]{1,0:T(8,128)(2,1)}, u32[]{:S(2)}) copy-start(bf16[1024,256]{1,0:T(8,128)(2,1)} %copy.16) | copy-start | bytes 1572868
  60.7 15.3 %copy-start.10 = (bf16[1024,256]{1,0:T(8,128)(2,1)S(1)}, bf16[1024,256]{1,0:T(8,128)(2,1)}, u32[]{:S(2)}) copy-start(bf16[1024,256]{1,0:T(8,128)(2,1)} %hist_ref.1) | copy-start | bytes 1572868
  60.7 15.3 %collective-permute-start.4 = (bf16[2,1024,256]{2,1,0:T(8,128)(2,1)}, bf16[2,1024,256]{2,1,0:T(8,128)(2,1)}, u32[]{:S(2)}, u32[]{:S(2)}) collective-permute-start(bf16[2,1024,256]{2,1,0:T(8,128)(2,1)} %bitcast.14.sm_ref), channel_id=1, source_target_pairs={{0,1},{1,0},{2,3},{3,2},{4,5},{5,4},{6,7},{7,6},{8,9},{9,8},{10,11... | collective-permute-start | bytes 3145736 | tf_op jit(solution)/shard_map/ppermute | solution.py:361
  61.2 3.8 %copy-start.23 = (bf16[1024,256]{1,0:T(8,128)(2,1)}, bf16[1024,256]{1,0:T(8,128)(2,1)S(1)}, u32[]{:S(2)}) copy-start(bf16[1024,256]{1,0:T(8,128)(2,1)S(1)} %collective-permute-done.3.zo_ref) | copy-start | bytes 1572868
  65.0 0.8 copy-start.11
  65.8 10.2 %copy-start.14 = (bf16[8,128,256]{2,1,0:T(8,128)(2,1)S(1)}, bf16[8,128,256]{2,1,0:T(8,128)(2,1)}, u32[]{:S(2)}) copy-start(bf16[8,128,256]{2,1,0:T(8,128)(2,1)} %copy-done.13) | copy-start | bytes 1572868
  65.8 52.5 %all-to-all-start.1 = ((bf16[16,128,256]{2,1,0:T(8,128)(2,1)}), bf16[16,128,256]{2,1,0:T(8,128)(2,1)}, u32[]{:S(2)}, u32[]{:S(2)}) async-start(bf16[16,128,256]{2,1,0:T(8,128)(2,1)} %get-tuple-element.51), calls=%async_computation.1 | async-start | bytes 2097152 | tf_op jit(solution)/shard_map/all_to_all | solution.py:357
  76.0 11.9 %copy-start.2 = (bf16[1,32,128,128]{3,2,1,0:T(8,128)(2,1)S(1)}, bf16[1,32,128,128]{3,2,1,0:T(8,128)(2,1)}, u32[]{:S(2)}) copy-start(bf16[1,32,128,128]{3,2,1,0:T(8,128)(2,1)} %param.18) | copy-start | bytes 3145732
  76.0 11.9 %copy-start.12 = (bf16[8,128,256]{2,1,0:T(8,128)(2,1)S(1)}, bf16[8,128,256]{2,1,0:T(8,128)(2,1)}, u32[]{:S(2)}) copy-start(bf16[8,128,256]{2,1,0:T(8,128)(2,1)} %copy-done.11) | copy-start | bytes 1572868
  76.0 1.2 copy-start.16
  77.2 1.0 copy-start.24
  84.4 7.4 %collective-permute-start.6 = (bf16[4,32,512]{2,1,0:T(8,128)(2,1)S(1)}, bf16[4,32,512]{2,1,0:T(8,128)(2,1)S(1)}, u32[]{:S(2)}, u32[]{:S(2)}) collective-permute-start(bf16[4,32,512]{2,1,0:T(8,128)(2,1)S(1)} %get-tuple-element.61), channel_id=1, source_target_pairs={{0,4},{2,6},{4,0},{6,2},{8,12},{10,14},{12,8},{14,10},{16,20},{18,... | collective-permute-start | bytes 393224 | tf_op jit(solution)/shard_map/ppermute | solution.py:332
  86.3 9.7 %collective-permute-start.5 = (bf16[4,32,512]{2,1,0:T(8,128)(2,1)S(1)}, bf16[4,32,512]{2,1,0:T(8,128)(2,1)S(1)}, u32[]{:S(2)}, u32[]{:S(2)}) collective-permute-start(bf16[4,32,512]{2,1,0:T(8,128)(2,1)S(1)} %get-tuple-element.62), channel_id=1, source_target_pairs={{0,2},{2,0},{4,6},{6,4},{8,10},{10,8},{12,14},{14,12},{16,18},{18,... | collective-permute-start | bytes 393224 | tf_op jit(solution)/shard_map/ppermute | solution.py:332
  87.8 13.2 %collective-permute-start.7 = (bf16[4,32,512]{2,1,0:T(8,128)(2,1)S(1)}, bf16[4,32,512]{2,1,0:T(8,128)(2,1)S(1)}, u32[]{:S(2)}, u32[]{:S(2)}) collective-permute-start(bf16[4,32,512]{2,1,0:T(8,128)(2,1)S(1)} %get-tuple-element.63), channel_id=1, source_target_pairs={{0,6},{2,4},{4,2},{6,0},{8,14},{10,12},{12,10},{14,8},{16,22},{18,... | collective-permute-start | bytes 393224 | tf_op jit(solution)/shard_map/ppermute | solution.py:332
  101.1 5.7 %collective-permute-start.8 = (bf16[1,32,512]{2,1,0:T(8,128)(2,1)S(1)}, bf16[1,32,512]{2,1,0:T(8,128)(2,1)S(1)}, u32[]{:S(2)}, u32[]{:S(2)}) collective-permute-start(bf16[1,32,512]{2,1,0:T(8,128)(2,1)S(1)} %get-tuple-element.68), channel_id=1, source_target_pairs={{0,8},{2,10},{4,12},{6,14},{8,0},{10,2},{12,4},{14,6},{16,24},{18,... | collective-permute-start | bytes 98312 | tf_op jit(solution)/shard_map/ppermute | solution.py:332
  101.2 7.9 %collective-permute-start.10 = (bf16[1,32,512]{2,1,0:T(8,128)(2,1)S(1)}, bf16[1,32,512]{2,1,0:T(8,128)(2,1)S(1)}, u32[]{:S(2)}, u32[]{:S(2)}) collective-permute-start(bf16[1,32,512]{2,1,0:T(8,128)(2,1)S(1)} %get-tuple-element.69), channel_id=1, source_target_pairs={{0,24},{2,26},{4,28},{6,30},{8,16},{10,18},{12,20},{14,22},{16,8},... | collective-permute-start | bytes 98312 | tf_op jit(solution)/shard_map/ppermute | solution.py:332
  106.8 4.8 %collective-permute-start.9 = (bf16[1,32,512]{2,1,0:T(8,128)(2,1)S(1)}, bf16[1,32,512]{2,1,0:T(8,128)(2,1)S(1)}, u32[]{:S(2)}, u32[]{:S(2)}) collective-permute-start(bf16[1,32,512]{2,1,0:T(8,128)(2,1)S(1)} %get-tuple-element.70), channel_id=1, source_target_pairs={{0,16},{2,18},{4,20},{6,22},{8,24},{10,26},{12,28},{14,30},{16,0},... | collective-permute-start | bytes 98312 | tf_op jit(solution)/shard_map/ppermute | solution.py:332
  111.6 5.8 %collective-permute-start.13 = (bf16[1,32,512]{2,1,0:T(8,128)(2,1)S(1)}, bf16[1,32,512]{2,1,0:T(8,128)(2,1)S(1)}, u32[]{:S(2)}, u32[]{:S(2)}) collective-permute-start(bf16[1,32,512]{2,1,0:T(8,128)(2,1)S(1)} %fusion.8), channel_id=1, source_target_pairs={{0,24},{2,26},{4,28},{6,30},{8,16},{10,18},{12,20},{14,22},{16,8},... | collective-permute-start | bytes 98312 | tf_op jit(solution)/shard_map/ppermute | solution.py:332
  112.6 5.6 %collective-permute-start.12 = (bf16[1,32,512]{2,1,0:T(8,128)(2,1)S(1)}, bf16[1,32,512]{2,1,0:T(8,128)(2,1)S(1)}, u32[]{:S(2)}, u32[]{:S(2)}) collective-permute-start(bf16[1,32,512]{2,1,0:T(8,128)(2,1)S(1)} %fusion.8), channel_id=1, source_target_pairs={{0,16},{2,18},{4,20},{6,22},{8,24},{10,26},{12,28},{14,30},{16,0},... | collective-permute-start | bytes 98312 | tf_op jit(solution)/shard_map/ppermute | solution.py:332
  112.6 5.7 %collective-permute-start.11 = (bf16[1,32,512]{2,1,0:T(8,128)(2,1)S(1)}, bf16[1,32,512]{2,1,0:T(8,128)(2,1)S(1)}, u32[]{:S(2)}, u32[]{:S(2)}) collective-permute-start(bf16[1,32,512]{2,1,0:T(8,128)(2,1)S(1)} %fusion.8), channel_id=1, source_target_pairs={{0,8},{2,10},{4,12},{6,14},{8,0},{10,2},{12,4},{14,6},{16,24},{18,... | collective-permute-start | bytes 98312 | tf_op jit(solution)/shard_map/ppermute | solution.py:332
  118.3 6.7 %collective-permute-start.16 = (bf16[4,32,512]{2,1,0:T(8,128)(2,1)S(1)}, bf16[4,32,512]{2,1,0:T(8,128)(2,1)S(1)}, u32[]{:S(2)}, u32[]{:S(2)}) collective-permute-start(bf16[4,32,512]{2,1,0:T(8,128)(2,1)S(1)} %maximum_bitcast_fusion), channel_id=1, source_target_pairs={{0,6},{2,4},{4,2},{6,0},{8,14},{10,12},{12,10},{14,8},{16,22},{18,... | collective-permute-start | bytes 393224 | tf_op jit(solution)/shard_map/ppermute | solution.py:332
  119.6 6.1 %collective-permute-start.15 = (bf16[4,32,512]{2,1,0:T(8,128)(2,1)S(1)}, bf16[4,32,512]{2,1,0:T(8,128)(2,1)S(1)}, u32[]{:S(2)}, u32[]{:S(2)}) collective-permute-start(bf16[4,32,512]{2,1,0:T(8,128)(2,1)S(1)} %maximum_bitcast_fusion), channel_id=1, source_target_pairs={{0,4},{2,6},{4,0},{6,2},{8,12},{10,14},{12,8},{14,10},{16,20},{18,... | collective-permute-start | bytes 393224 | tf_op jit(solution)/shard_map/ppermute | solution.py:332
  121.1 5.0 %collective-permute-start.14 = (bf16[4,32,512]{2,1,0:T(8,128)(2,1)S(1)}, bf16[4,32,512]{2,1,0:T(8,128)(2,1)S(1)}, u32[]{:S(2)}, u32[]{:S(2)}) collective-permute-start(bf16[4,32,512]{2,1,0:T(8,128)(2,1)S(1)} %maximum_bitcast_fusion), channel_id=1, source_target_pairs={{0,2},{2,0},{4,6},{6,4},{8,10},{10,8},{12,14},{14,12},{16,18},{18,... | collective-permute-start | bytes 393224 | tf_op jit(solution)/shard_map/ppermute | solution.py:332

commit v3 on v2

--- a/solution.py
+++ b/solution.py
@@ -52,6 +52,32 @@
     )(*scalars, *arrays)
 
 
+def direct(body, scalars, arrays, in_spaces, out_shape, out_spaces, scratch=(), flops=0, name=None, vmem=None):
+    inside = [a for a, space in zip(arrays + out_shape, in_spaces + out_spaces) if space is pltpu.VMEM]
+    sizes = [math.prod(a.shape) * jnp.dtype(a.dtype).itemsize for a in inside]
+    sizes += [math.prod(a.shape) * jnp.dtype(a.dtype).itemsize for a in scratch if getattr(a, "memory_space", None) is pltpu.VMEM]
+    moved = sum(math.prod(a.shape) * jnp.dtype(a.dtype).itemsize for a in arrays + out_shape)
+    return pl.pallas_call(
+        body,
+        in_specs=[pl.BlockSpec(memory_space=pltpu.SMEM)] * len(scalars)
+        + [pl.BlockSpec(memory_space=space) for space in in_spaces],
+        out_specs=[pl.BlockSpec(memory_space=space) for space in out_spaces],
+        out_shape=out_shape,
+        scratch_shapes=list(scratch),
+        compiler_params=pltpu.CompilerParams(vmem_limit_bytes=vmem or sum(sizes) + VMEM_SPARE),
+        cost_estimate=pl.CostEstimate(flops=int(flops), bytes_accessed=int(moved), transcendentals=0),
+        name=name,
+    )(*scalars, *arrays)
+
+
+def each(count, step):
+    if count <= 4:
+        for i in range(count):
+            step(i)
+    else:
+        pl.loop(0, count)(step)
+
+
 def whole(shape):
     return pl.BlockSpec(shape, lambda i, *_: (0,) * len(shape))
 
@@ -69,18 +95,55 @@
     width = nodes.shape[2]
     group = group_of(peers)
 
-    def body(ids_ref, dst_ref, tiles_ref, nodes_ref, grads_ref, out_ref):
-        step = pl.program_id(0)
-        for j in range(group):
-            out_ref[j, :tile] = nodes_ref[ids_ref[step * group + j]]
-            out_ref[j, tile:] = dot_t(tiles_ref[j], grads_ref[dst_ref[step * group + j]]).astype(BF16)
-
-    return call(
-        body, (ids, targets), (tiles, nodes, grads), (peers // group,),
-        [lead((group, tile, tile)), whole(nodes.shape), whole(grads.shape)], lead((group, 2 * tile, width)),
-        jax.ShapeDtypeStruct((peers, 2 * tile, width), BF16),
+    def body(ids_ref, dst_ref, tiles_hbm, nodes_hbm, grads_hbm, out_hbm, tiles_ref, nodes_ref, grads_ref, back_ref, in_sem, tile_sem, pick_sem, out_sem):
+        def tiles_in(g):
+            part = pl.ds(g * group, group)
+            return pltpu.make_async_copy(tiles_hbm.at[part], tiles_ref.at[part], tile_sem.at[g])
+
+        def pick(p):
+            return pltpu.make_async_copy(nodes_ref.at[ids_ref[p]], out_hbm.at[p, pl.ds(0, tile)], pick_sem.at[p])
+
+        def give(p):
+            return pltpu.make_async_copy(back_ref.at[p], out_hbm.at[p, pl.ds(tile, tile)], out_sem.at[p])
+
+        def picks(g):
+            for j in range(group):
+                pick(g * group + j).start()
+
+        nodes_in = pltpu.make_async_copy(nodes_hbm, nodes_ref, in_sem.at[0])
+        grads_in = pltpu.make_async_copy(grads_hbm, grads_ref, in_sem.at[1])
+        nodes_in.start()
+        grads_in.start()
+        each(peers // group, lambda g: tiles_in(g).start())
+        nodes_in.wait()
+        each(peers // group, picks)
+        grads_in.wait()
+
+        def work(g):
+            tiles_in(g).wait()
+            for j in range(group):
+                p = g * group + j
+                back_ref[p] = dot_t(tiles_ref[p], grads_ref[dst_ref[p]]).astype(BF16)
+                give(p).start()
+
+        def finish(g):
+            for j in range(group):
+                give(g * group + j).wait()
+                pick(g * group + j).wait()
+
+        each(peers // group, work)
+        each(peers // group, finish)
+
+    return direct(
+        body, (ids, targets), [tiles, nodes, grads], [pltpu.HBM] * 3,
+        [jax.ShapeDtypeStruct((peers, 2 * tile, width), BF16)], [pltpu.HBM],
+        [
+            pltpu.VMEM(tiles.shape, BF16), pltpu.VMEM(nodes.shape, BF16), pltpu.VMEM(grads.shape, BF16),
+            pltpu.VMEM((peers, tile, width), BF16), pltpu.SemaphoreType.DMA((2,)), pltpu.SemaphoreType.DMA((peers // group,)),
+            pltpu.SemaphoreType.DMA((peers,)), pltpu.SemaphoreType.DMA((peers,)),
+        ],
         flops=2 * peers * tile * tile * width, name="prepare", vmem=VMEM_MOST,
-    )
+    )[0]
 
 
 def local_both(sources, targets, tiles, nodes, grads):
@@ -134,112 +197,127 @@
     )
 
 
+def streamed(received, offset, tile, buffer, sems, group):
+    def copy(g):
+        part = pl.ds(g * group, group)
+        return pltpu.make_async_copy(received.at[part, pl.ds(offset, tile)], buffer.at[part], sems.at[g])
+
+    return copy
+
+
 def remote_forward(targets, tiles, received, base):
     peers, tile, _ = tiles.shape
     width = received.shape[2]
-    group = group_of(peers)
-    steps = peers // group
-
-    def body(dst_ref, tiles_ref, recv_ref, base_ref, out_ref, acc_ref):
-        step = pl.program_id(0)
-
-        @pl.when(step == 0)
-        def _():
-            acc_ref[...] = base_ref[...]
-
-        for j in range(group):
-            acc_ref[dst_ref[step * group + j]] += dot(tiles_ref[j], recv_ref[j])
-
-        @pl.when(step == steps - 1)
-        def _():
-            out_ref[...] = acc_ref[...].astype(BF16)
-
-    return call(
-        body, (targets,), (tiles, received, base), (steps,),
-        [lead((group, tile, tile)), lead((group, tile, width)), whole(base.shape)],
-        whole(base.shape), jax.ShapeDtypeStruct(base.shape, BF16),
-        [pltpu.VMEM(base.shape, F32)],
+    group = 4 if peers % 4 == 0 else 1
+
+    def body(dst_ref, tiles_ref, recv_hbm, base_ref, out_ref, recv_ref, acc_ref, sems):
+        copy = streamed(recv_hbm, 0, tile, recv_ref, sems, group)
+        each(peers // group, lambda g: copy(g).start())
+        acc_ref[...] = base_ref[...]
+
+        def work(g):
+            copy(g).wait()
+            for j in range(group):
+                p = g * group + j
+                acc_ref[dst_ref[p]] += dot(tiles_ref[p], recv_ref[p])
+
+        each(peers // group, work)
+        out_ref[...] = acc_ref[...].astype(BF16)
+
+    return direct(
+        body, (targets,), [tiles, received, base], [pltpu.VMEM, pltpu.HBM, pltpu.VMEM],
+        [jax.ShapeDtypeStruct(base.shape, BF16)], [pltpu.VMEM],
+        [
+            pltpu.VMEM((peers, tile, width), BF16), pltpu.VMEM(base.shape, F32),
+            pltpu.SemaphoreType.DMA((peers // group,)),
+        ],
         flops=2 * peers * tile * tile * width, name="remote_forward",
-    )
-
-
-def silu_parts(z_mine, z_other, w_in):
+    )[0]
+
+
+def layer_one(z_mine, z_other, w_in):
     half = z_mine.shape[1]
     pre = dot(z_mine, w_in[:half]) + dot(z_other, w_in[half:])
-    return pre, 1.0 / (1.0 + jnp.exp(-pre))
+    return pre, 0.5 * jnp.tanh(0.5 * pre) + 0.5
 
 
 def middle(ids, flags, z_mine, z_other, w_in, w_out, hist_out):
     rows, half = z_mine.shape
     peers = ids.shape[0]
     count, tile, _ = hist_out.shape
-    per = 2 if count % 2 == 0 else 1
-    steps = count // per
-    span = per * tile
-
-    def body(ids_ref, flag_ref, zm_ref, zo_ref, wi_ref, wo_ref, hw_ref, prod_ref, send_ref):
-        step = pl.program_id(0)
-        pre, s = silu_parts(zm_ref[...], zo_ref[...], wi_ref[...])
-        prod = dot((pre * s).astype(BF16), wo_ref[:, :half]).astype(BF16)
-        for j in range(per):
-            prod_ref[step * per + j] = prod[j * tile : (j + 1) * tile]
-
-        @pl.when(step == steps - 1)
-        def _():
-            for p in range(peers):
-                fresh = flag_ref[p] == 1
-                block = ids_ref[p]
-
-                @pl.when(fresh)
-                def _():
-                    send_ref[p] = prod_ref[block]
-
-                @pl.when(jnp.logical_not(fresh))
-                def _():
-                    send_ref[p] = hw_ref[block]
-
-    return call(
-        body, (ids, flags), (z_mine, z_other, w_in, w_out, hist_out), (steps,),
-        [lead((span, half)), lead((span, half)), whole(w_in.shape), whole(w_out.shape), whole(hist_out.shape)],
-        [whole(hist_out.shape), whole((peers, tile, half))],
+    group = group_of(peers)
+
+    def body(ids_ref, flag_ref, zm_ref, zo_ref, wi_ref, wo_ref, hw_ref, prod_ref, send_hbm, sems):
+        def supply(source, p):
+            return pltpu.make_async_copy(source.at[ids_ref[p]], send_hbm.at[p], sems.at[p])
+
+        def stored(g):
+            for j in range(group):
+                p = g * group + j
+                pl.when(flag_ref[p] != 1)(lambda: supply(hw_ref, p).start())
+
+        def fresh(g):
+            for j in range(group):
+                p = g * group + j
+                pl.when(flag_ref[p] == 1)(lambda: supply(prod_ref, p).start())
+
+        def finish(g):
+            for j in range(group):
+                supply(hw_ref, g * group + j).wait()
+
+        each(peers // group, stored)
+        per = 2 if count % 2 == 0 else 1
+        for r in range(count // per):
+            part = slice(r * per * tile, (r + 1) * per * tile)
+            pre, s = layer_one(zm_ref[part], zo_ref[part], wi_ref)
+            prod = dot((pre * s).astype(BF16), wo_ref[:, :half]).astype(BF16)
+            prod_ref[r * per : (r + 1) * per] = prod.reshape(per, tile, half)
+        each(peers // group, fresh)
+        each(peers // group, finish)
+
+    return direct(
+        body, (ids, flags), [z_mine, z_other, w_in, w_out, hist_out], [pltpu.VMEM] * 5,
         [
             jax.ShapeDtypeStruct(hist_out.shape, BF16),
             jax.ShapeDtypeStruct((peers, tile, half), BF16),
         ],
-        flops=12 * rows * half * half, name="middle",
+        [pltpu.VMEM, pltpu.HBM],
+        [pltpu.SemaphoreType.DMA((peers,))],
+        flops=120 * rows * half * half, name="middle",
     )
 
 
 def gather_grads(ids, flags, returned, base):
     peers = returned.shape[0]
     count, tile, width = base.shape
-    group = group_of(peers)
-    steps = peers // group
-
-    def body(ids_ref, flag_ref, ret_ref, base_ref, out_ref, acc_ref):
-        step = pl.program_id(0)
-
-        @pl.when(step == 0)
-        def _():
-            acc_ref[0] = base_ref[...]
-            acc_ref[1] = jnp.zeros_like(base_ref)
-
-        for j in range(group):
-            p = step * group + j
-            side = jnp.where(flag_ref[p] == 1, 0, 1)
-            acc_ref[side, ids_ref[p]] += ret_ref[j].astype(F32)
-
-        @pl.when(step == steps - 1)
-        def _():
-            out_ref[...] = acc_ref[...].astype(BF16)
-
+    group = 4 if peers % 4 == 0 else 1
     both = (2,) + base.shape
-    return call(
-        body, (ids, flags), (returned, base), (steps,),
-        [pl.BlockSpec((group, tile, width), lambda i, *_: (i, 1, 0)), whole(base.shape)],
-        whole(both), jax.ShapeDtypeStruct(both, BF16),
-        [pltpu.VMEM(both, F32)], name="gather_grads",
-    )
+
+    def body(ids_ref, flag_ref, ret_hbm, base_ref, out_ref, ret_ref, acc_ref, sems):
+        copy = streamed(ret_hbm, tile, tile, ret_ref, sems, group)
+        each(peers // group, lambda g: copy(g).start())
+        acc_ref[0] = base_ref[...]
+        acc_ref[1] = jnp.zeros_like(base_ref)
+
+        def work(g):
+            copy(g).wait()
+            for j in range(group):
+                p = g * group + j
+                side = jnp.where(flag_ref[p] == 1, 0, 1)
+                acc_ref[side, ids_ref[p]] += ret_ref[p].astype(F32)
+
+        each(peers // group, work)
+        out_ref[...] = acc_ref[...].astype(BF16)
+
+    return direct(
+        body, (ids, flags), [returned, base], [pltpu.HBM, pltpu.VMEM],
+        [jax.ShapeDtypeStruct(both, BF16)], [pltpu.VMEM],
+        [
+            pltpu.VMEM((peers, tile, width), BF16), pltpu.VMEM(both, F32),
+            pltpu.SemaphoreType.DMA((peers // group,)),
+        ],
+        flops=32 * peers * tile * tile * width, name="gather_grads",
+    )[0]
 
 
 def chunking(peers, total, width):
@@ -250,49 +328,71 @@
 
 def backward(place, sums_mine, sums_other, history, z_mine, z_other, w_in, w_out, peers):
     _, rows, half = sums_mine.shape
-    step_rows = rows // 4
     row_chunks, col_chunks, chunk_rows, chunk_cols = chunking(peers, 2 * half, 2 * half)
-
-    def body(place_ref, sm_ref, so_ref, hist_ref, zm_ref, zo_ref, wi_ref, wo_ref, gh_ref, chunk_ref, acc_ref):
-        step = pl.program_id(0)
+    parts = 4
+    span = rows // parts
+
+    def body(place_ref, sm_hbm, so_hbm, hist_ref, zm_ref, zo_ref, wi_ref, wo_ref, gh_hbm, chunk_ref, sm_ref, so_ref, gh_ref, acc_ref, sm_sem, so_sem, gh_sem):
         me, side = place_ref[0], place_ref[1]
-
-        @pl.when(step == 0)
-        def _():
-            acc_ref[...] = jnp.zeros_like(acc_ref)
-
-        z = zm_ref[...]
-        pre, s = silu_parts(z, zo_ref[...], wi_ref[...])
-        dh = dot_nt(sm_ref[0], wo_ref[:, :half]) + dot_nt(so_ref[0], wo_ref[:, half:])
-        gh_ref[...] = dh[:, :half].astype(BF16)
-        dpre = (dh * s * (1.0 + pre * (1.0 - s))).astype(BF16)
-        hid = (pre[:, :half] * s[:, :half]).astype(BF16)
-        hist = hist_ref[...]
         own = pl.ds(pl.multiple_of(side * half, half), half)
         far = pl.ds(pl.multiple_of((1 - side) * half, half), half)
-        acc_ref[:half, own] += dot_t(z, dpre[:, :half])
-        acc_ref[:half, far] += dot_t(z, dpre[:, half:])
-        acc_ref[half:, own] += dot_t(hid, sm_ref[0]) + dot_t(hist, sm_ref[1])
-        acc_ref[half:, far] += dot_t(hid, so_ref[0]) + dot_t(hist, so_ref[1])
-
-        @pl.when(step == 3)
-        def _():
-            for c in range(peers):
-                r, k = c // col_chunks, c % col_chunks
-                piece = acc_ref[r * chunk_rows : (r + 1) * chunk_rows, k * chunk_cols : (k + 1) * chunk_cols]
-                chunk_ref[c ^ me] = piece.astype(BF16)
-
-    sums_spec = pl.BlockSpec((2, step_rows, half), lambda i, *_: (0, i, 0))
-    some = lead((step_rows, half))
-    return call(
-        body, (place,), (sums_mine, sums_other, history, z_mine, z_other, w_in, w_out), (4,),
-        [sums_spec, sums_spec, some, some, some, whole(w_in.shape), whole(w_out.shape)],
-        [some, whole((peers, chunk_rows, chunk_cols))],
+
+        def sums_in(r):
+            part = pl.ds(r * span, span)
+            return (
+                pltpu.make_async_copy(sm_hbm.at[:, part], sm_ref.at[:, part], sm_sem.at[r]),
+                pltpu.make_async_copy(so_hbm.at[:, part], so_ref.at[:, part], so_sem.at[r]),
+            )
+
+        def gh_out(r):
+            part = pl.ds(r * span, span)
+            return pltpu.make_async_copy(gh_ref.at[part], gh_hbm.at[part], gh_sem.at[r])
+
+        for r in range(parts):
+            for copy in sums_in(r):
+                copy.start()
+        for r in range(parts):
+            part = slice(r * span, (r + 1) * span)
+
+            def add(rows_, cols, value):
+                if r == 0:
+                    acc_ref[rows_, cols] = value
+                else:
+                    acc_ref[rows_, cols] += value
+
+            z, hist = zm_ref[part], hist_ref[part]
+            pre, s = layer_one(z, zo_ref[part], wi_ref)
+            hid = (pre[:, :half] * s[:, :half]).astype(BF16)
+            for copy in sums_in(r):
+                copy.wait()
+            dh = dot_nt(sm_ref[0, part], wo_ref[:, :half]) + dot_nt(so_ref[0, part], wo_ref[:, half:])
+            gh_ref[part] = dh[:, :half].astype(BF16)
+            gh_out(r).start()
+            dpre = (dh * s * (1.0 + pre * (1.0 - s))).astype(BF16)
+            add(slice(0, half), own, dot_t(z, dpre[:, :half]))
+            add(slice(0, half), far, dot_t(z, dpre[:, half:]))
+            add(slice(half, 2 * half), own, dot_t(hid, sm_ref[0, part]) + dot_t(hist, sm_ref[1, part]))
+            add(slice(half, 2 * half), far, dot_t(hid, so_ref[0, part]) + dot_t(hist, so_ref[1, part]))
+        for c in range(peers):
+            r, k = c // col_chunks, c % col_chunks
+            piece = acc_ref[r * chunk_rows : (r + 1) * chunk_rows, k * chunk_cols : (k + 1) * chunk_cols]
+            chunk_ref[c ^ me] = piece.astype(BF16)
+        for r in range(parts):
+            gh_out(r).wait()
+
+    return direct(
+        body, (place,), [sums_mine, sums_other, history, z_mine, z_other, w_in, w_out],
+        [pltpu.HBM] * 2 + [pltpu.VMEM] * 5,
         [
             jax.ShapeDtypeStruct((rows, half), BF16),
             jax.ShapeDtypeStruct((peers, chunk_rows, chunk_cols), BF16),
         ],
-        [pltpu.VMEM((2 * half, 2 * half), F32)],
+        [pltpu.HBM, pltpu.VMEM],
+        [
+            pltpu.VMEM(sums_mine.shape, BF16), pltpu.VMEM(sums_mine.shape, BF16),
+            pltpu.VMEM((rows, half), BF16), pltpu.VMEM((2 * half, 2 * half), F32),
+            pltpu.SemaphoreType.DMA((parts,)), pltpu.SemaphoreType.DMA((parts,)), pltpu.SemaphoreType.DMA((parts,)),
+        ],
         flops=28 * rows * half * half, name="backward",
     )
 
@@ -319,22 +419,18 @@
     )
 
 
-def stages(peers):
-    found, stride = [], 1
-    while stride < peers:
-        radix = min(4, peers // stride)
-        found.append((stride, radix))
-        stride *= radix
-    return found
+def digit(peers):
+    return min(4, peers)
 
 
 def hop(value, peers, offset):
     return lax.ppermute(value, "dom", [(i, i ^ offset) for i in range(peers)])
 
 
-def scatter_stage(held, peers, stride, radix):
-    parts = held.reshape((-1, radix) + held.shape[1:])
-    return parts[:, 0], [hop(parts[:, t], peers, t * stride) for t in range(1, radix)]
+def scatter_digit(chunks, peers):
+    radix = digit(peers)
+    parts = chunks.reshape((-1, radix) + chunks.shape[1:])
+    return parts[:, 0], [hop(parts[:, t], peers, t) for t in range(1, radix)]
 
 
 def add_pieces(kept, arrived):
@@ -344,8 +440,8 @@
     return total.astype(BF16)
 
 
-def gather_stage(held, peers, stride, radix):
-    arrived = [held] + [hop(held, peers, t * stride) for t in range(1, radix)]
+def gather_digit(held, peers):
+    arrived = [held] + [hop(held, peers, t) for t in range(1, digit(peers))]
     return jnp.stack(arrived, axis=1).reshape((-1,) + held.shape[1:])
 
 
@@ -383,7 +479,7 @@
     targets_remote, served_ids, flags = remote_dst[0], serve_block[0], push_flag[0]
     sources_local, targets_local = local_src[0], local_dst[0]
     side = lax.axis_index("hid")
-    place = jnp.stack([lax.axis_index("dom"), side]).astype(jnp.int32)
+    place = jnp.stack([lax.axis_index("dom") % digit(peers), side]).astype(jnp.int32)
 
     def blocks(values):
         return values.reshape(count, tile, half)
@@ -415,18 +511,17 @@
     grad_hidden, chunks = backward(
         place, sums, sums_other, history, z_first, z_other, w_in, w_out, peers
     )
-    plan = stages(peers)
-    kept, arrived = scatter_stage(chunks, peers, *plan[0])
+    kept, arrived = scatter_digit(chunks, peers)
     kept, hidden_out = tie((kept, hidden_out))
     base_out = local_forward(sources_local, targets_local, tiles_local, hidden_out)
     kept, base_out = tie((kept, base_out))
     held = add_pieces(kept, arrived)
-    for stage in plan[1:]:
-        held = add_pieces(*scatter_stage(held, peers, *stage))
-    for stage in reversed(plan[1:]):
-        held = gather_stage(held, peers, *stage)
+    offset = digit(peers)
+    while offset < peers:
+        held = add_pieces(held, [hop(held, peers, offset)])
+        offset *= 2
     held, supplied = tie((held, supplied))
-    held = gather_stage(held, peers, *plan[0])
+    held = gather_digit(held, peers)
     out = remote_forward(targets_remote, tiles_remote, supplied, base_out)
     held, out = tie((held, out))
     scale = float(rows * peers) ** (-0.5)

time: 128 us -> 124 us (0.969)
  starting transfers between devices: 37.1 us -> 33.4 us
  Pallas kernels: 26.1 us -> 24.7 us
    pallas_call x9 -> x3, Pallas kernels: 26.1 us -> 6.02 us  [call(): pl.pallas_call(body, grid_spec=pltpu.PrefetchScalarGridSpec(num_scalar_pr...]
    pallas_call x0 -> x6, Pallas kernels: none -> 18.7 us  [direct(): pl.pallas_call(body, in_specs=[pl.BlockSpec(memory_space=pltpu.SMEM)] * l...]
    ppermute x12 -> x8, starting transfers between devices: 17.3 us -> 13.4 us  [hop(): return lax.ppermute(value, 'dom', [(i, i ^ offset) for i in range(peers)])]
    ppermute x12 -> x8, waiting for transfers between devices: 19.3 us -> 19.9 us  [hop(): return lax.ppermute(value, 'dom', [(i, i ^ offset) for i in range(peers)])]
  transfers between devices with their start and end apart: 19 -> 15, of which waited for: 11 -> 9; matrix products, arithmetic and copies ran while one was open for 9% -> 9% of each run, Pallas kernels for 15% -> 14%
where the time goes in v3:
time: 124 us; the launch traced here: 123 us
  waiting for transfers between devices  44.5 us (36%)
  starting transfers between devices  33.4 us (27%)
  Pallas kernels  24.7 us (20%)
  local copies, waits for them, and re-layouts  15.9 us (13%)
  matrix products  2.6 us (2%)
  other arithmetic  1.32 us (1%)
    all_to_all x2, waiting for transfers between devices, exchange(): lax.all_to_all(sending, 'dom', split_axis=0, concat_axis=0, tiled=True)  24.5 us
    ppermute x8, waiting for transfers between devices, hop(): return lax.ppermute(value, 'dom', [(i, i ^ offset) for i in range(peers)])  19.9 us
    all_to_all x2, starting transfers between devices, exchange(): lax.all_to_all(sending, 'dom', split_axis=0, concat_axis=0, tiled=True)  18.7 us
    pallas_call x6, Pallas kernels, direct(): pl.pallas_call(body, in_specs=[pl.BlockSpec(memory_space=pltpu.SMEM)] * l...  18.7 us
    ppermute x8, starting transfers between devices, hop(): return lax.ppermute(value, 'dom', [(i, i ^ offset) for i in range(peers)])  13.4 us
    unnamed x56, local copies, waits for them, and re-layouts  10 us
    pallas_call x3, Pallas kernels, call(): pl.pallas_call(body, grid_spec=pltpu.PrefetchScalarGridSpec(num_scalar_pr...  6.02 us
    concatenate x2, local copies, waits for them, and re-layouts, own_first(): joined = jnp.concatenate([weight, swap(weight)], axis=0)  2.7 us
  transfers between devices with their start and end apart: 15, of which 9 were waited for; matrix products, arithmetic and copies ran while one was open for 9% of the time, Pallas kernels for 14%

profile of v3, /device:TPU:0, one launch (start us, length us, event | category | flops | bytes accessed | tf_op | source)
XLA Modules:
  0.0 123.3 jit_solution(889394999243533663)
XLA Ops:
  0.6 3.7 %prepare.1 = bf16[16,256,256]{2,1,0:T(8,128)(2,1)} custom-call(s32[16]{0:T(128)} %bitcast.69, s32[16]{0:T(128)} %bitcast.62, bf16[16,128,128]{2,1,0:T(8,128)(2,1)} %bitcast.47, bf16[8,128,256]{2,1,0:T(8,128)(2,1)} %bitcast.53, bf16[8,128,256]{2,1,0:T(8,128)(2,1)} %bitcast.55), custom_call_target="tpu_custom_call" | custom-call | flops 134217728 | bytes 3670016 | tf_op jit(solution)/shard_map/prepare/pallas_call | solution.py:60
  4.3 0.0 copy-start.26
  4.3 0.0 copy-start.1
  4.3 0.0 copy-start.17
  4.3 0.0 copy-start.18
  4.3 8.5 %all-to-all-start = ((bf16[16,256,256]{2,1,0:T(8,128)(2,1)}), bf16[16,256,256]{2,1,0:T(8,128)(2,1)S(1)}, u32[]{:S(2)}, u32[]{:S(2)}) async-start(bf16[16,256,256]{2,1,0:T(8,128)(2,1)} %prepare.1), calls=%async_computation | async-start | bytes 4194304 | tf_op jit(solution)/shard_map/all_to_all | solution.py:453
  12.8 0.1 collective-permute-start
  12.9 0.5 collective-permute-start.1
  13.4 0.1 collective-permute-start.2
  13.5 0.7 constant_dynamic-update-slice_fusion.1
  14.2 1.0 copy-done.3
  15.3 1.0 copy-done.4
  16.3 2.6 %local_both.1 = (f32[8,128,256]{2,1,0:T(8,128)S(1)}, f32[8,128,256]{2,1,0:T(8,128)S(1)}) custom-call(s32[32]{0:T(128)S(1)} %bitcast.65, s32[32]{0:T(128)S(1)} %bitcast.67, bf16[32,128,128]{2,1,0:T(8,128)(2,1)S(1)} %bitcast.50, bf16[8,128,256]{2,1,0:T(8,128)(2,1)S(1)} %bitcast.54, bf16[8,128,256]{2,1,0:T(8,128)(2,1)S(1)} %bitcast.56), custom_call_target="tpu_custom_call" | custom-call | flops 536870912 | bytes 4194304 | tf_op jit(solution)/shard_map/local_both/pallas_call | solution.py:39
  18.9 1.0 copy-done.5
  19.9 1.0 copy-done.20
  20.9 1.0 constant_dynamic-update-slice_fusion.3
  21.8 1.7 %constant_dynamic-update-slice_fusion = bf16[512,512]{1,0:T(8,128)(2,1)} fusion(bf16[512,512]{1,0:T(8,128)(2,1)} %constant_dynamic-update-slice_fusion.1, bf16[256,512]{1,0:T(8,128)(2,1)} %collective-permute-done), kind=kLoop, calls=%fused_computation.16 | loop fusion | bytes 524288 | tf_op jit(solution)/shard_map/concatenate | solution.py:488
  23.5 1.0 constant_dynamic-update-slice_fusion.2
  24.6 1.1 fusion.6
  25.7 0.0 copy-start.7
  25.7 0.1 maximum_select_fusion.1.wo_ref
  25.8 0.9 maximum_select_fusion.wi_ref
  26.7 1.4 %fusion.2 = f32[256,1024]{1,0:T(8,128)S(1)} fusion(bf16[1024,256]{1,0:T(8,128)(2,1)} %collective-permute-done.2, bf16[512,512]{1,0:T(8,128)(2,1)S(1)} %maximum_select_fusion.1.wo_ref), kind=kOutput, calls=%fused_computation.13 | convolution fusion | flops 134217728 | bytes 1703936 | tf_op jit(solution)/shard_map/dot_general | solution.py:18
  28.2 1.1 fusion.1
  29.3 2.0 %copy.16 = bf16[1024,256]{1,0:T(8,128)(2,1)} copy(bf16[1024,256]{0,1:T(8,128)(2,1)} %fusion.1) | data formatting | bytes 1048576 | tf_op jit(solution)/shard_map/convert_element_type | solution.py:498
  31.4 24.5 %all-to-all-done.recv_hbm.ret_hbm = bf16[16,256,256]{2,1,0:T(8,128)(2,1)S(1)} async-done(((bf16[16,256,256]{2,1,0:T(8,128)(2,1)}), bf16[16,256,256]{2,1,0:T(8,128)(2,1)S(1)}, u32[]{:S(2)}, u32[]{:S(2)}) %all-to-all-start) | async-done | bytes 2097184 | tf_op jit(solution)/shard_map/all_to_all | solution.py:453
  55.9 1.2 copy-done.6
  57.1 1.7 %remote_forward.2 = bf16[8,128,256]{2,1,0:T(8,128)(2,1)S(1)} custom-call(s32[16]{0:T(128)S(1)} %bitcast.63, bf16[16,128,128]{2,1,0:T(8,128)(2,1)S(1)} %bitcast.48, bf16[16,256,256]{2,1,0:T(8,128)(2,1)S(1)} %all-to-all-done.recv_hbm.ret_hbm, f32[8,128,256]{2,1,0:T(8,128)S(1)} %copy-done.6), custom_call_target="tpu_custom_call" | custom-call | flops 134217728 | bytes 4194304 | tf_op jit(solution)/shard_map/remote_forward/pallas_call | solution.py:60
  58.8 0.0 copy-start.11
  58.8 0.1 collective-permute-start.3
  58.9 0.0 copy-start.13
  58.9 0.0 copy-start.15
  59.0 2.1 %gather_grads.1 = bf16[2,8,128,256]{3,2,1,0:T(8,128)(2,1)} custom-call(s32[16]{0:T(128)S(1)} %bitcast.70, s32[16]{0:T(128)S(1)} %bitcast.72, bf16[16,256,256]{2,1,0:T(8,128)(2,1)S(1)} %all-to-all-done.recv_hbm.ret_hbm, f32[8,128,256]{2,1,0:T(8,128)S(1)} %copy-done.21), custom_call_target="tpu_custom_call" | custom-call | flops 2147483648 | bytes 4194304 | tf_op jit(solution)/shard_map/gather_grads/pallas_call | solution.py:60
  61.0 0.5 collective-permute-start.4
  61.6 0.0 copy-start.22
  61.6 2.7 %middle.1 = (bf16[8,128,256]{2,1,0:T(8,128)(2,1)S(1)}, bf16[16,128,256]{2,1,0:T(8,128)(2,1)}) custom-call(s32[16]{0:T(128)S(1)} %bitcast.71, s32[16]{0:T(128)S(1)} %bitcast.73, bf16[1024,256]{1,0:T(8,128)(2,1)S(1)} %bitcast.58, bf16[1024,256]{1,0:T(8,128)(2,1)S(1)} %collective-permute-done.3.zo_ref, bf16[512,512]{1,0:T(8,128)(2,1)S(1)} %copy-done.13, ...), custom_call_target="tpu_custom_call" | custom-call | flops 8053063680 | bytes 4194304 | tf_op jit(solution)/shard_map/middle/pallas_call | solution.py:60
  64.3 0.0 copy-start.9
  64.3 0.8 copy-done.9
  65.1 10.3 %all-to-all-start.1 = ((bf16[16,128,256]{2,1,0:T(8,128)(2,1)}), bf16[16,128,256]{2,1,0:T(8,128)(2,1)}, u32[]{:S(2)}, u32[]{:S(2)}) async-start(bf16[16,128,256]{2,1,0:T(8,128)(2,1)} %get-tuple-element.51), calls=%async_computation.1 | async-start | bytes 2097152 | tf_op jit(solution)/shard_map/all_to_all | solution.py:453
  75.4 0.1 pad_add_fusion.place_ref
  75.5 1.1 copy-done.14
  76.6 1.0 copy-done.23
  77.7 5.3 %backward.1 = (bf16[1024,256]{1,0:T(8,128)(2,1)}, bf16[16,32,512]{2,1,0:T(8,128)(2,1)S(1)}) custom-call(s32[2]{0:T(128)S(1)} %pad_add_fusion.place_ref, bf16[2,1024,256]{2,1,0:T(8,128)(2,1)} %bitcast.14.sm_hbm, bf16[2,1024,256]{2,1,0:T(8,128)(2,1)} %collective-permute-done.4.so_hbm, bf16[1024,256]{1,0:T(8,128)(2,1)S(1)} %copy-done.8, ...), custom_call_target="tpu_custom_call" | custom-call | flops 1879048192 | bytes 5767168 | tf_op jit(solution)/shard_map/backward/pallas_call | solution.py:60
  83.0 1.9 %collective-permute-start.6 = (bf16[4,32,512]{2,1,0:T(8,128)(2,1)S(1)}, bf16[4,32,512]{2,1,0:T(8,128)(2,1)S(1)}, u32[]{:S(2)}, u32[]{:S(2)}) collective-permute-start(bf16[4,32,512]{2,1,0:T(8,128)(2,1)S(1)} %get-tuple-element.61), channel_id=1, source_target_pairs={{0,4},{2,6},{4,0},{6,2},{8,12},{10,14},{12,8},{14,10},{16,20},{18,... | collective-permute-start | bytes 393224 | tf_op jit(solution)/shard_map/ppermute | solution.py:427
  85.0 1.5 %collective-permute-start.5 = (bf16[4,32,512]{2,1,0:T(8,128)(2,1)S(1)}, bf16[4,32,512]{2,1,0:T(8,128)(2,1)S(1)}, u32[]{:S(2)}, u32[]{:S(2)}) collective-permute-start(bf16[4,32,512]{2,1,0:T(8,128)(2,1)S(1)} %get-tuple-element.62), channel_id=1, source_target_pairs={{0,2},{2,0},{4,6},{6,4},{8,10},{10,8},{12,14},{14,12},{16,18},{18,... | collective-permute-start | bytes 393224 | tf_op jit(solution)/shard_map/ppermute | solution.py:427
  86.4 0.2 collective-permute-start.7
  86.6 1.9 %local_forward.1.base_ref = f32[8,128,256]{2,1,0:T(8,128)S(1)} custom-call(s32[32]{0:T(128)S(1)} %bitcast.66, s32[32]{0:T(128)S(1)} %bitcast.68, bf16[32,128,128]{2,1,0:T(8,128)(2,1)S(1)} %bitcast.51, bf16[8,128,256]{2,1,0:T(8,128)(2,1)S(1)} %copy-done.10), custom_call_target="tpu_custom_call" | custom-call | flops 268435456 | bytes 2621440 | tf_op jit(solution)/shard_map/local_forward/pallas_call | solution.py:39
  88.5 1.6 %collective-permute-done.6 = bf16[4,32,512]{2,1,0:T(8,128)(2,1)S(1)} collective-permute-done((bf16[4,32,512]{2,1,0:T(8,128)(2,1)S(1)}, bf16[4,32,512]{2,1,0:T(8,128)(2,1)S(1)}, u32[]{:S(2)}, u32[]{:S(2)}) %collective-permute-start.6) | collective-permute-done | bytes 131104 | tf_op jit(solution)/shard_map/ppermute | solution.py:427
  90.1 5.1 %collective-permute-done.5 = bf16[4,32,512]{2,1,0:T(8,128)(2,1)S(1)} collective-permute-done((bf16[4,32,512]{2,1,0:T(8,128)(2,1)S(1)}, bf16[4,32,512]{2,1,0:T(8,128)(2,1)S(1)}, u32[]{:S(2)}, u32[]{:S(2)}) %collective-permute-start.5) | collective-permute-done | bytes 131104 | tf_op jit(solution)/shard_map/ppermute | solution.py:427
  95.2 3.9 %collective-permute-done.7 = bf16[4,32,512]{2,1,0:T(8,128)(2,1)S(1)} collective-permute-done((bf16[4,32,512]{2,1,0:T(8,128)(2,1)S(1)}, bf16[4,32,512]{2,1,0:T(8,128)(2,1)S(1)}, u32[]{:S(2)}, u32[]{:S(2)}) %collective-permute-start.7) | collective-permute-done | bytes 131104 | tf_op jit(solution)/shard_map/ppermute | solution.py:427
  99.0 0.1 add_convert_fusion.2
  99.1 0.1 collective-permute-start.8
  99.2 5.0 %collective-permute-done.8 = bf16[4,32,512]{2,1,0:T(8,128)(2,1)S(1)} collective-permute-done((bf16[4,32,512]{2,1,0:T(8,128)(2,1)S(1)}, bf16[4,32,512]{2,1,0:T(8,128)(2,1)S(1)}, u32[]{:S(2)}, u32[]{:S(2)}) %collective-permute-start.8) | collective-permute-done | bytes 131104 | tf_op jit(solution)/shard_map/ppermute | solution.py:427
  104.2 6.2 %collective-permute-start.9 = (bf16[4,32,512]{2,1,0:T(8,128)(2,1)S(1)}, bf16[4,32,512]{2,1,0:T(8,128)(2,1)S(1)}, u32[]{:S(2)}, u32[]{:S(2)}) collective-permute-start(bf16[4,32,512]{2,1,0:T(8,128)(2,1)S(1)} %add_convert_fusion.1), channel_id=1, source_target_pairs={{0,16},{2,18},{4,20},{6,22},{8,24},{10,26},{12,28},{14,30},{16,0},... | collective-permute-start | bytes 393224 | tf_op jit(solution)/shard_map/ppermute | solution.py:427
  110.4 3.3 %collective-permute-done.9 = bf16[4,32,512]{2,1,0:T(8,128)(2,1)S(1)} collective-permute-done((bf16[4,32,512]{2,1,0:T(8,128)(2,1)S(1)}, bf16[4,32,512]{2,1,0:T(8,128)(2,1)S(1)}, u32[]{:S(2)}, u32[]{:S(2)}) %collective-permute-start.9) | collective-permute-done | bytes 131104 | tf_op jit(solution)/shard_map/ppermute | solution.py:427
  113.8 1.9 %collective-permute-start.12 = (bf16[4,32,512]{2,1,0:T(8,128)(2,1)S(1)}, bf16[4,32,512]{2,1,0:T(8,128)(2,1)S(1)}, u32[]{:S(2)}, u32[]{:S(2)}) collective-permute-start(bf16[4,32,512]{2,1,0:T(8,128)(2,1)S(1)} %add_convert_fusion), channel_id=1, source_target_pairs={{0,6},{2,4},{4,2},{6,0},{8,14},{10,12},{12,10},{14,8},{16,22},{18,... | collective-permute-start | bytes 393224 | tf_op jit(solution)/shard_map/ppermute | solution.py:427
  115.6 1.1 collective-permute-start.11
  116.7 0.6 collective-permute-start.10
  117.3 3.3 %remote_forward.3 = bf16[8,128,256]{2,1,0:T(8,128)(2,1)} custom-call(s32[16]{0:T(128)S(1)} %bitcast.64, bf16[16,128,128]{2,1,0:T(8,128)(2,1)S(1)} %bitcast.49, bf16[16,128,256]{2,1,0:T(8,128)(2,1)} %all-to-all-done.1.recv_hbm, f32[8,128,256]{2,1,0:T(8,128)S(1)} %local_forward.1.base_ref), custom_call_target="tpu_custom_call" | custom-call | flops 134217728 | bytes 3145728 | tf_op jit(solution)/shard_map/remote_forward/pallas_call | solution.py:60
  120.6 0.2 collective-permute-done.12
  120.8 0.8 collective-permute-done.11
  121.6 0.1 collective-permute-done.10
  121.7 0.1 pad_maximum_fusion
  121.8 1.5 %finish_weights.1 = (f32[256,512]{1,0:T(8,128)}, f32[256,512]{1,0:T(8,128)}) custom-call(s32[2]{0:T(128)S(1)} %pad_add_fusion.place_ref, bf16[16,32,512]{2,1,0:T(8,128)(2,1)S(1)} %bitcast.52), custom_call_target="tpu_custom_call" | custom-call | bytes 1572864 | tf_op jit(solution)/shard_map/finish_weights/pallas_call | solution.py:39
  (46 shorter events, 0.2 us)
Async XLA Ops:
  4.3 8.5 %copy-start.26 = (bf16[256,512]{1,0:T(8,128)(2,1)S(1)}, bf16[256,512]{1,0:T(8,128)(2,1)}, u32[]{:S(2)}) copy-start(bf16[256,512]{1,0:T(8,128)(2,1)} %param.21) | copy-start | bytes 786436
  4.3 9.9 %copy-start.1 = (bf16[1,32,128,128]{3,2,1,0:T(8,128)(2,1)S(1)}, bf16[1,32,128,128]{3,2,1,0:T(8,128)(2,1)}, u32[]{:S(2)}) copy-start(bf16[1,32,128,128]{3,2,1,0:T(8,128)(2,1)} %param.18) | copy-start | bytes 3145732
  4.3 9.9 %copy-start.17 = (s32[1,32]{1,0:T(1,128)S(1)}, s32[1,32]{1,0:T(1,128)}, u32[]{:S(2)}) copy-start(s32[1,32]{1,0:T(1,128)} %param.19) | copy-start | bytes 388
  4.3 9.9 %copy-start.18 = (s32[1,32]{1,0:T(1,128)S(1)}, s32[1,32]{1,0:T(1,128)}, u32[]{:S(2)}) copy-start(s32[1,32]{1,0:T(1,128)} %param.20) | copy-start | bytes 388
  4.3 51.5 %all-to-all-start = ((bf16[16,256,256]{2,1,0:T(8,128)(2,1)}), bf16[16,256,256]{2,1,0:T(8,128)(2,1)S(1)}, u32[]{:S(2)}, u32[]{:S(2)}) async-start(bf16[16,256,256]{2,1,0:T(8,128)(2,1)} %prepare.1), calls=%async_computation | async-start | bytes 4194304 | tf_op jit(solution)/shard_map/all_to_all | solution.py:453
  12.8 9.0 %collective-permute-start = (bf16[256,512]{1,0:T(8,128)(2,1)S(1)}, bf16[256,512]{1,0:T(8,128)(2,1)}, u32[]{:S(2)}, u32[]{:S(2)}) collective-permute-start(bf16[256,512]{1,0:T(8,128)(2,1)S(1)} %copy-done.26), channel_id=1, source_target_pairs={{0,1},{1,0},{2,3},{3,2},{4,5},{5,4},{6,7},{7,6},{8,9},{9,8},{10,11... | collective-permute-start | bytes 786440 | tf_op jit(solution)/shard_map/ppermute | solution.py:457
  12.9 10.6 %collective-permute-start.1 = (bf16[256,512]{1,0:T(8,128)(2,1)}, bf16[256,512]{1,0:T(8,128)(2,1)}, u32[]{:S(2)}, u32[]{:S(2)}) collective-permute-start(bf16[256,512]{1,0:T(8,128)(2,1)} %param.22), channel_id=1, source_target_pairs={{0,1},{1,0},{2,3},{3,2},{4,5},{5,4},{6,7},{7,6},{8,9},{9,8},{10,11... | collective-permute-start | bytes 786440 | tf_op jit(solution)/shard_map/ppermute | solution.py:457
  13.4 13.3 %collective-permute-start.2 = (bf16[1024,256]{1,0:T(8,128)(2,1)}, bf16[1024,256]{1,0:T(8,128)(2,1)}, u32[]{:S(2)}, u32[]{:S(2)}) collective-permute-start(bf16[1024,256]{1,0:T(8,128)(2,1)} %hist_ref.1), channel_id=1, source_target_pairs={{0,1},{1,0},{2,3},{3,2},{4,5},{5,4},{6,7},{7,6},{8,9},{9,8},{10,11... | collective-permute-start | bytes 1572872 | tf_op jit(solution)/shard_map/ppermute | solution.py:457
  14.2 1.0 copy-start.3
  15.2 1.0 copy-start.4
  18.9 1.0 copy-start.5
  19.9 1.0 copy-start.20
  23.5 2.3 %copy-start.25 = (bf16[512,512]{1,0:T(8,128)(2,1)S(1)}, bf16[512,512]{1,0:T(8,128)(2,1)}, u32[]{:S(2)}) copy-start(bf16[512,512]{1,0:T(8,128)(2,1)} %constant_dynamic-update-slice_fusion) | copy-start | bytes 1572868
  25.7 2.5 %copy-start.7 = (bf16[1024,256]{1,0:T(8,128)(2,1)S(1)}, bf16[1024,256]{1,0:T(8,128)(2,1)}, u32[]{:S(2)}) copy-start(bf16[1024,256]{1,0:T(8,128)(2,1)} %hist_ref.1) | copy-start | bytes 1572868
  26.7 29.2 %copy-start = (bf16[1,16,128,128]{3,2,1,0:T(8,128)(2,1)S(1)}, bf16[1,16,128,128]{3,2,1,0:T(8,128)(2,1)}, u32[]{:S(2)}) copy-start(bf16[1,16,128,128]{3,2,1,0:T(8,128)(2,1)} %param.14) | copy-start | bytes 1572868
  26.7 29.2 %copy-start.16 = (s32[1,16]{1,0:T(1,128)S(1)}, s32[1,16]{1,0:T(1,128)}, u32[]{:S(2)}) copy-start(s32[1,16]{1,0:T(1,128)} %param.15) | copy-start | bytes 196
  55.9 1.2 copy-start.6
  57.1 1.8 %copy-start.19 = (s32[1,16]{1,0:T(1,128)S(1)}, s32[1,16]{1,0:T(1,128)}, u32[]{:S(2)}) copy-start(s32[1,16]{1,0:T(1,128)} %param.16) | copy-start | bytes 196
  57.1 1.8 %copy-start.21 = (f32[8,128,256]{2,1,0:T(8,128)S(1)}, f32[8,128,256]{2,1,0:T(8,128)}, u32[]{:S(2)}) copy-start(f32[8,128,256]{2,1,0:T(8,128)} %copy-done.20) | copy-start | bytes 3145732
  57.1 1.8 %copy-start.24 = (s32[1,16]{1,0:T(1,128)S(1)}, s32[1,16]{1,0:T(1,128)}, u32[]{:S(2)}) copy-start(s32[1,16]{1,0:T(1,128)} %param.17) | copy-start | bytes 196
  58.8 2.8 %copy-start.11 = (bf16[8,128,256]{2,1,0:T(8,128)(2,1)}, bf16[8,128,256]{2,1,0:T(8,128)(2,1)S(1)}, u32[]{:S(2)}) copy-start(bf16[8,128,256]{2,1,0:T(8,128)(2,1)S(1)} %remote_forward.2) | copy-start | bytes 1572868
  58.8 2.8 %collective-permute-start.3 = (bf16[1024,256]{1,0:T(8,128)(2,1)S(1)}, bf16[1024,256]{1,0:T(8,128)(2,1)S(1)}, u32[]{:S(2)}, u32[]{:S(2)}) collective-permute-start(bf16[1024,256]{1,0:T(8,128)(2,1)S(1)} %bitcast.57), channel_id=1, source_target_pairs={{0,1},{1,0},{2,3},{3,2},{4,5},{5,4},{6,7},{7,6},{8,9},{9,8},{10,11... | collective-permute-start | bytes 1572872 | tf_op jit(solution)/shard_map/ppermute | solution.py:457
  58.9 2.6 %copy-start.13 = (bf16[512,512]{1,0:T(8,128)(2,1)S(1)}, bf16[512,512]{1,0:T(8,128)(2,1)}, u32[]{:S(2)}) copy-start(bf16[512,512]{1,0:T(8,128)(2,1)} %maximum_select_fusion.wi_ref) | copy-start | bytes 1572868
  58.9 2.6 %copy-start.15 = (bf16[1024,256]{1,0:T(8,128)(2,1)S(1)}, bf16[1024,256]{1,0:T(8,128)(2,1)}, u32[]{:S(2)}) copy-start(bf16[1024,256]{1,0:T(8,128)(2,1)} %copy.16) | copy-start | bytes 1572868
  61.0 14.4 %collective-permute-start.4 = (bf16[2,1024,256]{2,1,0:T(8,128)(2,1)}, bf16[2,1024,256]{2,1,0:T(8,128)(2,1)}, u32[]{:S(2)}, u32[]{:S(2)}) collective-permute-start(bf16[2,1024,256]{2,1,0:T(8,128)(2,1)} %bitcast.14.sm_hbm), channel_id=1, source_target_pairs={{0,1},{1,0},{2,3},{3,2},{4,5},{5,4},{6,7},{7,6},{8,9},{9,8},{10,11... | collective-permute-start | bytes 3145736 | tf_op jit(solution)/shard_map/ppermute | solution.py:457
  61.6 2.7 %copy-start.22 = (bf16[1024,256]{1,0:T(8,128)(2,1)}, bf16[1024,256]{1,0:T(8,128)(2,1)S(1)}, u32[]{:S(2)}) copy-start(bf16[1024,256]{1,0:T(8,128)(2,1)S(1)} %collective-permute-done.3.zo_ref) | copy-start | bytes 1572868
  64.3 0.8 copy-start.9
  65.1 10.4 %copy-start.8 = (bf16[1024,256]{1,0:T(8,128)(2,1)S(1)}, bf16[1024,256]{1,0:T(8,128)(2,1)}, u32[]{:S(2)}) copy-start(bf16[1024,256]{1,0:T(8,128)(2,1)} %hist_ref.1) | copy-start | bytes 1572868
  65.1 10.4 %copy-start.12 = (bf16[8,128,256]{2,1,0:T(8,128)(2,1)S(1)}, bf16[8,128,256]{2,1,0:T(8,128)(2,1)}, u32[]{:S(2)}) copy-start(bf16[8,128,256]{2,1,0:T(8,128)(2,1)} %copy-done.11) | copy-start | bytes 1572868
  65.1 48.7 %all-to-all-start.1 = ((bf16[16,128,256]{2,1,0:T(8,128)(2,1)}), bf16[16,128,256]{2,1,0:T(8,128)(2,1)}, u32[]{:S(2)}, u32[]{:S(2)}) async-start(bf16[16,128,256]{2,1,0:T(8,128)(2,1)} %get-tuple-element.51), calls=%async_computation.1 | async-start | bytes 2097152 | tf_op jit(solution)/shard_map/all_to_all | solution.py:453
  75.5 11.1 %copy-start.2 = (bf16[1,32,128,128]{3,2,1,0:T(8,128)(2,1)S(1)}, bf16[1,32,128,128]{3,2,1,0:T(8,128)(2,1)}, u32[]{:S(2)}) copy-start(bf16[1,32,128,128]{3,2,1,0:T(8,128)(2,1)} %param.18) | copy-start | bytes 3145732
  75.5 11.1 %copy-start.10 = (bf16[8,128,256]{2,1,0:T(8,128)(2,1)S(1)}, bf16[8,128,256]{2,1,0:T(8,128)(2,1)}, u32[]{:S(2)}) copy-start(bf16[8,128,256]{2,1,0:T(8,128)(2,1)} %copy-done.9) | copy-start | bytes 1572868
  75.5 1.2 copy-start.14
  76.6 1.0 copy-start.23
  83.0 7.0 %collective-permute-start.6 = (bf16[4,32,512]{2,1,0:T(8,128)(2,1)S(1)}, bf16[4,32,512]{2,1,0:T(8,128)(2,1)S(1)}, u32[]{:S(2)}, u32[]{:S(2)}) collective-permute-start(bf16[4,32,512]{2,1,0:T(8,128)(2,1)S(1)} %get-tuple-element.61), channel_id=1, source_target_pairs={{0,4},{2,6},{4,0},{6,2},{8,12},{10,14},{12,8},{14,10},{16,20},{18,... | collective-permute-start | bytes 393224 | tf_op jit(solution)/shard_map/ppermute | solution.py:427
  85.0 10.2 %collective-permute-start.5 = (bf16[4,32,512]{2,1,0:T(8,128)(2,1)S(1)}, bf16[4,32,512]{2,1,0:T(8,128)(2,1)S(1)}, u32[]{:S(2)}, u32[]{:S(2)}) collective-permute-start(bf16[4,32,512]{2,1,0:T(8,128)(2,1)S(1)} %get-tuple-element.62), channel_id=1, source_target_pairs={{0,2},{2,0},{4,6},{6,4},{8,10},{10,8},{12,14},{14,12},{16,18},{18,... | collective-permute-start | bytes 393224 | tf_op jit(solution)/shard_map/ppermute | solution.py:427
  86.4 12.6 %collective-permute-start.7 = (bf16[4,32,512]{2,1,0:T(8,128)(2,1)S(1)}, bf16[4,32,512]{2,1,0:T(8,128)(2,1)S(1)}, u32[]{:S(2)}, u32[]{:S(2)}) collective-permute-start(bf16[4,32,512]{2,1,0:T(8,128)(2,1)S(1)} %get-tuple-element.63), channel_id=1, source_target_pairs={{0,6},{2,4},{4,2},{6,0},{8,14},{10,12},{12,10},{14,8},{16,22},{18,... | collective-permute-start | bytes 393224 | tf_op jit(solution)/shard_map/ppermute | solution.py:427
  99.1 5.0 %collective-permute-start.8 = (bf16[4,32,512]{2,1,0:T(8,128)(2,1)S(1)}, bf16[4,32,512]{2,1,0:T(8,128)(2,1)S(1)}, u32[]{:S(2)}, u32[]{:S(2)}) collective-permute-start(bf16[4,32,512]{2,1,0:T(8,128)(2,1)S(1)} %add_convert_fusion.2), channel_id=1, source_target_pairs={{0,8},{2,10},{4,12},{6,14},{8,0},{10,2},{12,4},{14,6},{16,24},{18,... | collective-permute-start | bytes 393224 | tf_op jit(solution)/shard_map/ppermute | solution.py:427
  104.2 9.5 %collective-permute-start.9 = (bf16[4,32,512]{2,1,0:T(8,128)(2,1)S(1)}, bf16[4,32,512]{2,1,0:T(8,128)(2,1)S(1)}, u32[]{:S(2)}, u32[]{:S(2)}) collective-permute-start(bf16[4,32,512]{2,1,0:T(8,128)(2,1)S(1)} %add_convert_fusion.1), channel_id=1, source_target_pairs={{0,16},{2,18},{4,20},{6,22},{8,24},{10,26},{12,28},{14,30},{16,0},... | collective-permute-start | bytes 393224 | tf_op jit(solution)/shard_map/ppermute | solution.py:427
  113.8 7.0 %collective-permute-start.12 = (bf16[4,32,512]{2,1,0:T(8,128)(2,1)S(1)}, bf16[4,32,512]{2,1,0:T(8,128)(2,1)S(1)}, u32[]{:S(2)}, u32[]{:S(2)}) collective-permute-start(bf16[4,32,512]{2,1,0:T(8,128)(2,1)S(1)} %add_convert_fusion), channel_id=1, source_target_pairs={{0,6},{2,4},{4,2},{6,0},{8,14},{10,12},{12,10},{14,8},{16,22},{18,... | collective-permute-start | bytes 393224 | tf_op jit(solution)/shard_map/ppermute | solution.py:427
  115.6 6.0 %collective-permute-start.11 = (bf16[4,32,512]{2,1,0:T(8,128)(2,1)S(1)}, bf16[4,32,512]{2,1,0:T(8,128)(2,1)S(1)}, u32[]{:S(2)}, u32[]{:S(2)}) collective-permute-start(bf16[4,32,512]{2,1,0:T(8,128)(2,1)S(1)} %add_convert_fusion), channel_id=1, source_target_pairs={{0,4},{2,6},{4,0},{6,2},{8,12},{10,14},{12,8},{14,10},{16,20},{18,... | collective-permute-start | bytes 393224 | tf_op jit(solution)/shard_map/ppermute | solution.py:427
  116.7 5.0 %collective-permute-start.10 = (bf16[4,32,512]{2,1,0:T(8,128)(2,1)S(1)}, bf16[4,32,512]{2,1,0:T(8,128)(2,1)S(1)}, u32[]{:S(2)}, u32[]{:S(2)}) collective-permute-start(bf16[4,32,512]{2,1,0:T(8,128)(2,1)S(1)} %add_convert_fusion), channel_id=1, source_target_pairs={{0,2},{2,0},{4,6},{6,4},{8,10},{10,8},{12,14},{14,12},{16,18},{18,... | collective-permute-start | bytes 393224 | tf_op jit(solution)/shard_map/ppermute | solution.py:427

commit v4 on v3

--- a/solution.py
+++ b/solution.py
@@ -205,32 +205,36 @@
     return copy
 
 
-def remote_forward(targets, tiles, received, base):
+def remote_forward(targets, tiles, received, base, stream):
     peers, tile, _ = tiles.shape
     width = received.shape[2]
     group = 4 if peers % 4 == 0 else 1
 
-    def body(dst_ref, tiles_ref, recv_hbm, base_ref, out_ref, recv_ref, acc_ref, sems):
-        copy = streamed(recv_hbm, 0, tile, recv_ref, sems, group)
-        each(peers // group, lambda g: copy(g).start())
+    def body(dst_ref, tiles_ref, recv_hbm, base_ref, out_ref, acc_ref, *rest):
+        if stream:
+            recv_ref, sems = rest
+            copy = streamed(recv_hbm, 0, tile, recv_ref, sems, group)
+            each(peers // group, lambda g: copy(g).start())
+        else:
+            recv_ref = recv_hbm
         acc_ref[...] = base_ref[...]
 
         def work(g):
-            copy(g).wait()
+            if stream:
+                copy(g).wait()
             for j in range(group):
                 p = g * group + j
-                acc_ref[dst_ref[p]] += dot(tiles_ref[p], recv_ref[p])
+                acc_ref[dst_ref[p]] += dot(tiles_ref[p], recv_ref[p, :tile])
 
         each(peers // group, work)
         out_ref[...] = acc_ref[...].astype(BF16)
 
+    scratch = [pltpu.VMEM(base.shape, F32)]
+    if stream:
+        scratch += [pltpu.VMEM((peers, tile, width), BF16), pltpu.SemaphoreType.DMA((peers // group,))]
     return direct(
-        body, (targets,), [tiles, received, base], [pltpu.VMEM, pltpu.HBM, pltpu.VMEM],
-        [jax.ShapeDtypeStruct(base.shape, BF16)], [pltpu.VMEM],
-        [
-            pltpu.VMEM((peers, tile, width), BF16), pltpu.VMEM(base.shape, F32),
-            pltpu.SemaphoreType.DMA((peers // group,)),
-        ],
+        body, (targets,), [tiles, received, base], [pltpu.VMEM, pltpu.HBM if stream else pltpu.VMEM, pltpu.VMEM],
+        [jax.ShapeDtypeStruct(base.shape, BF16)], [pltpu.VMEM], scratch,
         flops=2 * peers * tile * tile * width, name="remote_forward",
     )[0]
 
@@ -293,29 +297,22 @@
     group = 4 if peers % 4 == 0 else 1
     both = (2,) + base.shape
 
-    def body(ids_ref, flag_ref, ret_hbm, base_ref, out_ref, ret_ref, acc_ref, sems):
-        copy = streamed(ret_hbm, tile, tile, ret_ref, sems, group)
-        each(peers // group, lambda g: copy(g).start())
+    def body(ids_ref, flag_ref, ret_ref, base_ref, out_ref, acc_ref):
         acc_ref[0] = base_ref[...]
         acc_ref[1] = jnp.zeros_like(base_ref)
 
         def work(g):
-            copy(g).wait()
             for j in range(group):
                 p = g * group + j
                 side = jnp.where(flag_ref[p] == 1, 0, 1)
-                acc_ref[side, ids_ref[p]] += ret_ref[p].astype(F32)
+                acc_ref[side, ids_ref[p]] += ret_ref[p, tile:].astype(F32)
 
         each(peers // group, work)
         out_ref[...] = acc_ref[...].astype(BF16)
 
     return direct(
-        body, (ids, flags), [returned, base], [pltpu.HBM, pltpu.VMEM],
-        [jax.ShapeDtypeStruct(both, BF16)], [pltpu.VMEM],
-        [
-            pltpu.VMEM((peers, tile, width), BF16), pltpu.VMEM(both, F32),
-            pltpu.SemaphoreType.DMA((peers // group,)),
-        ],
+        body, (ids, flags), [returned, base], [pltpu.VMEM, pltpu.VMEM],
+        [jax.ShapeDtypeStruct(both, BF16)], [pltpu.VMEM], [pltpu.VMEM(both, F32)],
         flops=32 * peers * tile * tile * width, name="gather_grads",
     )[0]
 
@@ -500,7 +497,7 @@
     received, w_in, w_out, hist_out, base_forward, base_back = tie(
         (received, w_in, w_out, hist_out, base_forward, base_back)
     )
-    z_first = remote_forward(targets_remote, tiles_remote, received, base_forward).reshape(rows, half)
+    z_first = remote_forward(targets_remote, tiles_remote, received, base_forward, False).reshape(rows, half)
     z_first, received = tie((z_first, received))
     z_other = swap(z_first)
     sums = gather_grads(served_ids, flags, received, base_back).reshape(2, rows, half)
@@ -522,7 +519,7 @@
         offset *= 2
     held, supplied = tie((held, supplied))
     held = gather_digit(held, peers)
-    out = remote_forward(targets_remote, tiles_remote, supplied, base_out)
+    out = remote_forward(targets_remote, tiles_remote, supplied, base_out, True)
     held, out = tie((held, out))
     scale = float(rows * peers) ** (-0.5)
     grad_in, grad_out = finish_weights(place, held, half, scale)

time: 124 us -> 123 us (level)
  no operation moved by 1% of the time
where the time goes in v4:
time: 123 us
  waiting for transfers between devices  44.7 us (36%)
  starting transfers between devices  33.1 us (27%)
  Pallas kernels  23.9 us (19%)
  local copies, waits for them, and re-layouts  16 us (13%)
  matrix products  2.6 us (2%)
  other arithmetic  1.32 us (1%)
    all_to_all x2, waiting for transfers between devices, exchange(): lax.all_to_all(sending, 'dom', split_axis=0, concat_axis=0, tiled=True)  24.5 us
    ppermute x8, waiting for transfers between devices, hop(): return lax.ppermute(value, 'dom', [(i, i ^ offset) for i in range(peers)])  20.1 us
    all_to_all x2, starting transfers between devices, exchange(): lax.all_to_all(sending, 'dom', split_axis=0, concat_axis=0, tiled=True)  18.6 us
    pallas_call x6, Pallas kernels, direct(): pl.pallas_call(body, in_specs=[pl.BlockSpec(memory_space=pltpu.SMEM)] * l...  17.9 us
    ppermute x8, starting transfers between devices, hop(): return lax.ppermute(value, 'dom', [(i, i ^ offset) for i in range(peers)])  13.4 us
    unnamed x56, local copies, waits for them, and re-layouts  10.1 us
    pallas_call x3, Pallas kernels, call(): pl.pallas_call(body, grid_spec=pltpu.PrefetchScalarGridSpec(num_scalar_pr...  6.02 us
    concatenate x2, local copies, waits for them, and re-layouts, own_first(): joined = jnp.concatenate([weight, swap(weight)], axis=0)  2.7 us
  transfers between devices with their start and end apart: 15, of which 9 were waited for; matrix products, arithmetic and copies ran while one was open for 9% of the time, Pallas kernels for 14%

profile of v4, /device:TPU:0, one launch (start us, length us, event | category | flops | bytes accessed | tf_op | source)
XLA Modules:
  0.0 122.6 jit_solution(15469553190626062034)
XLA Ops:
  0.6 3.7 %prepare.1 = bf16[16,256,256]{2,1,0:T(8,128)(2,1)} custom-call(s32[16]{0:T(128)} %bitcast.69, s32[16]{0:T(128)} %bitcast.62, bf16[16,128,128]{2,1,0:T(8,128)(2,1)} %bitcast.47, bf16[8,128,256]{2,1,0:T(8,128)(2,1)} %bitcast.53, bf16[8,128,256]{2,1,0:T(8,128)(2,1)} %bitcast.55), custom_call_target="tpu_custom_call" | custom-call | flops 134217728 | bytes 3670016 | tf_op jit(solution)/shard_map/prepare/pallas_call | solution.py:60
  4.3 0.0 copy-start.26
  4.3 0.0 copy-start.1
  4.3 0.0 copy-start.17
  4.3 0.0 copy-start.18
  4.3 8.5 %all-to-all-start = ((bf16[16,256,256]{2,1,0:T(8,128)(2,1)}), bf16[16,256,256]{2,1,0:T(8,128)(2,1)S(1)}, u32[]{:S(2)}, u32[]{:S(2)}) async-start(bf16[16,256,256]{2,1,0:T(8,128)(2,1)} %prepare.1), calls=%async_computation | async-start | bytes 4194304 | tf_op jit(solution)/shard_map/all_to_all | solution.py:450
  12.8 0.1 collective-permute-start
  12.9 0.5 collective-permute-start.1
  13.4 0.1 collective-permute-start.2
  13.5 0.7 constant_dynamic-update-slice_fusion.1
  14.2 1.0 copy-done.3
  15.3 1.0 copy-done.4
  16.3 2.6 %local_both.1 = (f32[8,128,256]{2,1,0:T(8,128)S(1)}, f32[8,128,256]{2,1,0:T(8,128)S(1)}) custom-call(s32[32]{0:T(128)S(1)} %bitcast.65, s32[32]{0:T(128)S(1)} %bitcast.67, bf16[32,128,128]{2,1,0:T(8,128)(2,1)S(1)} %bitcast.50, bf16[8,128,256]{2,1,0:T(8,128)(2,1)S(1)} %bitcast.54, bf16[8,128,256]{2,1,0:T(8,128)(2,1)S(1)} %bitcast.56), custom_call_target="tpu_custom_call" | custom-call | flops 536870912 | bytes 4194304 | tf_op jit(solution)/shard_map/local_both/pallas_call | solution.py:39
  18.9 1.0 copy-done.5
  19.9 1.0 copy-done.20
  20.9 1.0 constant_dynamic-update-slice_fusion.3
  21.8 1.7 %constant_dynamic-update-slice_fusion = bf16[512,512]{1,0:T(8,128)(2,1)} fusion(bf16[512,512]{1,0:T(8,128)(2,1)} %constant_dynamic-update-slice_fusion.1, bf16[256,512]{1,0:T(8,128)(2,1)} %collective-permute-done), kind=kLoop, calls=%fused_computation.16 | loop fusion | bytes 524288 | tf_op jit(solution)/shard_map/concatenate | solution.py:485
  23.5 1.0 constant_dynamic-update-slice_fusion.2
  24.6 1.1 fusion.6
  25.7 0.0 copy-start.7
  25.7 0.1 maximum_select_fusion.1.wo_ref
  25.8 0.9 maximum_select_fusion.wi_ref
  26.7 1.4 %fusion.2 = f32[256,1024]{1,0:T(8,128)S(1)} fusion(bf16[1024,256]{1,0:T(8,128)(2,1)} %collective-permute-done.2, bf16[512,512]{1,0:T(8,128)(2,1)S(1)} %maximum_select_fusion.1.wo_ref), kind=kOutput, calls=%fused_computation.13 | convolution fusion | flops 134217728 | bytes 1703936 | tf_op jit(solution)/shard_map/dot_general | solution.py:18
  28.2 1.1 fusion.1
  29.3 2.0 %copy.16 = bf16[1024,256]{1,0:T(8,128)(2,1)} copy(bf16[1024,256]{0,1:T(8,128)(2,1)} %fusion.1) | data formatting | bytes 1048576 | tf_op jit(solution)/shard_map/convert_element_type | solution.py:495
  31.4 24.5 %all-to-all-done.recv_hbm.ret_ref = bf16[16,256,256]{2,1,0:T(8,128)(2,1)S(1)} async-done(((bf16[16,256,256]{2,1,0:T(8,128)(2,1)}), bf16[16,256,256]{2,1,0:T(8,128)(2,1)S(1)}, u32[]{:S(2)}, u32[]{:S(2)}) %all-to-all-start) | async-done | bytes 2097184 | tf_op jit(solution)/shard_map/all_to_all | solution.py:450
  55.9 1.2 copy-done.6
  57.1 1.0 remote_forward.2
  58.2 0.0 copy-start.11
  58.2 0.1 collective-permute-start.3
  58.3 0.1 copy-done.21
  58.4 2.0 %gather_grads.1 = bf16[2,8,128,256]{3,2,1,0:T(8,128)(2,1)} custom-call(s32[16]{0:T(128)S(1)} %bitcast.70, s32[16]{0:T(128)S(1)} %bitcast.72, bf16[16,256,256]{2,1,0:T(8,128)(2,1)S(1)} %all-to-all-done.recv_hbm.ret_ref, f32[8,128,256]{2,1,0:T(8,128)S(1)} %copy-done.21), custom_call_target="tpu_custom_call" | custom-call | flops 2147483648 | bytes 4194304 | tf_op jit(solution)/shard_map/gather_grads/pallas_call | solution.py:60
  60.3 0.4 collective-permute-start.4
  60.8 0.0 copy-start.22
  60.8 2.7 %middle.1 = (bf16[8,128,256]{2,1,0:T(8,128)(2,1)S(1)}, bf16[16,128,256]{2,1,0:T(8,128)(2,1)}) custom-call(s32[16]{0:T(128)S(1)} %bitcast.71, s32[16]{0:T(128)S(1)} %bitcast.73, bf16[1024,256]{1,0:T(8,128)(2,1)S(1)} %bitcast.58, bf16[1024,256]{1,0:T(8,128)(2,1)S(1)} %collective-permute-done.3.zo_ref, bf16[512,512]{1,0:T(8,128)(2,1)S(1)} %copy-done.13, ...), custom_call_target="tpu_custom_call" | custom-call | flops 8053063680 | bytes 4194304 | tf_op jit(solution)/shard_map/middle/pallas_call | solution.py:60
  63.4 0.0 copy-start.9
  63.5 0.8 copy-done.9
  64.2 10.2 %all-to-all-start.1 = ((bf16[16,128,256]{2,1,0:T(8,128)(2,1)}), bf16[16,128,256]{2,1,0:T(8,128)(2,1)}, u32[]{:S(2)}, u32[]{:S(2)}) async-start(bf16[16,128,256]{2,1,0:T(8,128)(2,1)} %get-tuple-element.51), calls=%async_computation.1 | async-start | bytes 2097152 | tf_op jit(solution)/shard_map/all_to_all | solution.py:450
  74.5 0.1 pad_add_fusion.place_ref
  74.5 0.0 copy-start.14
  74.6 1.1 copy-done.14
  75.7 1.0 copy-done.23
  76.8 5.3 %backward.1 = (bf16[1024,256]{1,0:T(8,128)(2,1)}, bf16[16,32,512]{2,1,0:T(8,128)(2,1)S(1)}) custom-call(s32[2]{0:T(128)S(1)} %pad_add_fusion.place_ref, bf16[2,1024,256]{2,1,0:T(8,128)(2,1)} %bitcast.14.sm_hbm, bf16[2,1024,256]{2,1,0:T(8,128)(2,1)} %collective-permute-done.4.so_hbm, bf16[1024,256]{1,0:T(8,128)(2,1)S(1)} %copy-done.8, ...), custom_call_target="tpu_custom_call" | custom-call | flops 1879048192 | bytes 5767168 | tf_op jit(solution)/shard_map/backward/pallas_call | solution.py:60
  82.1 1.9 %collective-permute-start.6 = (bf16[4,32,512]{2,1,0:T(8,128)(2,1)S(1)}, bf16[4,32,512]{2,1,0:T(8,128)(2,1)S(1)}, u32[]{:S(2)}, u32[]{:S(2)}) collective-permute-start(bf16[4,32,512]{2,1,0:T(8,128)(2,1)S(1)} %get-tuple-element.61), channel_id=1, source_target_pairs={{0,4},{2,6},{4,0},{6,2},{8,12},{10,14},{12,8},{14,10},{16,20},{18,... | collective-permute-start | bytes 393224 | tf_op jit(solution)/shard_map/ppermute | solution.py:424
  84.0 1.5 %collective-permute-start.5 = (bf16[4,32,512]{2,1,0:T(8,128)(2,1)S(1)}, bf16[4,32,512]{2,1,0:T(8,128)(2,1)S(1)}, u32[]{:S(2)}, u32[]{:S(2)}) collective-permute-start(bf16[4,32,512]{2,1,0:T(8,128)(2,1)S(1)} %get-tuple-element.62), channel_id=1, source_target_pairs={{0,2},{2,0},{4,6},{6,4},{8,10},{10,8},{12,14},{14,12},{16,18},{18,... | collective-permute-start | bytes 393224 | tf_op jit(solution)/shard_map/ppermute | solution.py:424
  85.5 0.2 collective-permute-start.7
  85.7 1.9 %local_forward.1.base_ref = f32[8,128,256]{2,1,0:T(8,128)S(1)} custom-call(s32[32]{0:T(128)S(1)} %bitcast.66, s32[32]{0:T(128)S(1)} %bitcast.68, bf16[32,128,128]{2,1,0:T(8,128)(2,1)S(1)} %bitcast.51, bf16[8,128,256]{2,1,0:T(8,128)(2,1)S(1)} %copy-done.10), custom_call_target="tpu_custom_call" | custom-call | flops 268435456 | bytes 2621440 | tf_op jit(solution)/shard_map/local_forward/pallas_call | solution.py:39
  87.6 1.7 %collective-permute-done.6 = bf16[4,32,512]{2,1,0:T(8,128)(2,1)S(1)} collective-permute-done((bf16[4,32,512]{2,1,0:T(8,128)(2,1)S(1)}, bf16[4,32,512]{2,1,0:T(8,128)(2,1)S(1)}, u32[]{:S(2)}, u32[]{:S(2)}) %collective-permute-start.6) | collective-permute-done | bytes 131104 | tf_op jit(solution)/shard_map/ppermute | solution.py:424
  89.3 5.0 %collective-permute-done.5 = bf16[4,32,512]{2,1,0:T(8,128)(2,1)S(1)} collective-permute-done((bf16[4,32,512]{2,1,0:T(8,128)(2,1)S(1)}, bf16[4,32,512]{2,1,0:T(8,128)(2,1)S(1)}, u32[]{:S(2)}, u32[]{:S(2)}) %collective-permute-start.5) | collective-permute-done | bytes 131104 | tf_op jit(solution)/shard_map/ppermute | solution.py:424
  94.3 3.9 %collective-permute-done.7 = bf16[4,32,512]{2,1,0:T(8,128)(2,1)S(1)} collective-permute-done((bf16[4,32,512]{2,1,0:T(8,128)(2,1)S(1)}, bf16[4,32,512]{2,1,0:T(8,128)(2,1)S(1)}, u32[]{:S(2)}, u32[]{:S(2)}) %collective-permute-start.7) | collective-permute-done | bytes 131104 | tf_op jit(solution)/shard_map/ppermute | solution.py:424
  98.2 0.1 add_convert_fusion.2
  98.2 0.1 collective-permute-start.8
  98.3 5.0 %collective-permute-done.8 = bf16[4,32,512]{2,1,0:T(8,128)(2,1)S(1)} collective-permute-done((bf16[4,32,512]{2,1,0:T(8,128)(2,1)S(1)}, bf16[4,32,512]{2,1,0:T(8,128)(2,1)S(1)}, u32[]{:S(2)}, u32[]{:S(2)}) %collective-permute-start.8) | collective-permute-done | bytes 131104 | tf_op jit(solution)/shard_map/ppermute | solution.py:424
  103.3 6.2 %collective-permute-start.9 = (bf16[4,32,512]{2,1,0:T(8,128)(2,1)S(1)}, bf16[4,32,512]{2,1,0:T(8,128)(2,1)S(1)}, u32[]{:S(2)}, u32[]{:S(2)}) collective-permute-start(bf16[4,32,512]{2,1,0:T(8,128)(2,1)S(1)} %add_convert_fusion.1), channel_id=1, source_target_pairs={{0,16},{2,18},{4,20},{6,22},{8,24},{10,26},{12,28},{14,30},{16,0},... | collective-permute-start | bytes 393224 | tf_op jit(solution)/shard_map/ppermute | solution.py:424
  109.5 3.3 %collective-permute-done.9 = bf16[4,32,512]{2,1,0:T(8,128)(2,1)S(1)} collective-permute-done((bf16[4,32,512]{2,1,0:T(8,128)(2,1)S(1)}, bf16[4,32,512]{2,1,0:T(8,128)(2,1)S(1)}, u32[]{:S(2)}, u32[]{:S(2)}) %collective-permute-start.9) | collective-permute-done | bytes 131104 | tf_op jit(solution)/shard_map/ppermute | solution.py:424
  112.9 1.9 %collective-permute-start.12 = (bf16[4,32,512]{2,1,0:T(8,128)(2,1)S(1)}, bf16[4,32,512]{2,1,0:T(8,128)(2,1)S(1)}, u32[]{:S(2)}, u32[]{:S(2)}) collective-permute-start(bf16[4,32,512]{2,1,0:T(8,128)(2,1)S(1)} %add_convert_fusion), channel_id=1, source_target_pairs={{0,6},{2,4},{4,2},{6,0},{8,14},{10,12},{12,10},{14,8},{16,22},{18,... | collective-permute-start | bytes 393224 | tf_op jit(solution)/shard_map/ppermute | solution.py:424
  114.7 1.3 %collective-permute-start.11 = (bf16[4,32,512]{2,1,0:T(8,128)(2,1)S(1)}, bf16[4,32,512]{2,1,0:T(8,128)(2,1)S(1)}, u32[]{:S(2)}, u32[]{:S(2)}) collective-permute-start(bf16[4,32,512]{2,1,0:T(8,128)(2,1)S(1)} %add_convert_fusion), channel_id=1, source_target_pairs={{0,4},{2,6},{4,0},{6,2},{8,12},{10,14},{12,8},{14,10},{16,20},{18,... | collective-permute-start | bytes 393224 | tf_op jit(solution)/shard_map/ppermute | solution.py:424
  116.0 0.4 collective-permute-start.10
  116.4 3.3 %remote_forward.3 = bf16[8,128,256]{2,1,0:T(8,128)(2,1)} custom-call(s32[16]{0:T(128)S(1)} %bitcast.64, bf16[16,128,128]{2,1,0:T(8,128)(2,1)S(1)} %bitcast.49, bf16[16,128,256]{2,1,0:T(8,128)(2,1)} %all-to-all-done.1.recv_hbm, f32[8,128,256]{2,1,0:T(8,128)S(1)} %local_forward.1.base_ref), custom_call_target="tpu_custom_call" | custom-call | flops 134217728 | bytes 3145728 | tf_op jit(solution)/shard_map/remote_forward/pallas_call | solution.py:60
  119.7 0.2 collective-permute-done.12
  119.9 0.8 collective-permute-done.11
  120.7 0.2 collective-permute-done.10
  121.0 0.1 pad_maximum_fusion
  121.0 1.5 %finish_weights.1 = (f32[256,512]{1,0:T(8,128)}, f32[256,512]{1,0:T(8,128)}) custom-call(s32[2]{0:T(128)S(1)} %pad_add_fusion.place_ref, bf16[16,32,512]{2,1,0:T(8,128)(2,1)S(1)} %bitcast.52), custom_call_target="tpu_custom_call" | custom-call | bytes 1572864 | tf_op jit(solution)/shard_map/finish_weights/pallas_call | solution.py:39
  (46 shorter events, 0.2 us)
Async XLA Ops:
  4.3 8.5 %copy-start.26 = (bf16[256,512]{1,0:T(8,128)(2,1)S(1)}, bf16[256,512]{1,0:T(8,128)(2,1)}, u32[]{:S(2)}) copy-start(bf16[256,512]{1,0:T(8,128)(2,1)} %param.21) | copy-start | bytes 786436
  4.3 9.9 %copy-start.1 = (bf16[1,32,128,128]{3,2,1,0:T(8,128)(2,1)S(1)}, bf16[1,32,128,128]{3,2,1,0:T(8,128)(2,1)}, u32[]{:S(2)}) copy-start(bf16[1,32,128,128]{3,2,1,0:T(8,128)(2,1)} %param.18) | copy-start | bytes 3145732
  4.3 9.9 %copy-start.17 = (s32[1,32]{1,0:T(1,128)S(1)}, s32[1,32]{1,0:T(1,128)}, u32[]{:S(2)}) copy-start(s32[1,32]{1,0:T(1,128)} %param.19) | copy-start | bytes 388
  4.3 9.9 %copy-start.18 = (s32[1,32]{1,0:T(1,128)S(1)}, s32[1,32]{1,0:T(1,128)}, u32[]{:S(2)}) copy-start(s32[1,32]{1,0:T(1,128)} %param.20) | copy-start | bytes 388
  4.3 51.5 %all-to-all-start = ((bf16[16,256,256]{2,1,0:T(8,128)(2,1)}), bf16[16,256,256]{2,1,0:T(8,128)(2,1)S(1)}, u32[]{:S(2)}, u32[]{:S(2)}) async-start(bf16[16,256,256]{2,1,0:T(8,128)(2,1)} %prepare.1), calls=%async_computation | async-start | bytes 4194304 | tf_op jit(solution)/shard_map/all_to_all | solution.py:450
  12.8 9.0 %collective-permute-start = (bf16[256,512]{1,0:T(8,128)(2,1)S(1)}, bf16[256,512]{1,0:T(8,128)(2,1)}, u32[]{:S(2)}, u32[]{:S(2)}) collective-permute-start(bf16[256,512]{1,0:T(8,128)(2,1)S(1)} %copy-done.26), channel_id=1, source_target_pairs={{0,1},{1,0},{2,3},{3,2},{4,5},{5,4},{6,7},{7,6},{8,9},{9,8},{10,11... | collective-permute-start | bytes 786440 | tf_op jit(solution)/shard_map/ppermute | solution.py:454
  12.9 10.6 %collective-permute-start.1 = (bf16[256,512]{1,0:T(8,128)(2,1)}, bf16[256,512]{1,0:T(8,128)(2,1)}, u32[]{:S(2)}, u32[]{:S(2)}) collective-permute-start(bf16[256,512]{1,0:T(8,128)(2,1)} %param.22), channel_id=1, source_target_pairs={{0,1},{1,0},{2,3},{3,2},{4,5},{5,4},{6,7},{7,6},{8,9},{9,8},{10,11... | collective-permute-start | bytes 786440 | tf_op jit(solution)/shard_map/ppermute | solution.py:454
  13.4 13.3 %collective-permute-start.2 = (bf16[1024,256]{1,0:T(8,128)(2,1)}, bf16[1024,256]{1,0:T(8,128)(2,1)}, u32[]{:S(2)}, u32[]{:S(2)}) collective-permute-start(bf16[1024,256]{1,0:T(8,128)(2,1)} %hist_ref.1), channel_id=1, source_target_pairs={{0,1},{1,0},{2,3},{3,2},{4,5},{5,4},{6,7},{7,6},{8,9},{9,8},{10,11... | collective-permute-start | bytes 1572872 | tf_op jit(solution)/shard_map/ppermute | solution.py:454
  14.2 1.0 copy-start.3
  15.2 1.0 copy-start.4
  18.9 1.0 copy-start.5
  19.9 1.0 copy-start.20
  23.5 2.3 %copy-start.25 = (bf16[512,512]{1,0:T(8,128)(2,1)S(1)}, bf16[512,512]{1,0:T(8,128)(2,1)}, u32[]{:S(2)}) copy-start(bf16[512,512]{1,0:T(8,128)(2,1)} %constant_dynamic-update-slice_fusion) | copy-start | bytes 1572868
  25.7 2.5 %copy-start.7 = (bf16[1024,256]{1,0:T(8,128)(2,1)S(1)}, bf16[1024,256]{1,0:T(8,128)(2,1)}, u32[]{:S(2)}) copy-start(bf16[1024,256]{1,0:T(8,128)(2,1)} %hist_ref.1) | copy-start | bytes 1572868
  26.7 29.2 %copy-start = (bf16[1,16,128,128]{3,2,1,0:T(8,128)(2,1)S(1)}, bf16[1,16,128,128]{3,2,1,0:T(8,128)(2,1)}, u32[]{:S(2)}) copy-start(bf16[1,16,128,128]{3,2,1,0:T(8,128)(2,1)} %param.14) | copy-start | bytes 1572868
  26.7 29.2 %copy-start.16 = (s32[1,16]{1,0:T(1,128)S(1)}, s32[1,16]{1,0:T(1,128)}, u32[]{:S(2)}) copy-start(s32[1,16]{1,0:T(1,128)} %param.15) | copy-start | bytes 196
  55.9 1.2 %copy-start.6 = (f32[8,128,256]{2,1,0:T(8,128)S(1)}, f32[8,128,256]{2,1,0:T(8,128)}, u32[]{:S(2)}) copy-start(f32[8,128,256]{2,1,0:T(8,128)} %copy-done.5) | copy-start | bytes 3145732
  57.1 1.1 copy-start.19
  57.1 1.2 %copy-start.21 = (f32[8,128,256]{2,1,0:T(8,128)S(1)}, f32[8,128,256]{2,1,0:T(8,128)}, u32[]{:S(2)}) copy-start(f32[8,128,256]{2,1,0:T(8,128)} %copy-done.20) | copy-start | bytes 3145732
  57.1 1.2 %copy-start.24 = (s32[1,16]{1,0:T(1,128)S(1)}, s32[1,16]{1,0:T(1,128)}, u32[]{:S(2)}) copy-start(s32[1,16]{1,0:T(1,128)} %param.17) | copy-start | bytes 196
  58.2 2.6 %copy-start.11 = (bf16[8,128,256]{2,1,0:T(8,128)(2,1)}, bf16[8,128,256]{2,1,0:T(8,128)(2,1)S(1)}, u32[]{:S(2)}) copy-start(bf16[8,128,256]{2,1,0:T(8,128)(2,1)S(1)} %remote_forward.2) | copy-start | bytes 1572868
  58.2 2.6 %collective-permute-start.3 = (bf16[1024,256]{1,0:T(8,128)(2,1)S(1)}, bf16[1024,256]{1,0:T(8,128)(2,1)S(1)}, u32[]{:S(2)}, u32[]{:S(2)}) collective-permute-start(bf16[1024,256]{1,0:T(8,128)(2,1)S(1)} %bitcast.57), channel_id=1, source_target_pairs={{0,1},{1,0},{2,3},{3,2},{4,5},{5,4},{6,7},{7,6},{8,9},{9,8},{10,11... | collective-permute-start | bytes 1572872 | tf_op jit(solution)/shard_map/ppermute | solution.py:454
  58.4 2.4 %copy-start.13 = (bf16[512,512]{1,0:T(8,128)(2,1)S(1)}, bf16[512,512]{1,0:T(8,128)(2,1)}, u32[]{:S(2)}) copy-start(bf16[512,512]{1,0:T(8,128)(2,1)} %maximum_select_fusion.wi_ref) | copy-start | bytes 1572868
  58.4 2.4 %copy-start.15 = (bf16[1024,256]{1,0:T(8,128)(2,1)S(1)}, bf16[1024,256]{1,0:T(8,128)(2,1)}, u32[]{:S(2)}) copy-start(bf16[1024,256]{1,0:T(8,128)(2,1)} %copy.16) | copy-start | bytes 1572868
  60.3 14.2 %collective-permute-start.4 = (bf16[2,1024,256]{2,1,0:T(8,128)(2,1)}, bf16[2,1024,256]{2,1,0:T(8,128)(2,1)}, u32[]{:S(2)}, u32[]{:S(2)}) collective-permute-start(bf16[2,1024,256]{2,1,0:T(8,128)(2,1)} %bitcast.14.sm_hbm), channel_id=1, source_target_pairs={{0,1},{1,0},{2,3},{3,2},{4,5},{5,4},{6,7},{7,6},{8,9},{9,8},{10,11... | collective-permute-start | bytes 3145736 | tf_op jit(solution)/shard_map/ppermute | solution.py:454
  60.8 2.7 %copy-start.22 = (bf16[1024,256]{1,0:T(8,128)(2,1)}, bf16[1024,256]{1,0:T(8,128)(2,1)S(1)}, u32[]{:S(2)}) copy-start(bf16[1024,256]{1,0:T(8,128)(2,1)S(1)} %collective-permute-done.3.zo_ref) | copy-start | bytes 1572868
  63.4 0.8 copy-start.9
  64.2 10.3 %copy-start.8 = (bf16[1024,256]{1,0:T(8,128)(2,1)S(1)}, bf16[1024,256]{1,0:T(8,128)(2,1)}, u32[]{:S(2)}) copy-start(bf16[1024,256]{1,0:T(8,128)(2,1)} %hist_ref.1) | copy-start | bytes 1572868
  64.2 10.3 %copy-start.12 = (bf16[8,128,256]{2,1,0:T(8,128)(2,1)S(1)}, bf16[8,128,256]{2,1,0:T(8,128)(2,1)}, u32[]{:S(2)}) copy-start(bf16[8,128,256]{2,1,0:T(8,128)(2,1)} %copy-done.11) | copy-start | bytes 1572868
  64.2 48.6 %all-to-all-start.1 = ((bf16[16,128,256]{2,1,0:T(8,128)(2,1)}), bf16[16,128,256]{2,1,0:T(8,128)(2,1)}, u32[]{:S(2)}, u32[]{:S(2)}) async-start(bf16[16,128,256]{2,1,0:T(8,128)(2,1)} %get-tuple-element.51), calls=%async_computation.1 | async-start | bytes 2097152 | tf_op jit(solution)/shard_map/all_to_all | solution.py:450
  74.5 11.1 %copy-start.2 = (bf16[1,32,128,128]{3,2,1,0:T(8,128)(2,1)S(1)}, bf16[1,32,128,128]{3,2,1,0:T(8,128)(2,1)}, u32[]{:S(2)}) copy-start(bf16[1,32,128,128]{3,2,1,0:T(8,128)(2,1)} %param.18) | copy-start | bytes 3145732
  74.5 11.2 %copy-start.10 = (bf16[8,128,256]{2,1,0:T(8,128)(2,1)S(1)}, bf16[8,128,256]{2,1,0:T(8,128)(2,1)}, u32[]{:S(2)}) copy-start(bf16[8,128,256]{2,1,0:T(8,128)(2,1)} %copy-done.9) | copy-start | bytes 1572868
  74.5 1.2 copy-start.14
  75.7 1.0 copy-start.23
  82.1 7.2 %collective-permute-start.6 = (bf16[4,32,512]{2,1,0:T(8,128)(2,1)S(1)}, bf16[4,32,512]{2,1,0:T(8,128)(2,1)S(1)}, u32[]{:S(2)}, u32[]{:S(2)}) collective-permute-start(bf16[4,32,512]{2,1,0:T(8,128)(2,1)S(1)} %get-tuple-element.61), channel_id=1, source_target_pairs={{0,4},{2,6},{4,0},{6,2},{8,12},{10,14},{12,8},{14,10},{16,20},{18,... | collective-permute-start | bytes 393224 | tf_op jit(solution)/shard_map/ppermute | solution.py:424
  84.0 10.2 %collective-permute-start.5 = (bf16[4,32,512]{2,1,0:T(8,128)(2,1)S(1)}, bf16[4,32,512]{2,1,0:T(8,128)(2,1)S(1)}, u32[]{:S(2)}, u32[]{:S(2)}) collective-permute-start(bf16[4,32,512]{2,1,0:T(8,128)(2,1)S(1)} %get-tuple-element.62), channel_id=1, source_target_pairs={{0,2},{2,0},{4,6},{6,4},{8,10},{10,8},{12,14},{14,12},{16,18},{18,... | collective-permute-start | bytes 393224 | tf_op jit(solution)/shard_map/ppermute | solution.py:424
  85.5 12.7 %collective-permute-start.7 = (bf16[4,32,512]{2,1,0:T(8,128)(2,1)S(1)}, bf16[4,32,512]{2,1,0:T(8,128)(2,1)S(1)}, u32[]{:S(2)}, u32[]{:S(2)}) collective-permute-start(bf16[4,32,512]{2,1,0:T(8,128)(2,1)S(1)} %get-tuple-element.63), channel_id=1, source_target_pairs={{0,6},{2,4},{4,2},{6,0},{8,14},{10,12},{12,10},{14,8},{16,22},{18,... | collective-permute-start | bytes 393224 | tf_op jit(solution)/shard_map/ppermute | solution.py:424
  98.2 5.0 %collective-permute-start.8 = (bf16[4,32,512]{2,1,0:T(8,128)(2,1)S(1)}, bf16[4,32,512]{2,1,0:T(8,128)(2,1)S(1)}, u32[]{:S(2)}, u32[]{:S(2)}) collective-permute-start(bf16[4,32,512]{2,1,0:T(8,128)(2,1)S(1)} %add_convert_fusion.2), channel_id=1, source_target_pairs={{0,8},{2,10},{4,12},{6,14},{8,0},{10,2},{12,4},{14,6},{16,24},{18,... | collective-permute-start | bytes 393224 | tf_op jit(solution)/shard_map/ppermute | solution.py:424
  103.3 9.5 %collective-permute-start.9 = (bf16[4,32,512]{2,1,0:T(8,128)(2,1)S(1)}, bf16[4,32,512]{2,1,0:T(8,128)(2,1)S(1)}, u32[]{:S(2)}, u32[]{:S(2)}) collective-permute-start(bf16[4,32,512]{2,1,0:T(8,128)(2,1)S(1)} %add_convert_fusion.1), channel_id=1, source_target_pairs={{0,16},{2,18},{4,20},{6,22},{8,24},{10,26},{12,28},{14,30},{16,0},... | collective-permute-start | bytes 393224 | tf_op jit(solution)/shard_map/ppermute | solution.py:424
  112.9 7.1 %collective-permute-start.12 = (bf16[4,32,512]{2,1,0:T(8,128)(2,1)S(1)}, bf16[4,32,512]{2,1,0:T(8,128)(2,1)S(1)}, u32[]{:S(2)}, u32[]{:S(2)}) collective-permute-start(bf16[4,32,512]{2,1,0:T(8,128)(2,1)S(1)} %add_convert_fusion), channel_id=1, source_target_pairs={{0,6},{2,4},{4,2},{6,0},{8,14},{10,12},{12,10},{14,8},{16,22},{18,... | collective-permute-start | bytes 393224 | tf_op jit(solution)/shard_map/ppermute | solution.py:424
  114.7 6.0 %collective-permute-start.11 = (bf16[4,32,512]{2,1,0:T(8,128)(2,1)S(1)}, bf16[4,32,512]{2,1,0:T(8,128)(2,1)S(1)}, u32[]{:S(2)}, u32[]{:S(2)}) collective-permute-start(bf16[4,32,512]{2,1,0:T(8,128)(2,1)S(1)} %add_convert_fusion), channel_id=1, source_target_pairs={{0,4},{2,6},{4,0},{6,2},{8,12},{10,14},{12,8},{14,10},{16,20},{18,... | collective-permute-start | bytes 393224 | tf_op jit(solution)/shard_map/ppermute | solution.py:424
  116.0 5.0 %collective-permute-start.10 = (bf16[4,32,512]{2,1,0:T(8,128)(2,1)S(1)}, bf16[4,32,512]{2,1,0:T(8,128)(2,1)S(1)}, u32[]{:S(2)}, u32[]{:S(2)}) collective-permute-start(bf16[4,32,512]{2,1,0:T(8,128)(2,1)S(1)} %add_convert_fusion), channel_id=1, source_target_pairs={{0,2},{2,0},{4,6},{6,4},{8,10},{10,8},{12,14},{14,12},{16,18},{18,... | collective-permute-start | bytes 393224 | tf_op jit(solution)/shard_map/ppermute | solution.py:424

commit v5 on v4

--- a/solution.py
+++ b/solution.py
@@ -173,30 +173,6 @@
     )
 
 
-def local_forward(sources, targets, tiles, nodes):
-    many, tile, _ = tiles.shape
-    group = group_of(many)
-
-    def body(src_ref, dst_ref, tiles_ref, nodes_ref, fwd_ref):
-        step = pl.program_id(0)
-
-        @pl.when(step == 0)
-        def _():
-            fwd_ref[...] = jnp.zeros_like(fwd_ref)
-
-        for j in range(group):
-            src = src_ref[step * group + j]
-            dst = dst_ref[step * group + j]
-            fwd_ref[dst] += dot(tiles_ref[j], nodes_ref[src])
-
-    return call(
-        body, (sources, targets), (tiles, nodes), (many // group,),
-        [lead((group, tile, tile)), whole(nodes.shape)],
-        whole(nodes.shape), jax.ShapeDtypeStruct(nodes.shape, F32),
-        flops=2 * many * tile * tile * nodes.shape[2], name="local_forward",
-    )
-
-
 def streamed(received, offset, tile, buffer, sems, group):
     def copy(g):
         part = pl.ds(g * group, group)
@@ -245,13 +221,23 @@
     return pre, 0.5 * jnp.tanh(0.5 * pre) + 0.5
 
 
+def supplied_product(zm_ref, zo_ref, wi_ref, wo_ref, prod_ref):
+    count, tile, half = prod_ref.shape
+    per = 2 if count % 2 == 0 else 1
+    for r in range(count // per):
+        part = slice(r * per * tile, (r + 1) * per * tile)
+        pre, s = layer_one(zm_ref[part], zo_ref[part], wi_ref)
+        prod = dot((pre * s).astype(BF16), wo_ref[:, :half]).astype(BF16)
+        prod_ref[r * per : (r + 1) * per] = prod.reshape(per, tile, half)
+
+
 def middle(ids, flags, z_mine, z_other, w_in, w_out, hist_out):
     rows, half = z_mine.shape
     peers = ids.shape[0]
     count, tile, _ = hist_out.shape
     group = group_of(peers)
 
-    def body(ids_ref, flag_ref, zm_ref, zo_ref, wi_ref, wo_ref, hw_ref, prod_ref, send_hbm, sems):
+    def body(ids_ref, flag_ref, zm_ref, zo_ref, wi_ref, wo_ref, hw_ref, send_hbm, prod_ref, sems):
         def supply(source, p):
             return pltpu.make_async_copy(source.at[ids_ref[p]], send_hbm.at[p], sems.at[p])
 
@@ -270,34 +256,57 @@
                 supply(hw_ref, g * group + j).wait()
 
         each(peers // group, stored)
-        per = 2 if count % 2 == 0 else 1
-        for r in range(count // per):
-            part = slice(r * per * tile, (r + 1) * per * tile)
-            pre, s = layer_one(zm_ref[part], zo_ref[part], wi_ref)
-            prod = dot((pre * s).astype(BF16), wo_ref[:, :half]).astype(BF16)
-            prod_ref[r * per : (r + 1) * per] = prod.reshape(per, tile, half)
+        supplied_product(zm_ref, zo_ref, wi_ref, wo_ref, prod_ref)
         each(peers // group, fresh)
         each(peers // group, finish)
 
     return direct(
         body, (ids, flags), [z_mine, z_other, w_in, w_out, hist_out], [pltpu.VMEM] * 5,
+        [jax.ShapeDtypeStruct((peers, tile, half), BF16)], [pltpu.HBM],
+        [pltpu.VMEM(hist_out.shape, BF16), pltpu.SemaphoreType.DMA((peers,))],
+        flops=120 * rows * half * half, name="middle", vmem=61 * 1024 * 1024,
+    )[0]
+
+
+def local_out(sources, targets, tiles, sums_mine, sums_other, w_in, w_out):
+    many, tile, _ = tiles.shape
+    _, rows, half = sums_mine.shape
+    shape = (rows // tile, tile, half)
+
+    def body(src_ref, dst_ref, tiles_ref, sm_hbm, so_hbm, wi_ref, wo_ref, out_ref, zm_ref, zo_ref, prod_ref, sems):
+        copies = [
+            pltpu.make_async_copy(sm_hbm.at[2], zm_ref, sems.at[0]),
+            pltpu.make_async_copy(so_hbm.at[2], zo_ref, sems.at[1]),
+        ]
+        for copy in copies:
+            copy.start()
+        for copy in copies:
+            copy.wait()
+        supplied_product(zm_ref, zo_ref, wi_ref, wo_ref, prod_ref)
+        out_ref[...] = jnp.zeros_like(out_ref)
+        for k in range(many):
+            out_ref[dst_ref[k]] += dot(tiles_ref[k], prod_ref[src_ref[k]])
+
+    return direct(
+        body, (sources, targets), [tiles, sums_mine, sums_other, w_in, w_out],
+        [pltpu.VMEM] + [pltpu.HBM] * 2 + [pltpu.VMEM] * 2,
+        [jax.ShapeDtypeStruct(shape, F32)], [pltpu.VMEM],
         [
-            jax.ShapeDtypeStruct(hist_out.shape, BF16),
-            jax.ShapeDtypeStruct((peers, tile, half), BF16),
+            pltpu.VMEM((rows, half), BF16), pltpu.VMEM((rows, half), BF16), pltpu.VMEM(shape, BF16),
+            pltpu.SemaphoreType.DMA((2,)),
         ],
-        [pltpu.VMEM, pltpu.HBM],
-        [pltpu.SemaphoreType.DMA((peers,))],
-        flops=120 * rows * half * half, name="middle",
-    )
-
-
-def gather_grads(ids, flags, returned, base):
+        flops=12 * rows * half * half + 2 * many * tile * tile * half, name="local_out",
+    )[0]
+
+
+def gather_grads(ids, flags, returned, base, z_mine):
     peers = returned.shape[0]
     count, tile, width = base.shape
     group = 4 if peers % 4 == 0 else 1
     both = (2,) + base.shape
 
-    def body(ids_ref, flag_ref, ret_ref, base_ref, out_ref, acc_ref):
+    def body(ids_ref, flag_ref, ret_ref, base_ref, z_ref, out_ref, acc_ref):
+        out_ref[2] = z_ref[...]
         acc_ref[0] = base_ref[...]
         acc_ref[1] = jnp.zeros_like(base_ref)
 
@@ -308,11 +317,11 @@
                 acc_ref[side, ids_ref[p]] += ret_ref[p, tile:].astype(F32)
 
         each(peers // group, work)
-        out_ref[...] = acc_ref[...].astype(BF16)
-
-    return direct(
-        body, (ids, flags), [returned, base], [pltpu.VMEM, pltpu.VMEM],
-        [jax.ShapeDtypeStruct(both, BF16)], [pltpu.VMEM], [pltpu.VMEM(both, F32)],
+        out_ref[:2] = acc_ref[...].astype(BF16)
+
+    return direct(
+        body, (ids, flags), [returned, base, z_mine], [pltpu.VMEM] * 3,
+        [jax.ShapeDtypeStruct((3,) + base.shape, BF16)], [pltpu.VMEM], [pltpu.VMEM(both, F32)],
         flops=32 * peers * tile * tile * width, name="gather_grads",
     )[0]
 
@@ -323,13 +332,13 @@
     return row_chunks, col_chunks, total // row_chunks, width // col_chunks
 
 
-def backward(place, sums_mine, sums_other, history, z_mine, z_other, w_in, w_out, peers):
+def backward(place, sums_mine, sums_other, history, w_in, w_out, peers):
     _, rows, half = sums_mine.shape
     row_chunks, col_chunks, chunk_rows, chunk_cols = chunking(peers, 2 * half, 2 * half)
     parts = 4
     span = rows // parts
 
-    def body(place_ref, sm_hbm, so_hbm, hist_ref, zm_ref, zo_ref, wi_ref, wo_ref, gh_hbm, chunk_ref, sm_ref, so_ref, gh_ref, acc_ref, sm_sem, so_sem, gh_sem):
+    def body(place_ref, sm_hbm, so_hbm, hist_ref, wi_ref, wo_ref, gh_hbm, chunk_ref, sm_ref, so_ref, gh_ref, acc_ref, sm_sem, so_sem, gh_sem):
         me, side = place_ref[0], place_ref[1]
         own = pl.ds(pl.multiple_of(side * half, half), half)
         far = pl.ds(pl.multiple_of((1 - side) * half, half), half)
@@ -357,11 +366,11 @@
                 else:
                     acc_ref[rows_, cols] += value
 
-            z, hist = zm_ref[part], hist_ref[part]
-            pre, s = layer_one(z, zo_ref[part], wi_ref)
-            hid = (pre[:, :half] * s[:, :half]).astype(BF16)
             for copy in sums_in(r):
                 copy.wait()
+            z, hist = sm_ref[2, part], hist_ref[part]
+            pre, s = layer_one(z, so_ref[2, part], wi_ref)
+            hid = (pre[:, :half] * s[:, :half]).astype(BF16)
             dh = dot_nt(sm_ref[0, part], wo_ref[:, :half]) + dot_nt(so_ref[0, part], wo_ref[:, half:])
             gh_ref[part] = dh[:, :half].astype(BF16)
             gh_out(r).start()
@@ -378,15 +387,15 @@
             gh_out(r).wait()
 
     return direct(
-        body, (place,), [sums_mine, sums_other, history, z_mine, z_other, w_in, w_out],
-        [pltpu.HBM] * 2 + [pltpu.VMEM] * 5,
+        body, (place,), [sums_mine, sums_other, history, w_in, w_out],
+        [pltpu.HBM] * 2 + [pltpu.VMEM] * 3,
         [
             jax.ShapeDtypeStruct((rows, half), BF16),
             jax.ShapeDtypeStruct((peers, chunk_rows, chunk_cols), BF16),
         ],
         [pltpu.HBM, pltpu.VMEM],
         [
-            pltpu.VMEM(sums_mine.shape, BF16), pltpu.VMEM(sums_mine.shape, BF16),
+            pltpu.VMEM((3, rows, half), BF16), pltpu.VMEM((3, rows, half), BF16),
             pltpu.VMEM((rows, half), BF16), pltpu.VMEM((2 * half, 2 * half), F32),
             pltpu.SemaphoreType.DMA((parts,)), pltpu.SemaphoreType.DMA((parts,)), pltpu.SemaphoreType.DMA((parts,)),
         ],
@@ -397,22 +406,32 @@
 def finish_weights(place, chunks, half, scale):
     peers, chunk_rows, chunk_cols = chunks.shape
     _, col_chunks, _, _ = chunking(peers, 2 * half, 2 * half)
-
-    def body(place_ref, chunk_ref, in_ref, out_ref):
+    steps = 4
+    span = half // steps
+
+    def body(place_ref, chunk_ref, in_hbm, out_hbm, all_ref, sems):
+        def leave(k):
+            target = in_hbm if k < steps else out_hbm
+            return pltpu.make_async_copy(
+                all_ref.at[pl.ds(k * span, span)], target.at[pl.ds(k % steps * span, span)], sems.at[k]
+            )
+
         me = place_ref[0]
+        sent = 0
         for c in range(peers):
             r, k = (c // col_chunks) * chunk_rows, c % col_chunks
             piece = chunk_ref[c ^ me].astype(F32) * scale
-            cols = slice(k * chunk_cols, (k + 1) * chunk_cols)
-            if r < half:
-                in_ref[r : r + chunk_rows, cols] = piece
-            else:
-                out_ref[r - half : r - half + chunk_rows, cols] = piece
+            all_ref[r : r + chunk_rows, k * chunk_cols : (k + 1) * chunk_cols] = piece
+            if k == col_chunks - 1 and (r + chunk_rows) % span == 0:
+                leave(sent).start()
+                sent += 1
+        for k in range(2 * steps):
+            leave(k).wait()
 
     shape = jax.ShapeDtypeStruct((half, 2 * half), F32)
-    return call(
-        body, (place,), (chunks,), (1,), [whole(chunks.shape)],
-        [whole(shape.shape)] * 2, [shape, shape], name="finish_weights",
+    return direct(
+        body, (place,), [chunks], [pltpu.VMEM], [shape, shape], [pltpu.HBM] * 2,
+        [pltpu.VMEM((2 * half, 2 * half), F32), pltpu.SemaphoreType.DMA((2 * steps,))], name="finish_weights",
     )
 
 
@@ -500,17 +519,17 @@
     z_first = remote_forward(targets_remote, tiles_remote, received, base_forward, False).reshape(rows, half)
     z_first, received = tie((z_first, received))
     z_other = swap(z_first)
-    sums = gather_grads(served_ids, flags, received, base_back).reshape(2, rows, half)
+    sums = gather_grads(served_ids, flags, received, base_back, blocks(z_first)).reshape(3, rows, half)
     sums_other = swap(sums)
-    hidden_out, sending = middle(served_ids, flags, z_first, z_other, w_in, w_out, hist_out)
-    sending, sums, z_first, z_other = tie((sending, sums, z_first, z_other))
+    sending = middle(served_ids, flags, z_first, z_other, w_in, w_out, hist_out)
+    sending, sums = tie((sending, sums))
     supplied = exchange(sending)
     grad_hidden, chunks = backward(
-        place, sums, sums_other, history, z_first, z_other, w_in, w_out, peers
+        place, sums, sums_other, history, w_in, w_out, peers
     )
     kept, arrived = scatter_digit(chunks, peers)
-    kept, hidden_out = tie((kept, hidden_out))
-    base_out = local_forward(sources_local, targets_local, tiles_local, hidden_out)
+    kept, sums = tie((kept, sums))
+    base_out = local_out(sources_local, targets_local, tiles_local, sums, sums_other, w_in, w_out)
     kept, base_out = tie((kept, base_out))
     held = add_pieces(kept, arrived)
     offset = digit(peers)

time: 123 us -> 121 us (0.984)
  waiting for transfers between devices: 44.7 us -> 40.2 us
  local copies, waits for them, and re-layouts: 16 us -> 13 us
  starting transfers between devices: 33.1 us -> 35.7 us
  Pallas kernels: 23.9 us -> 26.4 us
    pallas_call x6 -> x8, Pallas kernels: 17.9 us -> 23.8 us  [direct(): pl.pallas_call(body, in_specs=[pl.BlockSpec(memory_space=pltpu.SMEM)] * l...]
    ppermute x8, waiting for transfers between devices: 20.1 us -> 15.7 us  [hop(): return lax.ppermute(value, 'dom', [(i, i ^ offset) for i in range(peers)])]
    pallas_call x3 -> x1, Pallas kernels: 6.02 us -> 2.61 us  [call(): pl.pallas_call(body, grid_spec=pltpu.PrefetchScalarGridSpec(num_scalar_pr...]
    unnamed x56 -> x48, local copies, waits for them, and re-layouts: 10.1 us -> 7.13 us
    ppermute x8, starting transfers between devices: 13.4 us -> 16 us  [hop(): return lax.ppermute(value, 'dom', [(i, i ^ offset) for i in range(peers)])]
  transfers between devices with their start and end apart: 15 -> 15, of which waited for: 9 -> 7; matrix products, arithmetic and copies ran while one was open for 9% -> 10% of each run, Pallas kernels for 14% -> 17%
where the time goes in v5:
time: 121 us; the launch traced here: 120 us
  waiting for transfers between devices  40.2 us (33%)
  starting transfers between devices  35.7 us (30%)
  Pallas kernels  26.4 us (22%)
  local copies, waits for them, and re-layouts  13 us (11%)
  matrix products  2.59 us (2%)
  other arithmetic  1.38 us (1%)
    all_to_all x2, waiting for transfers between devices, exchange(): lax.all_to_all(sending, 'dom', split_axis=0, concat_axis=0, tiled=True)  24.4 us
    pallas_call x8, Pallas kernels, direct(): pl.pallas_call(body, in_specs=[pl.BlockSpec(memory_space=pltpu.SMEM)] * l...  23.8 us
    all_to_all x2, starting transfers between devices, exchange(): lax.all_to_all(sending, 'dom', split_axis=0, concat_axis=0, tiled=True)  18.6 us
    ppermute x8, starting transfers between devices, hop(): return lax.ppermute(value, 'dom', [(i, i ^ offset) for i in range(peers)])  16 us
    ppermute x8, waiting for transfers between devices, hop(): return lax.ppermute(value, 'dom', [(i, i ^ offset) for i in range(peers)])  15.7 us
    unnamed x48, local copies, waits for them, and re-layouts  7.13 us
    concatenate x2, local copies, waits for them, and re-layouts, own_first(): joined = jnp.concatenate([weight, swap(weight)], axis=0)  2.7 us
    pallas_call x1, Pallas kernels, call(): pl.pallas_call(body, grid_spec=pltpu.PrefetchScalarGridSpec(num_scalar_pr...  2.61 us
  transfers between devices with their start and end apart: 15, of which 7 were waited for; matrix products, arithmetic and copies ran while one was open for 10% of the time, Pallas kernels for 17%

profile of v5, /device:TPU:0, one launch (start us, length us, event | category | flops | bytes accessed | tf_op | source)
XLA Modules:
  0.0 120.3 jit_solution(1861192113028839533)
XLA Ops:
  0.6 3.6 %prepare.1 = bf16[16,256,256]{2,1,0:T(8,128)(2,1)} custom-call(s32[16]{0:T(128)} %bitcast.68, s32[16]{0:T(128)} %bitcast.61, bf16[16,128,128]{2,1,0:T(8,128)(2,1)} %bitcast.48, bf16[8,128,256]{2,1,0:T(8,128)(2,1)} %bitcast.54, bf16[8,128,256]{2,1,0:T(8,128)(2,1)} %bitcast.56), custom_call_target="tpu_custom_call" | custom-call | flops 134217728 | bytes 3670016 | tf_op jit(solution)/shard_map/prepare/pallas_call | solution.py:60
  4.2 0.0 copy-start.22
  4.3 0.0 copy-start.1
  4.3 0.0 copy-start.15
  4.3 0.0 copy-start.16
  4.3 8.5 %all-to-all-start = ((bf16[16,256,256]{2,1,0:T(8,128)(2,1)}), bf16[16,256,256]{2,1,0:T(8,128)(2,1)S(1)}, u32[]{:S(2)}, u32[]{:S(2)}) async-start(bf16[16,256,256]{2,1,0:T(8,128)(2,1)} %prepare.1), calls=%async_computation | async-start | bytes 4194304 | tf_op jit(solution)/shard_map/all_to_all | solution.py:469
  12.8 0.1 collective-permute-start
  12.9 0.5 collective-permute-start.1
  13.3 0.1 collective-permute-start.2
  13.4 0.7 constant_dynamic-update-slice_fusion.1
  14.2 1.0 copy-done.5
  15.2 1.0 copy-done.6
  16.2 2.6 %local_both.1 = (f32[8,128,256]{2,1,0:T(8,128)S(1)}, f32[8,128,256]{2,1,0:T(8,128)S(1)}) custom-call(s32[32]{0:T(128)S(1)} %bitcast.64, s32[32]{0:T(128)S(1)} %bitcast.66, bf16[32,128,128]{2,1,0:T(8,128)(2,1)S(1)} %bitcast.51, bf16[8,128,256]{2,1,0:T(8,128)(2,1)S(1)} %bitcast.55, bf16[8,128,256]{2,1,0:T(8,128)(2,1)S(1)} %bitcast.57), custom_call_target="tpu_custom_call" | custom-call | flops 536870912 | bytes 4194304 | tf_op jit(solution)/shard_map/local_both/pallas_call | solution.py:39
  18.9 1.0 copy-done.9
  19.8 1.0 copy-done.18
  20.8 1.0 constant_dynamic-update-slice_fusion.3
  21.8 0.0 collective-permute-done
  21.8 1.7 %constant_dynamic-update-slice_fusion = bf16[512,512]{1,0:T(8,128)(2,1)} fusion(bf16[512,512]{1,0:T(8,128)(2,1)} %constant_dynamic-update-slice_fusion.1, bf16[256,512]{1,0:T(8,128)(2,1)} %collective-permute-done), kind=kLoop, calls=%fused_computation.16 | loop fusion | bytes 524288 | tf_op jit(solution)/shard_map/concatenate | solution.py:504
  23.5 0.0 collective-permute-done.1
  23.5 1.0 constant_dynamic-update-slice_fusion.2
  24.6 1.1 fusion.6
  25.6 0.0 copy-start.11
  25.6 0.1 maximum_select_fusion.1.wo_ref
  25.8 0.0 copy-start.3
  25.8 1.0 maximum_select_fusion.wi_ref
  26.8 1.4 %fusion.2 = f32[256,1024]{1,0:T(8,128)S(1)} fusion(bf16[1024,256]{1,0:T(8,128)(2,1)} %collective-permute-done.2, bf16[512,512]{1,0:T(8,128)(2,1)S(1)} %maximum_select_fusion.1.wo_ref), kind=kOutput, calls=%fused_computation.13 | convolution fusion | flops 134217728 | bytes 1703936 | tf_op jit(solution)/shard_map/dot_general | solution.py:18
  28.2 1.1 fusion.1
  29.4 2.0 %copy.16 = bf16[1024,256]{1,0:T(8,128)(2,1)} copy(bf16[1024,256]{0,1:T(8,128)(2,1)} %fusion.1) | data formatting | bytes 1048576 | tf_op jit(solution)/shard_map/convert_element_type | solution.py:514
  31.4 24.4 %all-to-all-done.recv_hbm.ret_ref = bf16[16,256,256]{2,1,0:T(8,128)(2,1)S(1)} async-done(((bf16[16,256,256]{2,1,0:T(8,128)(2,1)}), bf16[16,256,256]{2,1,0:T(8,128)(2,1)S(1)}, u32[]{:S(2)}, u32[]{:S(2)}) %all-to-all-start) | async-done | bytes 2097184 | tf_op jit(solution)/shard_map/all_to_all | solution.py:469
  55.8 1.2 %copy-done.10 = f32[8,128,256]{2,1,0:T(8,128)S(1)} copy-done((f32[8,128,256]{2,1,0:T(8,128)S(1)}, f32[8,128,256]{2,1,0:T(8,128)}, u32[]{:S(2)}) %copy-start.10) | copy-done | bytes 1048600
  57.1 1.0 remote_forward.2
  58.1 0.0 copy-start.13
  58.1 0.1 collective-permute-start.3
  58.2 0.1 copy-done.19
  58.3 2.2 %gather_grads.1 = bf16[3,8,128,256]{3,2,1,0:T(8,128)(2,1)} custom-call(s32[16]{0:T(128)S(1)} %bitcast.70, s32[16]{0:T(128)S(1)} %bitcast.72, bf16[16,256,256]{2,1,0:T(8,128)(2,1)S(1)} %all-to-all-done.recv_hbm.ret_ref, f32[8,128,256]{2,1,0:T(8,128)S(1)} %copy-done.19, bf16[8,128,256]{2,1,0:T(8,128)(2,1)S(1)} %remote_forward.2), custom_call_target="tpu_custom_call" | custom-call | flops 2147483648 | bytes 5242880 | tf_op jit(solution)/shard_map/gather_grads/pallas_call | solution.py:60
  60.5 0.4 collective-permute-start.4
  60.9 0.0 collective-permute-done.3.zo_ref
  60.9 3.8 %middle.1 = bf16[16,128,256]{2,1,0:T(8,128)(2,1)} custom-call(s32[16]{0:T(128)} %bitcast.69, s32[16]{0:T(128)} %bitcast.71, bf16[1024,256]{1,0:T(8,128)(2,1)} %bitcast.59, bf16[1024,256]{1,0:T(8,128)(2,1)} %collective-permute-done.3.zo_ref, bf16[512,512]{1,0:T(8,128)(2,1)} %maximum_select_fusion.wi_ref, bf16[512,512]{1,0:T(8,128)(2,1)} %copy-done.3, ...), custom_call_target="tpu_custom_call" | custom-call | flops 8053063680 | bytes 3670016 | tf_op jit(solution)/shard_map/middle/pallas_call | solution.py:60
  64.7 0.0 copy-start.4
  64.7 0.0 copy-start.7
  64.7 0.0 copy-start.12
  64.7 10.1 %all-to-all-start.1 = ((bf16[16,128,256]{2,1,0:T(8,128)(2,1)}), bf16[16,128,256]{2,1,0:T(8,128)(2,1)S(1)}, u32[]{:S(2)}, u32[]{:S(2)}) async-start(bf16[16,128,256]{2,1,0:T(8,128)(2,1)} %middle.1), calls=%async_computation.1 | async-start | bytes 2097152 | tf_op jit(solution)/shard_map/all_to_all | solution.py:469
  74.9 0.1 pad_add_fusion.place_ref
  75.0 0.0 collective-permute-done.4.so_hbm
  75.0 5.3 %backward.1 = (bf16[1024,256]{1,0:T(8,128)(2,1)}, bf16[16,32,512]{2,1,0:T(8,128)(2,1)S(1)}) custom-call(s32[2]{0:T(128)S(1)} %pad_add_fusion.place_ref, bf16[3,1024,256]{2,1,0:T(8,128)(2,1)} %bitcast.15.sm_hbm, bf16[3,1024,256]{2,1,0:T(8,128)(2,1)} %collective-permute-done.4.so_hbm, bf16[1024,256]{1,0:T(8,128)(2,1)S(1)} %copy-done.12, ...), custom_call_target="tpu_custom_call" | custom-call | flops 1879048192 | bytes 5767168 | tf_op jit(solution)/shard_map/backward/pallas_call | solution.py:60
  80.4 2.0 %collective-permute-start.6 = (bf16[4,32,512]{2,1,0:T(8,128)(2,1)S(1)}, bf16[4,32,512]{2,1,0:T(8,128)(2,1)S(1)}, u32[]{:S(2)}, u32[]{:S(2)}) collective-permute-start(bf16[4,32,512]{2,1,0:T(8,128)(2,1)S(1)} %get-tuple-element.53), channel_id=1, source_target_pairs={{0,4},{2,6},{4,0},{6,2},{8,12},{10,14},{12,8},{14,10},{16,20},{18,... | collective-permute-start | bytes 393224 | tf_op jit(solution)/shard_map/ppermute | solution.py:443
  82.4 1.5 %collective-permute-start.5 = (bf16[4,32,512]{2,1,0:T(8,128)(2,1)S(1)}, bf16[4,32,512]{2,1,0:T(8,128)(2,1)S(1)}, u32[]{:S(2)}, u32[]{:S(2)}) collective-permute-start(bf16[4,32,512]{2,1,0:T(8,128)(2,1)S(1)} %get-tuple-element.54), channel_id=1, source_target_pairs={{0,2},{2,0},{4,6},{6,4},{8,10},{10,8},{12,14},{14,12},{16,18},{18,... | collective-permute-start | bytes 393224 | tf_op jit(solution)/shard_map/ppermute | solution.py:443
  83.8 0.1 collective-permute-start.7
  84.0 3.7 %local_out.1.base_ref = f32[8,128,256]{2,1,0:T(8,128)S(1)} custom-call(s32[32]{0:T(128)S(1)} %bitcast.65, s32[32]{0:T(128)S(1)} %bitcast.67, bf16[32,128,128]{2,1,0:T(8,128)(2,1)S(1)} %bitcast.52, bf16[3,1024,256]{2,1,0:T(8,128)(2,1)} %bitcast.15.sm_hbm, bf16[3,1024,256]{2,1,0:T(8,128)(2,1)} %collective-permute-done.4.so_hbm, ...), custom_call_target="tpu_custom_call" | custom-call | flops 1073741824 | bytes 6291456 | tf_op jit(solution)/shard_map/local_out/pallas_call | solution.py:60
  87.7 1.0 collective-permute-done.6
  88.7 5.0 %collective-permute-done.5 = bf16[4,32,512]{2,1,0:T(8,128)(2,1)S(1)} collective-permute-done((bf16[4,32,512]{2,1,0:T(8,128)(2,1)S(1)}, bf16[4,32,512]{2,1,0:T(8,128)(2,1)S(1)}, u32[]{:S(2)}, u32[]{:S(2)}) %collective-permute-start.5) | collective-permute-done | bytes 131104 | tf_op jit(solution)/shard_map/ppermute | solution.py:443
  93.7 1.9 %collective-permute-done.7 = bf16[4,32,512]{2,1,0:T(8,128)(2,1)S(1)} collective-permute-done((bf16[4,32,512]{2,1,0:T(8,128)(2,1)S(1)}, bf16[4,32,512]{2,1,0:T(8,128)(2,1)S(1)}, u32[]{:S(2)}, u32[]{:S(2)}) %collective-permute-start.7) | collective-permute-done | bytes 131104 | tf_op jit(solution)/shard_map/ppermute | solution.py:443
  95.6 0.1 add_convert_fusion.2
  95.7 2.3 %collective-permute-start.8 = (bf16[4,32,512]{2,1,0:T(8,128)(2,1)S(1)}, bf16[4,32,512]{2,1,0:T(8,128)(2,1)S(1)}, u32[]{:S(2)}, u32[]{:S(2)}) collective-permute-start(bf16[4,32,512]{2,1,0:T(8,128)(2,1)S(1)} %add_convert_fusion.2), channel_id=1, source_target_pairs={{0,8},{2,10},{4,12},{6,14},{8,0},{10,2},{12,4},{14,6},{16,24},{18,... | collective-permute-start | bytes 393224 | tf_op jit(solution)/shard_map/ppermute | solution.py:443
  97.9 3.2 %collective-permute-done.8 = bf16[4,32,512]{2,1,0:T(8,128)(2,1)S(1)} collective-permute-done((bf16[4,32,512]{2,1,0:T(8,128)(2,1)S(1)}, bf16[4,32,512]{2,1,0:T(8,128)(2,1)S(1)}, u32[]{:S(2)}, u32[]{:S(2)}) %collective-permute-start.8) | collective-permute-done | bytes 131104 | tf_op jit(solution)/shard_map/ppermute | solution.py:443
  101.2 6.7 %collective-permute-start.9 = (bf16[4,32,512]{2,1,0:T(8,128)(2,1)S(1)}, bf16[4,32,512]{2,1,0:T(8,128)(2,1)S(1)}, u32[]{:S(2)}, u32[]{:S(2)}) collective-permute-start(bf16[4,32,512]{2,1,0:T(8,128)(2,1)S(1)} %add_convert_fusion.1), channel_id=1, source_target_pairs={{0,16},{2,18},{4,20},{6,22},{8,24},{10,26},{12,28},{14,30},{16,0},... | collective-permute-start | bytes 393224 | tf_op jit(solution)/shard_map/ppermute | solution.py:443
  107.9 3.3 %collective-permute-done.9 = bf16[4,32,512]{2,1,0:T(8,128)(2,1)S(1)} collective-permute-done((bf16[4,32,512]{2,1,0:T(8,128)(2,1)S(1)}, bf16[4,32,512]{2,1,0:T(8,128)(2,1)S(1)}, u32[]{:S(2)}, u32[]{:S(2)}) %collective-permute-start.9) | collective-permute-done | bytes 131104 | tf_op jit(solution)/shard_map/ppermute | solution.py:443
  111.3 1.3 %collective-permute-start.12 = (bf16[4,32,512]{2,1,0:T(8,128)(2,1)S(1)}, bf16[4,32,512]{2,1,0:T(8,128)(2,1)S(1)}, u32[]{:S(2)}, u32[]{:S(2)}) collective-permute-start(bf16[4,32,512]{2,1,0:T(8,128)(2,1)S(1)} %add_convert_fusion), channel_id=1, source_target_pairs={{0,6},{2,4},{4,2},{6,0},{8,14},{10,12},{12,10},{14,8},{16,22},{18,... | collective-permute-start | bytes 393224 | tf_op jit(solution)/shard_map/ppermute | solution.py:443
  112.6 1.0 collective-permute-start.11
  113.6 1.2 %collective-permute-start.10 = (bf16[4,32,512]{2,1,0:T(8,128)(2,1)S(1)}, bf16[4,32,512]{2,1,0:T(8,128)(2,1)S(1)}, u32[]{:S(2)}, u32[]{:S(2)}) collective-permute-start(bf16[4,32,512]{2,1,0:T(8,128)(2,1)S(1)} %add_convert_fusion), channel_id=1, source_target_pairs={{0,2},{2,0},{4,6},{6,4},{8,10},{10,8},{12,14},{14,12},{16,18},{18,... | collective-permute-start | bytes 393224 | tf_op jit(solution)/shard_map/ppermute | solution.py:443
  114.8 2.5 %remote_forward.3 = bf16[8,128,256]{2,1,0:T(8,128)(2,1)} custom-call(s32[16]{0:T(128)S(1)} %bitcast.63, bf16[16,128,128]{2,1,0:T(8,128)(2,1)S(1)} %bitcast.50, bf16[16,128,256]{2,1,0:T(8,128)(2,1)S(1)} %all-to-all-done.1.recv_hbm, f32[8,128,256]{2,1,0:T(8,128)S(1)} %local_out.1.base_ref), custom_call_target="tpu_custom_call" | custom-call | flops 134217728 | bytes 3145728 | tf_op jit(solution)/shard_map/remote_forward/pallas_call | solution.py:60
  117.3 1.3 %collective-permute-done.11 = bf16[4,32,512]{2,1,0:T(8,128)(2,1)S(1)} collective-permute-done((bf16[4,32,512]{2,1,0:T(8,128)(2,1)S(1)}, bf16[4,32,512]{2,1,0:T(8,128)(2,1)S(1)}, u32[]{:S(2)}, u32[]{:S(2)}) %collective-permute-start.11) | collective-permute-done | bytes 131104 | tf_op jit(solution)/shard_map/ppermute | solution.py:443
  118.6 0.1 pad_maximum_fusion
  118.7 1.6 %finish_weights.1 = (f32[256,512]{1,0:T(8,128)}, f32[256,512]{1,0:T(8,128)}) custom-call(s32[2]{0:T(128)S(1)} %pad_add_fusion.place_ref, bf16[16,32,512]{2,1,0:T(8,128)(2,1)S(1)} %bitcast.53), custom_call_target="tpu_custom_call" | custom-call | bytes 1572864 | tf_op jit(solution)/shard_map/finish_weights/pallas_call | solution.py:60
  (38 shorter events, 0.2 us)
Async XLA Ops:
  4.2 8.5 %copy-start.22 = (bf16[256,512]{1,0:T(8,128)(2,1)S(1)}, bf16[256,512]{1,0:T(8,128)(2,1)}, u32[]{:S(2)}) copy-start(bf16[256,512]{1,0:T(8,128)(2,1)} %param.21) | copy-start | bytes 786436
  4.3 9.9 %copy-start.1 = (bf16[1,32,128,128]{3,2,1,0:T(8,128)(2,1)S(1)}, bf16[1,32,128,128]{3,2,1,0:T(8,128)(2,1)}, u32[]{:S(2)}) copy-start(bf16[1,32,128,128]{3,2,1,0:T(8,128)(2,1)} %param.18) | copy-start | bytes 3145732
  4.3 9.9 %copy-start.15 = (s32[1,32]{1,0:T(1,128)S(1)}, s32[1,32]{1,0:T(1,128)}, u32[]{:S(2)}) copy-start(s32[1,32]{1,0:T(1,128)} %param.19) | copy-start | bytes 388
  4.3 9.9 %copy-start.16 = (s32[1,32]{1,0:T(1,128)S(1)}, s32[1,32]{1,0:T(1,128)}, u32[]{:S(2)}) copy-start(s32[1,32]{1,0:T(1,128)} %param.20) | copy-start | bytes 388
  4.3 51.5 %all-to-all-start = ((bf16[16,256,256]{2,1,0:T(8,128)(2,1)}), bf16[16,256,256]{2,1,0:T(8,128)(2,1)S(1)}, u32[]{:S(2)}, u32[]{:S(2)}) async-start(bf16[16,256,256]{2,1,0:T(8,128)(2,1)} %prepare.1), calls=%async_computation | async-start | bytes 4194304 | tf_op jit(solution)/shard_map/all_to_all | solution.py:469
  12.8 9.0 %collective-permute-start = (bf16[256,512]{1,0:T(8,128)(2,1)S(1)}, bf16[256,512]{1,0:T(8,128)(2,1)}, u32[]{:S(2)}, u32[]{:S(2)}) collective-permute-start(bf16[256,512]{1,0:T(8,128)(2,1)S(1)} %copy-done.22), channel_id=1, source_target_pairs={{0,1},{1,0},{2,3},{3,2},{4,5},{5,4},{6,7},{7,6},{8,9},{9,8},{10,11... | collective-permute-start | bytes 786440 | tf_op jit(solution)/shard_map/ppermute | solution.py:473
  12.9 10.6 %collective-permute-start.1 = (bf16[256,512]{1,0:T(8,128)(2,1)}, bf16[256,512]{1,0:T(8,128)(2,1)}, u32[]{:S(2)}, u32[]{:S(2)}) collective-permute-start(bf16[256,512]{1,0:T(8,128)(2,1)} %param.22), channel_id=1, source_target_pairs={{0,1},{1,0},{2,3},{3,2},{4,5},{5,4},{6,7},{7,6},{8,9},{9,8},{10,11... | collective-permute-start | bytes 786440 | tf_op jit(solution)/shard_map/ppermute | solution.py:473
  13.3 13.4 %collective-permute-start.2 = (bf16[1024,256]{1,0:T(8,128)(2,1)}, bf16[1024,256]{1,0:T(8,128)(2,1)}, u32[]{:S(2)}, u32[]{:S(2)}) collective-permute-start(bf16[1024,256]{1,0:T(8,128)(2,1)} %hist_ref.1), channel_id=1, source_target_pairs={{0,1},{1,0},{2,3},{3,2},{4,5},{5,4},{6,7},{7,6},{8,9},{9,8},{10,11... | collective-permute-start | bytes 1572872 | tf_op jit(solution)/shard_map/ppermute | solution.py:473
  14.2 1.0 copy-start.5
  15.2 1.0 copy-start.6
  18.9 1.0 copy-start.9
  19.8 1.0 copy-start.18
  23.5 2.3 %copy-start.21 = (bf16[512,512]{1,0:T(8,128)(2,1)S(1)}, bf16[512,512]{1,0:T(8,128)(2,1)}, u32[]{:S(2)}) copy-start(bf16[512,512]{1,0:T(8,128)(2,1)} %constant_dynamic-update-slice_fusion) | copy-start | bytes 1572868
  25.6 2.6 %copy-start.11 = (bf16[1024,256]{1,0:T(8,128)(2,1)S(1)}, bf16[1024,256]{1,0:T(8,128)(2,1)}, u32[]{:S(2)}) copy-start(bf16[1024,256]{1,0:T(8,128)(2,1)} %hist_ref.1) | copy-start | bytes 1572868
  25.8 3.6 %copy-start.3 = (bf16[512,512]{1,0:T(8,128)(2,1)}, bf16[512,512]{1,0:T(8,128)(2,1)S(1)}, u32[]{:S(2)}) copy-start(bf16[512,512]{1,0:T(8,128)(2,1)S(1)} %maximum_select_fusion.1.wo_ref) | copy-start | bytes 1572868
  26.8 29.1 %copy-start = (bf16[1,16,128,128]{3,2,1,0:T(8,128)(2,1)S(1)}, bf16[1,16,128,128]{3,2,1,0:T(8,128)(2,1)}, u32[]{:S(2)}) copy-start(bf16[1,16,128,128]{3,2,1,0:T(8,128)(2,1)} %param.14) | copy-start | bytes 1572868
  26.8 29.1 %copy-start.14 = (s32[1,16]{1,0:T(1,128)S(1)}, s32[1,16]{1,0:T(1,128)}, u32[]{:S(2)}) copy-start(s32[1,16]{1,0:T(1,128)} %param.15) | copy-start | bytes 196
  55.8 1.2 %copy-start.10 = (f32[8,128,256]{2,1,0:T(8,128)S(1)}, f32[8,128,256]{2,1,0:T(8,128)}, u32[]{:S(2)}) copy-start(f32[8,128,256]{2,1,0:T(8,128)} %copy-done.9) | copy-start | bytes 3145732
  57.1 1.1 copy-start.17
  57.1 1.2 %copy-start.19 = (f32[8,128,256]{2,1,0:T(8,128)S(1)}, f32[8,128,256]{2,1,0:T(8,128)}, u32[]{:S(2)}) copy-start(f32[8,128,256]{2,1,0:T(8,128)} %copy-done.18) | copy-start | bytes 3145732
  57.1 1.2 %copy-start.20 = (s32[1,16]{1,0:T(1,128)S(1)}, s32[1,16]{1,0:T(1,128)}, u32[]{:S(2)}) copy-start(s32[1,16]{1,0:T(1,128)} %param.17) | copy-start | bytes 196
  58.1 2.4 %copy-start.13 = (bf16[8,128,256]{2,1,0:T(8,128)(2,1)}, bf16[8,128,256]{2,1,0:T(8,128)(2,1)S(1)}, u32[]{:S(2)}) copy-start(bf16[8,128,256]{2,1,0:T(8,128)(2,1)S(1)} %remote_forward.2) | copy-start | bytes 1572868
  58.1 2.8 %collective-permute-start.3 = (bf16[1024,256]{1,0:T(8,128)(2,1)S(1)}, bf16[1024,256]{1,0:T(8,128)(2,1)}, u32[]{:S(2)}, u32[]{:S(2)}) collective-permute-start(bf16[1024,256]{1,0:T(8,128)(2,1)S(1)} %bitcast.58), channel_id=1, source_target_pairs={{0,1},{1,0},{2,3},{3,2},{4,5},{5,4},{6,7},{7,6},{8,9},{9,8},{10,11... | collective-permute-start | bytes 1572872 | tf_op jit(solution)/shard_map/ppermute | solution.py:473
  60.5 14.5 %collective-permute-start.4 = (bf16[3,1024,256]{2,1,0:T(8,128)(2,1)}, bf16[3,1024,256]{2,1,0:T(8,128)(2,1)}, u32[]{:S(2)}, u32[]{:S(2)}) collective-permute-start(bf16[3,1024,256]{2,1,0:T(8,128)(2,1)} %bitcast.15.sm_hbm), channel_id=1, source_target_pairs={{0,1},{1,0},{2,3},{3,2},{4,5},{5,4},{6,7},{7,6},{8,9},{9,8},{10,11... | collective-permute-start | bytes 4718600 | tf_op jit(solution)/shard_map/ppermute | solution.py:473
  64.7 10.3 %copy-start.4 = (bf16[512,512]{1,0:T(8,128)(2,1)S(1)}, bf16[512,512]{1,0:T(8,128)(2,1)}, u32[]{:S(2)}) copy-start(bf16[512,512]{1,0:T(8,128)(2,1)} %copy-done.3) | copy-start | bytes 1572868
  64.7 10.3 %copy-start.7 = (bf16[512,512]{1,0:T(8,128)(2,1)S(1)}, bf16[512,512]{1,0:T(8,128)(2,1)}, u32[]{:S(2)}) copy-start(bf16[512,512]{1,0:T(8,128)(2,1)} %maximum_select_fusion.wi_ref) | copy-start | bytes 1572868
  64.7 10.3 %copy-start.12 = (bf16[1024,256]{1,0:T(8,128)(2,1)S(1)}, bf16[1024,256]{1,0:T(8,128)(2,1)}, u32[]{:S(2)}) copy-start(bf16[1024,256]{1,0:T(8,128)(2,1)} %hist_ref.1) | copy-start | bytes 1572868
  64.7 46.5 %all-to-all-start.1 = ((bf16[16,128,256]{2,1,0:T(8,128)(2,1)}), bf16[16,128,256]{2,1,0:T(8,128)(2,1)S(1)}, u32[]{:S(2)}, u32[]{:S(2)}) async-start(bf16[16,128,256]{2,1,0:T(8,128)(2,1)} %middle.1), calls=%async_computation.1 | async-start | bytes 2097152 | tf_op jit(solution)/shard_map/all_to_all | solution.py:469
  75.0 9.0 %copy-start.2 = (bf16[1,32,128,128]{3,2,1,0:T(8,128)(2,1)S(1)}, bf16[1,32,128,128]{3,2,1,0:T(8,128)(2,1)}, u32[]{:S(2)}) copy-start(bf16[1,32,128,128]{3,2,1,0:T(8,128)(2,1)} %param.18) | copy-start | bytes 3145732
  75.0 9.0 %copy-start.8 = (bf16[512,512]{1,0:T(8,128)(2,1)S(1)}, bf16[512,512]{1,0:T(8,128)(2,1)}, u32[]{:S(2)}) copy-start(bf16[512,512]{1,0:T(8,128)(2,1)} %maximum_select_fusion.wi_ref) | copy-start | bytes 1572868
  80.4 8.3 %collective-permute-start.6 = (bf16[4,32,512]{2,1,0:T(8,128)(2,1)S(1)}, bf16[4,32,512]{2,1,0:T(8,128)(2,1)S(1)}, u32[]{:S(2)}, u32[]{:S(2)}) collective-permute-start(bf16[4,32,512]{2,1,0:T(8,128)(2,1)S(1)} %get-tuple-element.53), channel_id=1, source_target_pairs={{0,4},{2,6},{4,0},{6,2},{8,12},{10,14},{12,8},{14,10},{16,20},{18,... | collective-permute-start | bytes 393224 | tf_op jit(solution)/shard_map/ppermute | solution.py:443
  82.4 11.3 %collective-permute-start.5 = (bf16[4,32,512]{2,1,0:T(8,128)(2,1)S(1)}, bf16[4,32,512]{2,1,0:T(8,128)(2,1)S(1)}, u32[]{:S(2)}, u32[]{:S(2)}) collective-permute-start(bf16[4,32,512]{2,1,0:T(8,128)(2,1)S(1)} %get-tuple-element.54), channel_id=1, source_target_pairs={{0,2},{2,0},{4,6},{6,4},{8,10},{10,8},{12,14},{14,12},{16,18},{18,... | collective-permute-start | bytes 393224 | tf_op jit(solution)/shard_map/ppermute | solution.py:443
  83.8 11.8 %collective-permute-start.7 = (bf16[4,32,512]{2,1,0:T(8,128)(2,1)S(1)}, bf16[4,32,512]{2,1,0:T(8,128)(2,1)S(1)}, u32[]{:S(2)}, u32[]{:S(2)}) collective-permute-start(bf16[4,32,512]{2,1,0:T(8,128)(2,1)S(1)} %get-tuple-element.55), channel_id=1, source_target_pairs={{0,6},{2,4},{4,2},{6,0},{8,14},{10,12},{12,10},{14,8},{16,22},{18,... | collective-permute-start | bytes 393224 | tf_op jit(solution)/shard_map/ppermute | solution.py:443
  95.7 5.5 %collective-permute-start.8 = (bf16[4,32,512]{2,1,0:T(8,128)(2,1)S(1)}, bf16[4,32,512]{2,1,0:T(8,128)(2,1)S(1)}, u32[]{:S(2)}, u32[]{:S(2)}) collective-permute-start(bf16[4,32,512]{2,1,0:T(8,128)(2,1)S(1)} %add_convert_fusion.2), channel_id=1, source_target_pairs={{0,8},{2,10},{4,12},{6,14},{8,0},{10,2},{12,4},{14,6},{16,24},{18,... | collective-permute-start | bytes 393224 | tf_op jit(solution)/shard_map/ppermute | solution.py:443
  101.2 10.0 %collective-permute-start.9 = (bf16[4,32,512]{2,1,0:T(8,128)(2,1)S(1)}, bf16[4,32,512]{2,1,0:T(8,128)(2,1)S(1)}, u32[]{:S(2)}, u32[]{:S(2)}) collective-permute-start(bf16[4,32,512]{2,1,0:T(8,128)(2,1)S(1)} %add_convert_fusion.1), channel_id=1, source_target_pairs={{0,16},{2,18},{4,20},{6,22},{8,24},{10,26},{12,28},{14,30},{16,0},... | collective-permute-start | bytes 393224 | tf_op jit(solution)/shard_map/ppermute | solution.py:443
  111.3 6.0 %collective-permute-start.12 = (bf16[4,32,512]{2,1,0:T(8,128)(2,1)S(1)}, bf16[4,32,512]{2,1,0:T(8,128)(2,1)S(1)}, u32[]{:S(2)}, u32[]{:S(2)}) collective-permute-start(bf16[4,32,512]{2,1,0:T(8,128)(2,1)S(1)} %add_convert_fusion), channel_id=1, source_target_pairs={{0,6},{2,4},{4,2},{6,0},{8,14},{10,12},{12,10},{14,8},{16,22},{18,... | collective-permute-start | bytes 393224 | tf_op jit(solution)/shard_map/ppermute | solution.py:443
  112.6 6.1 %collective-permute-start.11 = (bf16[4,32,512]{2,1,0:T(8,128)(2,1)S(1)}, bf16[4,32,512]{2,1,0:T(8,128)(2,1)S(1)}, u32[]{:S(2)}, u32[]{:S(2)}) collective-permute-start(bf16[4,32,512]{2,1,0:T(8,128)(2,1)S(1)} %add_convert_fusion), channel_id=1, source_target_pairs={{0,4},{2,6},{4,0},{6,2},{8,12},{10,14},{12,8},{14,10},{16,20},{18,... | collective-permute-start | bytes 393224 | tf_op jit(solution)/shard_map/ppermute | solution.py:443
  113.6 5.0 %collective-permute-start.10 = (bf16[4,32,512]{2,1,0:T(8,128)(2,1)S(1)}, bf16[4,32,512]{2,1,0:T(8,128)(2,1)S(1)}, u32[]{:S(2)}, u32[]{:S(2)}) collective-permute-start(bf16[4,32,512]{2,1,0:T(8,128)(2,1)S(1)} %add_convert_fusion), channel_id=1, source_target_pairs={{0,2},{2,0},{4,6},{6,4},{8,10},{10,8},{12,14},{14,12},{16,18},{18,... | collective-permute-start | bytes 393224 | tf_op jit(solution)/shard_map/ppermute | solution.py:443

commit v6 on v5

--- a/solution.py
+++ b/solution.py
@@ -335,7 +335,7 @@
 def backward(place, sums_mine, sums_other, history, w_in, w_out, peers):
     _, rows, half = sums_mine.shape
     row_chunks, col_chunks, chunk_rows, chunk_cols = chunking(peers, 2 * half, 2 * half)
-    parts = 4
+    parts = 2
     span = rows // parts
 
     def body(place_ref, sm_hbm, so_hbm, hist_ref, wi_ref, wo_ref, gh_hbm, chunk_ref, sm_ref, so_ref, gh_ref, acc_ref, sm_sem, so_sem, gh_sem):

time: 121 us -> 120 us (level)
  starting transfers between devices: 35.7 us -> 34.4 us
    ppermute x8, starting transfers between devices: 16 us -> 14.7 us  [hop(): return lax.ppermute(value, 'dom', [(i, i ^ offset) for i in range(peers)])]
  transfers between devices with their start and end apart: 15 -> 15, of which waited for: 7 -> 7; matrix products, arithmetic and copies ran while one was open for 10% -> 10% of each run, Pallas kernels for 17% -> 16%
where the time goes in v6:
time: 120 us; the launch traced here: 119 us
  waiting for transfers between devices  41.3 us (34%)
  starting transfers between devices  34.4 us (29%)
  Pallas kernels  25.7 us (21%)
  local copies, waits for them, and re-layouts  13 us (11%)
  matrix products  2.59 us (2%)
  other arithmetic  1.38 us (1%)
    all_to_all x2, waiting for transfers between devices, exchange(): lax.all_to_all(sending, 'dom', split_axis=0, concat_axis=0, tiled=True)  24.4 us
    pallas_call x8, Pallas kernels, direct(): pl.pallas_call(body, in_specs=[pl.BlockSpec(memory_space=pltpu.SMEM)] * l...  23.1 us
    all_to_all x2, starting transfers between devices, exchange(): lax.all_to_all(sending, 'dom', split_axis=0, concat_axis=0, tiled=True)  18.6 us
    ppermute x8, waiting for transfers between devices, hop(): return lax.ppermute(value, 'dom', [(i, i ^ offset) for i in range(peers)])  16.9 us
    ppermute x8, starting transfers between devices, hop(): return lax.ppermute(value, 'dom', [(i, i ^ offset) for i in range(peers)])  14.7 us
    unnamed x48, local copies, waits for them, and re-layouts  7.13 us
    concatenate x2, local copies, waits for them, and re-layouts, own_first(): joined = jnp.concatenate([weight, swap(weight)], axis=0)  2.7 us
    pallas_call x1, Pallas kernels, call(): pl.pallas_call(body, grid_spec=pltpu.PrefetchScalarGridSpec(num_scalar_pr...  2.61 us
  transfers between devices with their start and end apart: 15, of which 7 were waited for; matrix products, arithmetic and copies ran while one was open for 10% of the time, Pallas kernels for 16%

profile of v6, /device:TPU:0, one launch (start us, length us, event | category | flops | bytes accessed | tf_op | source)
XLA Modules:
  0.0 119.4 jit_solution(14111489976974908145)
XLA Ops:
  0.6 3.6 %prepare.1 = bf16[16,256,256]{2,1,0:T(8,128)(2,1)} custom-call(s32[16]{0:T(128)} %bitcast.68, s32[16]{0:T(128)} %bitcast.61, bf16[16,128,128]{2,1,0:T(8,128)(2,1)} %bitcast.48, bf16[8,128,256]{2,1,0:T(8,128)(2,1)} %bitcast.54, bf16[8,128,256]{2,1,0:T(8,128)(2,1)} %bitcast.56), custom_call_target="tpu_custom_call" | custom-call | flops 134217728 | bytes 3670016 | tf_op jit(solution)/shard_map/prepare/pallas_call | solution.py:60
  4.2 0.0 copy-start.22
  4.3 0.0 copy-start.1
  4.3 0.0 copy-start.15
  4.3 0.0 copy-start.16
  4.3 8.5 %all-to-all-start = ((bf16[16,256,256]{2,1,0:T(8,128)(2,1)}), bf16[16,256,256]{2,1,0:T(8,128)(2,1)S(1)}, u32[]{:S(2)}, u32[]{:S(2)}) async-start(bf16[16,256,256]{2,1,0:T(8,128)(2,1)} %prepare.1), calls=%async_computation | async-start | bytes 4194304 | tf_op jit(solution)/shard_map/all_to_all | solution.py:469
  12.8 0.1 collective-permute-start
  12.9 0.5 collective-permute-start.1
  13.3 0.1 collective-permute-start.2
  13.4 0.7 constant_dynamic-update-slice_fusion.1
  14.2 1.0 copy-done.5
  15.2 1.0 copy-done.6
  16.2 2.6 %local_both.1 = (f32[8,128,256]{2,1,0:T(8,128)S(1)}, f32[8,128,256]{2,1,0:T(8,128)S(1)}) custom-call(s32[32]{0:T(128)S(1)} %bitcast.64, s32[32]{0:T(128)S(1)} %bitcast.66, bf16[32,128,128]{2,1,0:T(8,128)(2,1)S(1)} %bitcast.51, bf16[8,128,256]{2,1,0:T(8,128)(2,1)S(1)} %bitcast.55, bf16[8,128,256]{2,1,0:T(8,128)(2,1)S(1)} %bitcast.57), custom_call_target="tpu_custom_call" | custom-call | flops 536870912 | bytes 4194304 | tf_op jit(solution)/shard_map/local_both/pallas_call | solution.py:39
  18.9 1.0 copy-done.9
  19.8 1.0 copy-done.18
  20.8 1.0 constant_dynamic-update-slice_fusion.3
  21.8 1.7 %constant_dynamic-update-slice_fusion = bf16[512,512]{1,0:T(8,128)(2,1)} fusion(bf16[512,512]{1,0:T(8,128)(2,1)} %constant_dynamic-update-slice_fusion.1, bf16[256,512]{1,0:T(8,128)(2,1)} %collective-permute-done), kind=kLoop, calls=%fused_computation.16 | loop fusion | bytes 524288 | tf_op jit(solution)/shard_map/concatenate | solution.py:504
  23.5 0.0 collective-permute-done.1
  23.5 1.0 constant_dynamic-update-slice_fusion.2
  24.6 1.1 fusion.6
  25.6 0.0 copy-start.11
  25.6 0.1 maximum_select_fusion.1.wo_ref
  25.8 0.0 copy-start.3
  25.8 1.0 maximum_select_fusion.wi_ref
  26.8 0.0 collective-permute-done.2
  26.8 1.4 %fusion.2 = f32[256,1024]{1,0:T(8,128)S(1)} fusion(bf16[1024,256]{1,0:T(8,128)(2,1)} %collective-permute-done.2, bf16[512,512]{1,0:T(8,128)(2,1)S(1)} %maximum_select_fusion.1.wo_ref), kind=kOutput, calls=%fused_computation.13 | convolution fusion | flops 134217728 | bytes 1703936 | tf_op jit(solution)/shard_map/dot_general | solution.py:18
  28.2 1.1 fusion.1
  29.4 2.0 %copy.16 = bf16[1024,256]{1,0:T(8,128)(2,1)} copy(bf16[1024,256]{0,1:T(8,128)(2,1)} %fusion.1) | data formatting | bytes 1048576 | tf_op jit(solution)/shard_map/convert_element_type | solution.py:514
  31.4 24.4 %all-to-all-done.recv_hbm.ret_ref = bf16[16,256,256]{2,1,0:T(8,128)(2,1)S(1)} async-done(((bf16[16,256,256]{2,1,0:T(8,128)(2,1)}), bf16[16,256,256]{2,1,0:T(8,128)(2,1)S(1)}, u32[]{:S(2)}, u32[]{:S(2)}) %all-to-all-start) | async-done | bytes 2097184 | tf_op jit(solution)/shard_map/all_to_all | solution.py:469
  55.8 1.2 %copy-done.10 = f32[8,128,256]{2,1,0:T(8,128)S(1)} copy-done((f32[8,128,256]{2,1,0:T(8,128)S(1)}, f32[8,128,256]{2,1,0:T(8,128)}, u32[]{:S(2)}) %copy-start.10) | copy-done | bytes 1048600
  57.1 1.0 remote_forward.2
  58.1 0.0 copy-start.13
  58.1 0.1 collective-permute-start.3
  58.2 0.1 copy-done.19
  58.3 2.2 %gather_grads.1 = bf16[3,8,128,256]{3,2,1,0:T(8,128)(2,1)} custom-call(s32[16]{0:T(128)S(1)} %bitcast.70, s32[16]{0:T(128)S(1)} %bitcast.72, bf16[16,256,256]{2,1,0:T(8,128)(2,1)S(1)} %all-to-all-done.recv_hbm.ret_ref, f32[8,128,256]{2,1,0:T(8,128)S(1)} %copy-done.19, bf16[8,128,256]{2,1,0:T(8,128)(2,1)S(1)} %remote_forward.2), custom_call_target="tpu_custom_call" | custom-call | flops 2147483648 | bytes 5242880 | tf_op jit(solution)/shard_map/gather_grads/pallas_call | solution.py:60
  60.5 0.4 collective-permute-start.4
  60.9 0.0 collective-permute-done.3.zo_ref
  60.9 3.8 %middle.1 = bf16[16,128,256]{2,1,0:T(8,128)(2,1)} custom-call(s32[16]{0:T(128)} %bitcast.69, s32[16]{0:T(128)} %bitcast.71, bf16[1024,256]{1,0:T(8,128)(2,1)} %bitcast.59, bf16[1024,256]{1,0:T(8,128)(2,1)} %collective-permute-done.3.zo_ref, bf16[512,512]{1,0:T(8,128)(2,1)} %maximum_select_fusion.wi_ref, bf16[512,512]{1,0:T(8,128)(2,1)} %copy-done.3, ...), custom_call_target="tpu_custom_call" | custom-call | flops 8053063680 | bytes 3670016 | tf_op jit(solution)/shard_map/middle/pallas_call | solution.py:60
  64.7 0.0 copy-start.4
  64.7 0.0 copy-start.7
  64.7 0.0 copy-start.12
  64.8 10.1 %all-to-all-start.1 = ((bf16[16,128,256]{2,1,0:T(8,128)(2,1)}), bf16[16,128,256]{2,1,0:T(8,128)(2,1)S(1)}, u32[]{:S(2)}, u32[]{:S(2)}) async-start(bf16[16,128,256]{2,1,0:T(8,128)(2,1)} %middle.1), calls=%async_computation.1 | async-start | bytes 2097152 | tf_op jit(solution)/shard_map/all_to_all | solution.py:469
  74.9 0.1 pad_add_fusion.place_ref
  74.9 0.0 collective-permute-done.4.so_hbm
  75.0 4.7 %backward.1 = (bf16[1024,256]{1,0:T(8,128)(2,1)}, bf16[16,32,512]{2,1,0:T(8,128)(2,1)S(1)}) custom-call(s32[2]{0:T(128)S(1)} %pad_add_fusion.place_ref, bf16[3,1024,256]{2,1,0:T(8,128)(2,1)} %bitcast.15.sm_hbm, bf16[3,1024,256]{2,1,0:T(8,128)(2,1)} %collective-permute-done.4.so_hbm, bf16[1024,256]{1,0:T(8,128)(2,1)S(1)} %copy-done.12, ...), custom_call_target="tpu_custom_call" | custom-call | flops 1879048192 | bytes 5767168 | tf_op jit(solution)/shard_map/backward/pallas_call | solution.py:60
  79.7 2.0 %collective-permute-start.6 = (bf16[4,32,512]{2,1,0:T(8,128)(2,1)S(1)}, bf16[4,32,512]{2,1,0:T(8,128)(2,1)S(1)}, u32[]{:S(2)}, u32[]{:S(2)}) collective-permute-start(bf16[4,32,512]{2,1,0:T(8,128)(2,1)S(1)} %get-tuple-element.53), channel_id=1, source_target_pairs={{0,4},{2,6},{4,0},{6,2},{8,12},{10,14},{12,8},{14,10},{16,20},{18,... | collective-permute-start | bytes 393224 | tf_op jit(solution)/shard_map/ppermute | solution.py:443
  81.7 1.5 %collective-permute-start.5 = (bf16[4,32,512]{2,1,0:T(8,128)(2,1)S(1)}, bf16[4,32,512]{2,1,0:T(8,128)(2,1)S(1)}, u32[]{:S(2)}, u32[]{:S(2)}) collective-permute-start(bf16[4,32,512]{2,1,0:T(8,128)(2,1)S(1)} %get-tuple-element.54), channel_id=1, source_target_pairs={{0,2},{2,0},{4,6},{6,4},{8,10},{10,8},{12,14},{14,12},{16,18},{18,... | collective-permute-start | bytes 393224 | tf_op jit(solution)/shard_map/ppermute | solution.py:443
  83.2 0.1 collective-permute-start.7
  83.3 3.7 %local_out.1.base_ref = f32[8,128,256]{2,1,0:T(8,128)S(1)} custom-call(s32[32]{0:T(128)S(1)} %bitcast.65, s32[32]{0:T(128)S(1)} %bitcast.67, bf16[32,128,128]{2,1,0:T(8,128)(2,1)S(1)} %bitcast.52, bf16[3,1024,256]{2,1,0:T(8,128)(2,1)} %bitcast.15.sm_hbm, bf16[3,1024,256]{2,1,0:T(8,128)(2,1)} %collective-permute-done.4.so_hbm, ...), custom_call_target="tpu_custom_call" | custom-call | flops 1073741824 | bytes 6291456 | tf_op jit(solution)/shard_map/local_out/pallas_call | solution.py:60
  87.0 0.6 collective-permute-done.6
  87.6 5.6 %collective-permute-done.5 = bf16[4,32,512]{2,1,0:T(8,128)(2,1)S(1)} collective-permute-done((bf16[4,32,512]{2,1,0:T(8,128)(2,1)S(1)}, bf16[4,32,512]{2,1,0:T(8,128)(2,1)S(1)}, u32[]{:S(2)}, u32[]{:S(2)}) %collective-permute-start.5) | collective-permute-done | bytes 131104 | tf_op jit(solution)/shard_map/ppermute | solution.py:443
  93.2 1.5 %collective-permute-done.7 = bf16[4,32,512]{2,1,0:T(8,128)(2,1)S(1)} collective-permute-done((bf16[4,32,512]{2,1,0:T(8,128)(2,1)S(1)}, bf16[4,32,512]{2,1,0:T(8,128)(2,1)S(1)}, u32[]{:S(2)}, u32[]{:S(2)}) %collective-permute-start.7) | collective-permute-done | bytes 131104 | tf_op jit(solution)/shard_map/ppermute | solution.py:443
  94.7 0.1 add_convert_fusion.2
  94.7 2.7 %collective-permute-start.8 = (bf16[4,32,512]{2,1,0:T(8,128)(2,1)S(1)}, bf16[4,32,512]{2,1,0:T(8,128)(2,1)S(1)}, u32[]{:S(2)}, u32[]{:S(2)}) collective-permute-start(bf16[4,32,512]{2,1,0:T(8,128)(2,1)S(1)} %add_convert_fusion.2), channel_id=1, source_target_pairs={{0,8},{2,10},{4,12},{6,14},{8,0},{10,2},{12,4},{14,6},{16,24},{18,... | collective-permute-start | bytes 393224 | tf_op jit(solution)/shard_map/ppermute | solution.py:443
  97.4 3.4 %collective-permute-done.8 = bf16[4,32,512]{2,1,0:T(8,128)(2,1)S(1)} collective-permute-done((bf16[4,32,512]{2,1,0:T(8,128)(2,1)S(1)}, bf16[4,32,512]{2,1,0:T(8,128)(2,1)S(1)}, u32[]{:S(2)}, u32[]{:S(2)}) %collective-permute-start.8) | collective-permute-done | bytes 131104 | tf_op jit(solution)/shard_map/ppermute | solution.py:443
  100.8 4.9 %collective-permute-start.9 = (bf16[4,32,512]{2,1,0:T(8,128)(2,1)S(1)}, bf16[4,32,512]{2,1,0:T(8,128)(2,1)S(1)}, u32[]{:S(2)}, u32[]{:S(2)}) collective-permute-start(bf16[4,32,512]{2,1,0:T(8,128)(2,1)S(1)} %add_convert_fusion.1), channel_id=1, source_target_pairs={{0,16},{2,18},{4,20},{6,22},{8,24},{10,26},{12,28},{14,30},{16,0},... | collective-permute-start | bytes 393224 | tf_op jit(solution)/shard_map/ppermute | solution.py:443
  105.8 4.3 %collective-permute-done.9 = bf16[4,32,512]{2,1,0:T(8,128)(2,1)S(1)} collective-permute-done((bf16[4,32,512]{2,1,0:T(8,128)(2,1)S(1)}, bf16[4,32,512]{2,1,0:T(8,128)(2,1)S(1)}, u32[]{:S(2)}, u32[]{:S(2)}) %collective-permute-start.9) | collective-permute-done | bytes 131104 | tf_op jit(solution)/shard_map/ppermute | solution.py:443
  110.1 0.0 all-to-all-done.1.recv_hbm
  110.1 2.7 %collective-permute-start.12 = (bf16[4,32,512]{2,1,0:T(8,128)(2,1)S(1)}, bf16[4,32,512]{2,1,0:T(8,128)(2,1)S(1)}, u32[]{:S(2)}, u32[]{:S(2)}) collective-permute-start(bf16[4,32,512]{2,1,0:T(8,128)(2,1)S(1)} %add_convert_fusion), channel_id=1, source_target_pairs={{0,6},{2,4},{4,2},{6,0},{8,14},{10,12},{12,10},{14,8},{16,22},{18,... | collective-permute-start | bytes 393224 | tf_op jit(solution)/shard_map/ppermute | solution.py:443
  112.8 0.9 collective-permute-start.10
  113.6 2.5 %remote_forward.3 = bf16[8,128,256]{2,1,0:T(8,128)(2,1)} custom-call(s32[16]{0:T(128)S(1)} %bitcast.63, bf16[16,128,128]{2,1,0:T(8,128)(2,1)S(1)} %bitcast.50, bf16[16,128,256]{2,1,0:T(8,128)(2,1)S(1)} %all-to-all-done.1.recv_hbm, f32[8,128,256]{2,1,0:T(8,128)S(1)} %local_out.1.base_ref), custom_call_target="tpu_custom_call" | custom-call | flops 134217728 | bytes 3145728 | tf_op jit(solution)/shard_map/remote_forward/pallas_call | solution.py:60
  116.1 1.6 %collective-permute-done.11 = bf16[4,32,512]{2,1,0:T(8,128)(2,1)S(1)} collective-permute-done((bf16[4,32,512]{2,1,0:T(8,128)(2,1)S(1)}, bf16[4,32,512]{2,1,0:T(8,128)(2,1)S(1)}, u32[]{:S(2)}, u32[]{:S(2)}) %collective-permute-start.11) | collective-permute-done | bytes 131104 | tf_op jit(solution)/shard_map/ppermute | solution.py:443
  117.7 0.1 pad_maximum_fusion
  117.8 1.6 %finish_weights.1 = (f32[256,512]{1,0:T(8,128)}, f32[256,512]{1,0:T(8,128)}) custom-call(s32[2]{0:T(128)S(1)} %pad_add_fusion.place_ref, bf16[16,32,512]{2,1,0:T(8,128)(2,1)S(1)} %bitcast.53), custom_call_target="tpu_custom_call" | custom-call | bytes 1572864 | tf_op jit(solution)/shard_map/finish_weights/pallas_call | solution.py:60
  (38 shorter events, 0.2 us)
Async XLA Ops:
  4.2 8.5 %copy-start.22 = (bf16[256,512]{1,0:T(8,128)(2,1)S(1)}, bf16[256,512]{1,0:T(8,128)(2,1)}, u32[]{:S(2)}) copy-start(bf16[256,512]{1,0:T(8,128)(2,1)} %param.21) | copy-start | bytes 786436
  4.3 9.9 %copy-start.1 = (bf16[1,32,128,128]{3,2,1,0:T(8,128)(2,1)S(1)}, bf16[1,32,128,128]{3,2,1,0:T(8,128)(2,1)}, u32[]{:S(2)}) copy-start(bf16[1,32,128,128]{3,2,1,0:T(8,128)(2,1)} %param.18) | copy-start | bytes 3145732
  4.3 9.9 %copy-start.15 = (s32[1,32]{1,0:T(1,128)S(1)}, s32[1,32]{1,0:T(1,128)}, u32[]{:S(2)}) copy-start(s32[1,32]{1,0:T(1,128)} %param.19) | copy-start | bytes 388
  4.3 9.9 %copy-start.16 = (s32[1,32]{1,0:T(1,128)S(1)}, s32[1,32]{1,0:T(1,128)}, u32[]{:S(2)}) copy-start(s32[1,32]{1,0:T(1,128)} %param.20) | copy-start | bytes 388
  4.3 51.5 %all-to-all-start = ((bf16[16,256,256]{2,1,0:T(8,128)(2,1)}), bf16[16,256,256]{2,1,0:T(8,128)(2,1)S(1)}, u32[]{:S(2)}, u32[]{:S(2)}) async-start(bf16[16,256,256]{2,1,0:T(8,128)(2,1)} %prepare.1), calls=%async_computation | async-start | bytes 4194304 | tf_op jit(solution)/shard_map/all_to_all | solution.py:469
  12.8 9.0 %collective-permute-start = (bf16[256,512]{1,0:T(8,128)(2,1)S(1)}, bf16[256,512]{1,0:T(8,128)(2,1)}, u32[]{:S(2)}, u32[]{:S(2)}) collective-permute-start(bf16[256,512]{1,0:T(8,128)(2,1)S(1)} %copy-done.22), channel_id=1, source_target_pairs={{0,1},{1,0},{2,3},{3,2},{4,5},{5,4},{6,7},{7,6},{8,9},{9,8},{10,11... | collective-permute-start | bytes 786440 | tf_op jit(solution)/shard_map/ppermute | solution.py:473
  12.9 10.6 %collective-permute-start.1 = (bf16[256,512]{1,0:T(8,128)(2,1)}, bf16[256,512]{1,0:T(8,128)(2,1)}, u32[]{:S(2)}, u32[]{:S(2)}) collective-permute-start(bf16[256,512]{1,0:T(8,128)(2,1)} %param.22), channel_id=1, source_target_pairs={{0,1},{1,0},{2,3},{3,2},{4,5},{5,4},{6,7},{7,6},{8,9},{9,8},{10,11... | collective-permute-start | bytes 786440 | tf_op jit(solution)/shard_map/ppermute | solution.py:473
  13.3 13.4 %collective-permute-start.2 = (bf16[1024,256]{1,0:T(8,128)(2,1)}, bf16[1024,256]{1,0:T(8,128)(2,1)}, u32[]{:S(2)}, u32[]{:S(2)}) collective-permute-start(bf16[1024,256]{1,0:T(8,128)(2,1)} %hist_ref.1), channel_id=1, source_target_pairs={{0,1},{1,0},{2,3},{3,2},{4,5},{5,4},{6,7},{7,6},{8,9},{9,8},{10,11... | collective-permute-start | bytes 1572872 | tf_op jit(solution)/shard_map/ppermute | solution.py:473
  14.2 1.0 copy-start.5
  15.2 1.0 copy-start.6
  18.9 1.0 copy-start.9
  19.8 1.0 copy-start.18
  23.5 2.3 %copy-start.21 = (bf16[512,512]{1,0:T(8,128)(2,1)S(1)}, bf16[512,512]{1,0:T(8,128)(2,1)}, u32[]{:S(2)}) copy-start(bf16[512,512]{1,0:T(8,128)(2,1)} %constant_dynamic-update-slice_fusion) | copy-start | bytes 1572868
  25.6 2.6 %copy-start.11 = (bf16[1024,256]{1,0:T(8,128)(2,1)S(1)}, bf16[1024,256]{1,0:T(8,128)(2,1)}, u32[]{:S(2)}) copy-start(bf16[1024,256]{1,0:T(8,128)(2,1)} %hist_ref.1) | copy-start | bytes 1572868
  25.8 3.6 %copy-start.3 = (bf16[512,512]{1,0:T(8,128)(2,1)}, bf16[512,512]{1,0:T(8,128)(2,1)S(1)}, u32[]{:S(2)}) copy-start(bf16[512,512]{1,0:T(8,128)(2,1)S(1)} %maximum_select_fusion.1.wo_ref) | copy-start | bytes 1572868
  26.8 29.1 %copy-start = (bf16[1,16,128,128]{3,2,1,0:T(8,128)(2,1)S(1)}, bf16[1,16,128,128]{3,2,1,0:T(8,128)(2,1)}, u32[]{:S(2)}) copy-start(bf16[1,16,128,128]{3,2,1,0:T(8,128)(2,1)} %param.14) | copy-start | bytes 1572868
  26.8 29.1 %copy-start.14 = (s32[1,16]{1,0:T(1,128)S(1)}, s32[1,16]{1,0:T(1,128)}, u32[]{:S(2)}) copy-start(s32[1,16]{1,0:T(1,128)} %param.15) | copy-start | bytes 196
  55.8 1.2 %copy-start.10 = (f32[8,128,256]{2,1,0:T(8,128)S(1)}, f32[8,128,256]{2,1,0:T(8,128)}, u32[]{:S(2)}) copy-start(f32[8,128,256]{2,1,0:T(8,128)} %copy-done.9) | copy-start | bytes 3145732
  57.1 1.1 copy-start.17
  57.1 1.2 %copy-start.19 = (f32[8,128,256]{2,1,0:T(8,128)S(1)}, f32[8,128,256]{2,1,0:T(8,128)}, u32[]{:S(2)}) copy-start(f32[8,128,256]{2,1,0:T(8,128)} %copy-done.18) | copy-start | bytes 3145732
  57.1 1.2 %copy-start.20 = (s32[1,16]{1,0:T(1,128)S(1)}, s32[1,16]{1,0:T(1,128)}, u32[]{:S(2)}) copy-start(s32[1,16]{1,0:T(1,128)} %param.17) | copy-start | bytes 196
  58.1 2.4 %copy-start.13 = (bf16[8,128,256]{2,1,0:T(8,128)(2,1)}, bf16[8,128,256]{2,1,0:T(8,128)(2,1)S(1)}, u32[]{:S(2)}) copy-start(bf16[8,128,256]{2,1,0:T(8,128)(2,1)S(1)} %remote_forward.2) | copy-start | bytes 1572868
  58.1 2.8 %collective-permute-start.3 = (bf16[1024,256]{1,0:T(8,128)(2,1)S(1)}, bf16[1024,256]{1,0:T(8,128)(2,1)}, u32[]{:S(2)}, u32[]{:S(2)}) collective-permute-start(bf16[1024,256]{1,0:T(8,128)(2,1)S(1)} %bitcast.58), channel_id=1, source_target_pairs={{0,1},{1,0},{2,3},{3,2},{4,5},{5,4},{6,7},{7,6},{8,9},{9,8},{10,11... | collective-permute-start | bytes 1572872 | tf_op jit(solution)/shard_map/ppermute | solution.py:473
  60.5 14.4 %collective-permute-start.4 = (bf16[3,1024,256]{2,1,0:T(8,128)(2,1)}, bf16[3,1024,256]{2,1,0:T(8,128)(2,1)}, u32[]{:S(2)}, u32[]{:S(2)}) collective-permute-start(bf16[3,1024,256]{2,1,0:T(8,128)(2,1)} %bitcast.15.sm_hbm), channel_id=1, source_target_pairs={{0,1},{1,0},{2,3},{3,2},{4,5},{5,4},{6,7},{7,6},{8,9},{9,8},{10,11... | collective-permute-start | bytes 4718600 | tf_op jit(solution)/shard_map/ppermute | solution.py:473
  64.7 10.2 %copy-start.4 = (bf16[512,512]{1,0:T(8,128)(2,1)S(1)}, bf16[512,512]{1,0:T(8,128)(2,1)}, u32[]{:S(2)}) copy-start(bf16[512,512]{1,0:T(8,128)(2,1)} %copy-done.3) | copy-start | bytes 1572868
  64.7 10.2 %copy-start.7 = (bf16[512,512]{1,0:T(8,128)(2,1)S(1)}, bf16[512,512]{1,0:T(8,128)(2,1)}, u32[]{:S(2)}) copy-start(bf16[512,512]{1,0:T(8,128)(2,1)} %maximum_select_fusion.wi_ref) | copy-start | bytes 1572868
  64.7 10.2 %copy-start.12 = (bf16[1024,256]{1,0:T(8,128)(2,1)S(1)}, bf16[1024,256]{1,0:T(8,128)(2,1)}, u32[]{:S(2)}) copy-start(bf16[1024,256]{1,0:T(8,128)(2,1)} %hist_ref.1) | copy-start | bytes 1572868
  64.8 45.3 %all-to-all-start.1 = ((bf16[16,128,256]{2,1,0:T(8,128)(2,1)}), bf16[16,128,256]{2,1,0:T(8,128)(2,1)S(1)}, u32[]{:S(2)}, u32[]{:S(2)}) async-start(bf16[16,128,256]{2,1,0:T(8,128)(2,1)} %middle.1), calls=%async_computation.1 | async-start | bytes 2097152 | tf_op jit(solution)/shard_map/all_to_all | solution.py:469
  74.9 8.3 %copy-start.2 = (bf16[1,32,128,128]{3,2,1,0:T(8,128)(2,1)S(1)}, bf16[1,32,128,128]{3,2,1,0:T(8,128)(2,1)}, u32[]{:S(2)}) copy-start(bf16[1,32,128,128]{3,2,1,0:T(8,128)(2,1)} %param.18) | copy-start | bytes 3145732
  74.9 8.3 %copy-start.8 = (bf16[512,512]{1,0:T(8,128)(2,1)S(1)}, bf16[512,512]{1,0:T(8,128)(2,1)}, u32[]{:S(2)}) copy-start(bf16[512,512]{1,0:T(8,128)(2,1)} %maximum_select_fusion.wi_ref) | copy-start | bytes 1572868
  79.7 7.9 %collective-permute-start.6 = (bf16[4,32,512]{2,1,0:T(8,128)(2,1)S(1)}, bf16[4,32,512]{2,1,0:T(8,128)(2,1)S(1)}, u32[]{:S(2)}, u32[]{:S(2)}) collective-permute-start(bf16[4,32,512]{2,1,0:T(8,128)(2,1)S(1)} %get-tuple-element.53), channel_id=1, source_target_pairs={{0,4},{2,6},{4,0},{6,2},{8,12},{10,14},{12,8},{14,10},{16,20},{18,... | collective-permute-start | bytes 393224 | tf_op jit(solution)/shard_map/ppermute | solution.py:443
  81.7 11.5 %collective-permute-start.5 = (bf16[4,32,512]{2,1,0:T(8,128)(2,1)S(1)}, bf16[4,32,512]{2,1,0:T(8,128)(2,1)S(1)}, u32[]{:S(2)}, u32[]{:S(2)}) collective-permute-start(bf16[4,32,512]{2,1,0:T(8,128)(2,1)S(1)} %get-tuple-element.54), channel_id=1, source_target_pairs={{0,2},{2,0},{4,6},{6,4},{8,10},{10,8},{12,14},{14,12},{16,18},{18,... | collective-permute-start | bytes 393224 | tf_op jit(solution)/shard_map/ppermute | solution.py:443
  83.2 11.5 %collective-permute-start.7 = (bf16[4,32,512]{2,1,0:T(8,128)(2,1)S(1)}, bf16[4,32,512]{2,1,0:T(8,128)(2,1)S(1)}, u32[]{:S(2)}, u32[]{:S(2)}) collective-permute-start(bf16[4,32,512]{2,1,0:T(8,128)(2,1)S(1)} %get-tuple-element.55), channel_id=1, source_target_pairs={{0,6},{2,4},{4,2},{6,0},{8,14},{10,12},{12,10},{14,8},{16,22},{18,... | collective-permute-start | bytes 393224 | tf_op jit(solution)/shard_map/ppermute | solution.py:443
  94.7 6.1 %collective-permute-start.8 = (bf16[4,32,512]{2,1,0:T(8,128)(2,1)S(1)}, bf16[4,32,512]{2,1,0:T(8,128)(2,1)S(1)}, u32[]{:S(2)}, u32[]{:S(2)}) collective-permute-start(bf16[4,32,512]{2,1,0:T(8,128)(2,1)S(1)} %add_convert_fusion.2), channel_id=1, source_target_pairs={{0,8},{2,10},{4,12},{6,14},{8,0},{10,2},{12,4},{14,6},{16,24},{18,... | collective-permute-start | bytes 393224 | tf_op jit(solution)/shard_map/ppermute | solution.py:443
  100.8 9.2 %collective-permute-start.9 = (bf16[4,32,512]{2,1,0:T(8,128)(2,1)S(1)}, bf16[4,32,512]{2,1,0:T(8,128)(2,1)S(1)}, u32[]{:S(2)}, u32[]{:S(2)}) collective-permute-start(bf16[4,32,512]{2,1,0:T(8,128)(2,1)S(1)} %add_convert_fusion.1), channel_id=1, source_target_pairs={{0,16},{2,18},{4,20},{6,22},{8,24},{10,26},{12,28},{14,30},{16,0},... | collective-permute-start | bytes 393224 | tf_op jit(solution)/shard_map/ppermute | solution.py:443
  110.1 6.0 %collective-permute-start.12 = (bf16[4,32,512]{2,1,0:T(8,128)(2,1)S(1)}, bf16[4,32,512]{2,1,0:T(8,128)(2,1)S(1)}, u32[]{:S(2)}, u32[]{:S(2)}) collective-permute-start(bf16[4,32,512]{2,1,0:T(8,128)(2,1)S(1)} %add_convert_fusion), channel_id=1, source_target_pairs={{0,6},{2,4},{4,2},{6,0},{8,14},{10,12},{12,10},{14,8},{16,22},{18,... | collective-permute-start | bytes 393224 | tf_op jit(solution)/shard_map/ppermute | solution.py:443
  112.8 5.0 %collective-permute-start.11 = (bf16[4,32,512]{2,1,0:T(8,128)(2,1)S(1)}, bf16[4,32,512]{2,1,0:T(8,128)(2,1)S(1)}, u32[]{:S(2)}, u32[]{:S(2)}) collective-permute-start(bf16[4,32,512]{2,1,0:T(8,128)(2,1)S(1)} %add_convert_fusion), channel_id=1, source_target_pairs={{0,4},{2,6},{4,0},{6,2},{8,12},{10,14},{12,8},{14,10},{16,20},{18,... | collective-permute-start | bytes 393224 | tf_op jit(solution)/shard_map/ppermute | solution.py:443
  112.8 5.0 %collective-permute-start.10 = (bf16[4,32,512]{2,1,0:T(8,128)(2,1)S(1)}, bf16[4,32,512]{2,1,0:T(8,128)(2,1)S(1)}, u32[]{:S(2)}, u32[]{:S(2)}) collective-permute-start(bf16[4,32,512]{2,1,0:T(8,128)(2,1)S(1)} %add_convert_fusion), channel_id=1, source_target_pairs={{0,2},{2,0},{4,6},{6,4},{8,10},{10,8},{12,14},{14,12},{16,18},{18,... | collective-permute-start | bytes 393224 | tf_op jit(solution)/shard_map/ppermute | solution.py:443

commit v7 on v6

--- a/solution.py
+++ b/solution.py
@@ -446,7 +446,7 @@
 def scatter_digit(chunks, peers):
     radix = digit(peers)
     parts = chunks.reshape((-1, radix) + chunks.shape[1:])
-    return parts[:, 0], [hop(parts[:, t], peers, t) for t in range(1, radix)]
+    return parts[:, 0], [hop(parts[:, t], peers, t) for t in reversed(range(1, radix))]
 
 
 def add_pieces(kept, arrived):

time: 120 us -> 120 us (level)
  transfers between devices with their start and end apart: 15 -> 15, of which waited for: 7 -> 8; matrix products, arithmetic and copies ran while one was open for 10% -> 10% of each run, Pallas kernels for 16% -> 16%
where the time goes in v7:
time: 120 us
  waiting for transfers between devices  42.1 us (35%)
  starting transfers between devices  34 us (28%)
  Pallas kernels  25.7 us (21%)
  local copies, waits for them, and re-layouts  13 us (11%)
  matrix products  2.59 us (2%)
  other arithmetic  1.38 us (1%)
    all_to_all x2, waiting for transfers between devices, exchange(): lax.all_to_all(sending, 'dom', split_axis=0, concat_axis=0, tiled=True)  24.4 us
    pallas_call x8, Pallas kernels, direct(): pl.pallas_call(body, in_specs=[pl.BlockSpec(memory_space=pltpu.SMEM)] * l...  23.1 us
    all_to_all x2, starting transfers between devices, exchange(): lax.all_to_all(sending, 'dom', split_axis=0, concat_axis=0, tiled=True)  18.6 us
    ppermute x8, waiting for transfers between devices, hop(): return lax.ppermute(value, 'dom', [(i, i ^ offset) for i in range(peers)])  17.6 us
    ppermute x8, starting transfers between devices, hop(): return lax.ppermute(value, 'dom', [(i, i ^ offset) for i in range(peers)])  14.3 us
    unnamed x48, local copies, waits for them, and re-layouts  7.13 us
    concatenate x2, local copies, waits for them, and re-layouts, own_first(): joined = jnp.concatenate([weight, swap(weight)], axis=0)  2.7 us
    pallas_call x1, Pallas kernels, call(): pl.pallas_call(body, grid_spec=pltpu.PrefetchScalarGridSpec(num_scalar_pr...  2.61 us
  transfers between devices with their start and end apart: 15, of which 8 were waited for; matrix products, arithmetic and copies ran while one was open for 10% of the time, Pallas kernels for 16%

profile of v7, /device:TPU:0, one launch (start us, length us, event | category | flops | bytes accessed | tf_op | source)
XLA Modules:
  0.0 119.8 jit_solution(7258526872319625160)
XLA Ops:
  0.6 3.6 %prepare.1 = bf16[16,256,256]{2,1,0:T(8,128)(2,1)} custom-call(s32[16]{0:T(128)} %bitcast.68, s32[16]{0:T(128)} %bitcast.61, bf16[16,128,128]{2,1,0:T(8,128)(2,1)} %bitcast.48, bf16[8,128,256]{2,1,0:T(8,128)(2,1)} %bitcast.54, bf16[8,128,256]{2,1,0:T(8,128)(2,1)} %bitcast.56), custom_call_target="tpu_custom_call" | custom-call | flops 134217728 | bytes 3670016 | tf_op jit(solution)/shard_map/prepare/pallas_call | solution.py:60
  4.2 0.0 copy-start.22
  4.3 0.0 copy-start.1
  4.3 0.0 copy-start.15
  4.3 0.0 copy-start.16
  4.3 8.5 %all-to-all-start = ((bf16[16,256,256]{2,1,0:T(8,128)(2,1)}), bf16[16,256,256]{2,1,0:T(8,128)(2,1)S(1)}, u32[]{:S(2)}, u32[]{:S(2)}) async-start(bf16[16,256,256]{2,1,0:T(8,128)(2,1)} %prepare.1), calls=%async_computation | async-start | bytes 4194304 | tf_op jit(solution)/shard_map/all_to_all | solution.py:469
  12.8 0.1 collective-permute-start
  12.9 0.5 collective-permute-start.1
  13.3 0.1 collective-permute-start.2
  13.4 0.7 constant_dynamic-update-slice_fusion.1
  14.2 1.0 copy-done.5
  15.2 1.0 copy-done.6
  16.2 2.6 %local_both.1 = (f32[8,128,256]{2,1,0:T(8,128)S(1)}, f32[8,128,256]{2,1,0:T(8,128)S(1)}) custom-call(s32[32]{0:T(128)S(1)} %bitcast.64, s32[32]{0:T(128)S(1)} %bitcast.66, bf16[32,128,128]{2,1,0:T(8,128)(2,1)S(1)} %bitcast.51, bf16[8,128,256]{2,1,0:T(8,128)(2,1)S(1)} %bitcast.55, bf16[8,128,256]{2,1,0:T(8,128)(2,1)S(1)} %bitcast.57), custom_call_target="tpu_custom_call" | custom-call | flops 536870912 | bytes 4194304 | tf_op jit(solution)/shard_map/local_both/pallas_call | solution.py:39
  18.9 1.0 copy-done.9
  19.8 1.0 copy-done.18
  20.8 1.0 constant_dynamic-update-slice_fusion.3
  21.8 0.0 collective-permute-done
  21.8 1.7 %constant_dynamic-update-slice_fusion = bf16[512,512]{1,0:T(8,128)(2,1)} fusion(bf16[512,512]{1,0:T(8,128)(2,1)} %constant_dynamic-update-slice_fusion.1, bf16[256,512]{1,0:T(8,128)(2,1)} %collective-permute-done), kind=kLoop, calls=%fused_computation.16 | loop fusion | bytes 524288 | tf_op jit(solution)/shard_map/concatenate | solution.py:504
  23.5 1.0 constant_dynamic-update-slice_fusion.2
  24.6 1.1 fusion.6
  25.6 0.0 copy-start.11
  25.6 0.1 maximum_select_fusion.1.wo_ref
  25.8 0.0 copy-start.3
  25.8 1.0 maximum_select_fusion.wi_ref
  26.8 0.0 collective-permute-done.2
  26.8 1.4 %fusion.2 = f32[256,1024]{1,0:T(8,128)S(1)} fusion(bf16[1024,256]{1,0:T(8,128)(2,1)} %collective-permute-done.2, bf16[512,512]{1,0:T(8,128)(2,1)S(1)} %maximum_select_fusion.1.wo_ref), kind=kOutput, calls=%fused_computation.13 | convolution fusion | flops 134217728 | bytes 1703936 | tf_op jit(solution)/shard_map/dot_general | solution.py:18
  28.2 1.1 fusion.1
  29.4 2.0 %copy.16 = bf16[1024,256]{1,0:T(8,128)(2,1)} copy(bf16[1024,256]{0,1:T(8,128)(2,1)} %fusion.1) | data formatting | bytes 1048576 | tf_op jit(solution)/shard_map/convert_element_type | solution.py:514
  31.4 24.4 %all-to-all-done.recv_hbm.ret_ref = bf16[16,256,256]{2,1,0:T(8,128)(2,1)S(1)} async-done(((bf16[16,256,256]{2,1,0:T(8,128)(2,1)}), bf16[16,256,256]{2,1,0:T(8,128)(2,1)S(1)}, u32[]{:S(2)}, u32[]{:S(2)}) %all-to-all-start) | async-done | bytes 2097184 | tf_op jit(solution)/shard_map/all_to_all | solution.py:469
  55.8 1.2 %copy-done.10 = f32[8,128,256]{2,1,0:T(8,128)S(1)} copy-done((f32[8,128,256]{2,1,0:T(8,128)S(1)}, f32[8,128,256]{2,1,0:T(8,128)}, u32[]{:S(2)}) %copy-start.10) | copy-done | bytes 1048600
  57.1 1.0 remote_forward.2
  58.1 0.0 copy-start.13
  58.1 0.1 collective-permute-start.3
  58.2 0.1 copy-done.19
  58.3 2.2 %gather_grads.1 = bf16[3,8,128,256]{3,2,1,0:T(8,128)(2,1)} custom-call(s32[16]{0:T(128)S(1)} %bitcast.70, s32[16]{0:T(128)S(1)} %bitcast.72, bf16[16,256,256]{2,1,0:T(8,128)(2,1)S(1)} %all-to-all-done.recv_hbm.ret_ref, f32[8,128,256]{2,1,0:T(8,128)S(1)} %copy-done.19, bf16[8,128,256]{2,1,0:T(8,128)(2,1)S(1)} %remote_forward.2), custom_call_target="tpu_custom_call" | custom-call | flops 2147483648 | bytes 5242880 | tf_op jit(solution)/shard_map/gather_grads/pallas_call | solution.py:60
  60.5 0.4 collective-permute-start.4
  60.9 3.8 %middle.1 = bf16[16,128,256]{2,1,0:T(8,128)(2,1)} custom-call(s32[16]{0:T(128)} %bitcast.69, s32[16]{0:T(128)} %bitcast.71, bf16[1024,256]{1,0:T(8,128)(2,1)} %bitcast.59, bf16[1024,256]{1,0:T(8,128)(2,1)} %collective-permute-done.3.zo_ref, bf16[512,512]{1,0:T(8,128)(2,1)} %maximum_select_fusion.wi_ref, bf16[512,512]{1,0:T(8,128)(2,1)} %copy-done.3, ...), custom_call_target="tpu_custom_call" | custom-call | flops 8053063680 | bytes 3670016 | tf_op jit(solution)/shard_map/middle/pallas_call | solution.py:60
  64.7 0.0 copy-start.4
  64.7 0.0 copy-start.7
  64.7 0.0 copy-start.12
  64.8 10.2 %all-to-all-start.1 = ((bf16[16,128,256]{2,1,0:T(8,128)(2,1)}), bf16[16,128,256]{2,1,0:T(8,128)(2,1)S(1)}, u32[]{:S(2)}, u32[]{:S(2)}) async-start(bf16[16,128,256]{2,1,0:T(8,128)(2,1)} %middle.1), calls=%async_computation.1 | async-start | bytes 2097152 | tf_op jit(solution)/shard_map/all_to_all | solution.py:469
  75.0 0.1 pad_add_fusion.place_ref
  75.0 0.0 collective-permute-done.4.so_hbm
  75.1 4.7 %backward.1 = (bf16[1024,256]{1,0:T(8,128)(2,1)}, bf16[16,32,512]{2,1,0:T(8,128)(2,1)S(1)}) custom-call(s32[2]{0:T(128)S(1)} %pad_add_fusion.place_ref, bf16[3,1024,256]{2,1,0:T(8,128)(2,1)} %bitcast.15.sm_hbm, bf16[3,1024,256]{2,1,0:T(8,128)(2,1)} %collective-permute-done.4.so_hbm, bf16[1024,256]{1,0:T(8,128)(2,1)S(1)} %copy-done.12, ...), custom_call_target="tpu_custom_call" | custom-call | flops 1879048192 | bytes 5767168 | tf_op jit(solution)/shard_map/backward/pallas_call | solution.py:60
  79.8 2.0 %collective-permute-start.6 = (bf16[4,32,512]{2,1,0:T(8,128)(2,1)S(1)}, bf16[4,32,512]{2,1,0:T(8,128)(2,1)S(1)}, u32[]{:S(2)}, u32[]{:S(2)}) collective-permute-start(bf16[4,32,512]{2,1,0:T(8,128)(2,1)S(1)} %get-tuple-element.53), channel_id=1, source_target_pairs={{0,4},{2,6},{4,0},{6,2},{8,12},{10,14},{12,8},{14,10},{16,20},{18,... | collective-permute-start | bytes 393224 | tf_op jit(solution)/shard_map/ppermute | solution.py:443
  81.8 1.5 %collective-permute-start.5 = (bf16[4,32,512]{2,1,0:T(8,128)(2,1)S(1)}, bf16[4,32,512]{2,1,0:T(8,128)(2,1)S(1)}, u32[]{:S(2)}, u32[]{:S(2)}) collective-permute-start(bf16[4,32,512]{2,1,0:T(8,128)(2,1)S(1)} %get-tuple-element.54), channel_id=1, source_target_pairs={{0,6},{2,4},{4,2},{6,0},{8,14},{10,12},{12,10},{14,8},{16,22},{18,... | collective-permute-start | bytes 393224 | tf_op jit(solution)/shard_map/ppermute | solution.py:443
  83.2 0.1 collective-permute-start.7
  83.4 3.7 %local_out.1.base_ref = f32[8,128,256]{2,1,0:T(8,128)S(1)} custom-call(s32[32]{0:T(128)S(1)} %bitcast.65, s32[32]{0:T(128)S(1)} %bitcast.67, bf16[32,128,128]{2,1,0:T(8,128)(2,1)S(1)} %bitcast.52, bf16[3,1024,256]{2,1,0:T(8,128)(2,1)} %bitcast.15.sm_hbm, bf16[3,1024,256]{2,1,0:T(8,128)(2,1)} %collective-permute-done.4.so_hbm, ...), custom_call_target="tpu_custom_call" | custom-call | flops 1073741824 | bytes 6291456 | tf_op jit(solution)/shard_map/local_out/pallas_call | solution.py:60
  87.1 5.1 %collective-permute-done.6 = bf16[4,32,512]{2,1,0:T(8,128)(2,1)S(1)} collective-permute-done((bf16[4,32,512]{2,1,0:T(8,128)(2,1)S(1)}, bf16[4,32,512]{2,1,0:T(8,128)(2,1)S(1)}, u32[]{:S(2)}, u32[]{:S(2)}) %collective-permute-start.6) | collective-permute-done | bytes 131104 | tf_op jit(solution)/shard_map/ppermute | solution.py:443
  92.2 1.6 %collective-permute-done.5 = bf16[4,32,512]{2,1,0:T(8,128)(2,1)S(1)} collective-permute-done((bf16[4,32,512]{2,1,0:T(8,128)(2,1)S(1)}, bf16[4,32,512]{2,1,0:T(8,128)(2,1)S(1)}, u32[]{:S(2)}, u32[]{:S(2)}) %collective-permute-start.5) | collective-permute-done | bytes 131104 | tf_op jit(solution)/shard_map/ppermute | solution.py:443
  93.8 0.9 collective-permute-done.7
  94.7 0.1 add_convert_fusion.2
  94.8 1.8 %collective-permute-start.8 = (bf16[4,32,512]{2,1,0:T(8,128)(2,1)S(1)}, bf16[4,32,512]{2,1,0:T(8,128)(2,1)S(1)}, u32[]{:S(2)}, u32[]{:S(2)}) collective-permute-start(bf16[4,32,512]{2,1,0:T(8,128)(2,1)S(1)} %add_convert_fusion.2), channel_id=1, source_target_pairs={{0,8},{2,10},{4,12},{6,14},{8,0},{10,2},{12,4},{14,6},{16,24},{18,... | collective-permute-start | bytes 393224 | tf_op jit(solution)/shard_map/ppermute | solution.py:443
  96.6 4.3 %collective-permute-done.8 = bf16[4,32,512]{2,1,0:T(8,128)(2,1)S(1)} collective-permute-done((bf16[4,32,512]{2,1,0:T(8,128)(2,1)S(1)}, bf16[4,32,512]{2,1,0:T(8,128)(2,1)S(1)}, u32[]{:S(2)}, u32[]{:S(2)}) %collective-permute-start.8) | collective-permute-done | bytes 131104 | tf_op jit(solution)/shard_map/ppermute | solution.py:443
  100.9 5.4 %collective-permute-start.9 = (bf16[4,32,512]{2,1,0:T(8,128)(2,1)S(1)}, bf16[4,32,512]{2,1,0:T(8,128)(2,1)S(1)}, u32[]{:S(2)}, u32[]{:S(2)}) collective-permute-start(bf16[4,32,512]{2,1,0:T(8,128)(2,1)S(1)} %add_convert_fusion.1), channel_id=1, source_target_pairs={{0,16},{2,18},{4,20},{6,22},{8,24},{10,26},{12,28},{14,30},{16,0},... | collective-permute-start | bytes 393224 | tf_op jit(solution)/shard_map/ppermute | solution.py:443
  106.3 3.7 %collective-permute-done.9 = bf16[4,32,512]{2,1,0:T(8,128)(2,1)S(1)} collective-permute-done((bf16[4,32,512]{2,1,0:T(8,128)(2,1)S(1)}, bf16[4,32,512]{2,1,0:T(8,128)(2,1)S(1)}, u32[]{:S(2)}, u32[]{:S(2)}) %collective-permute-start.9) | collective-permute-done | bytes 131104 | tf_op jit(solution)/shard_map/ppermute | solution.py:443
  110.0 2.4 %collective-permute-start.12 = (bf16[4,32,512]{2,1,0:T(8,128)(2,1)S(1)}, bf16[4,32,512]{2,1,0:T(8,128)(2,1)S(1)}, u32[]{:S(2)}, u32[]{:S(2)}) collective-permute-start(bf16[4,32,512]{2,1,0:T(8,128)(2,1)S(1)} %add_convert_fusion), channel_id=1, source_target_pairs={{0,6},{2,4},{4,2},{6,0},{8,14},{10,12},{12,10},{14,8},{16,22},{18,... | collective-permute-start | bytes 393224 | tf_op jit(solution)/shard_map/ppermute | solution.py:443
  112.5 0.7 collective-permute-start.11
  113.1 0.4 collective-permute-start.10
  113.6 2.5 %remote_forward.3 = bf16[8,128,256]{2,1,0:T(8,128)(2,1)} custom-call(s32[16]{0:T(128)S(1)} %bitcast.63, bf16[16,128,128]{2,1,0:T(8,128)(2,1)S(1)} %bitcast.50, bf16[16,128,256]{2,1,0:T(8,128)(2,1)S(1)} %all-to-all-done.1.recv_hbm, f32[8,128,256]{2,1,0:T(8,128)S(1)} %local_out.1.base_ref), custom_call_target="tpu_custom_call" | custom-call | flops 134217728 | bytes 3145728 | tf_op jit(solution)/shard_map/remote_forward/pallas_call | solution.py:60
  116.1 1.4 %collective-permute-done.11 = bf16[4,32,512]{2,1,0:T(8,128)(2,1)S(1)} collective-permute-done((bf16[4,32,512]{2,1,0:T(8,128)(2,1)S(1)}, bf16[4,32,512]{2,1,0:T(8,128)(2,1)S(1)}, u32[]{:S(2)}, u32[]{:S(2)}) %collective-permute-start.11) | collective-permute-done | bytes 131104 | tf_op jit(solution)/shard_map/ppermute | solution.py:443
  117.4 0.7 collective-permute-done.10
  118.1 0.1 pad_maximum_fusion
  118.2 1.6 %finish_weights.1 = (f32[256,512]{1,0:T(8,128)}, f32[256,512]{1,0:T(8,128)}) custom-call(s32[2]{0:T(128)S(1)} %pad_add_fusion.place_ref, bf16[16,32,512]{2,1,0:T(8,128)(2,1)S(1)} %bitcast.53), custom_call_target="tpu_custom_call" | custom-call | bytes 1572864 | tf_op jit(solution)/shard_map/finish_weights/pallas_call | solution.py:60
  (38 shorter events, 0.2 us)
Async XLA Ops:
  4.2 8.5 %copy-start.22 = (bf16[256,512]{1,0:T(8,128)(2,1)S(1)}, bf16[256,512]{1,0:T(8,128)(2,1)}, u32[]{:S(2)}) copy-start(bf16[256,512]{1,0:T(8,128)(2,1)} %param.21) | copy-start | bytes 786436
  4.3 9.9 %copy-start.1 = (bf16[1,32,128,128]{3,2,1,0:T(8,128)(2,1)S(1)}, bf16[1,32,128,128]{3,2,1,0:T(8,128)(2,1)}, u32[]{:S(2)}) copy-start(bf16[1,32,128,128]{3,2,1,0:T(8,128)(2,1)} %param.18) | copy-start | bytes 3145732
  4.3 9.9 %copy-start.15 = (s32[1,32]{1,0:T(1,128)S(1)}, s32[1,32]{1,0:T(1,128)}, u32[]{:S(2)}) copy-start(s32[1,32]{1,0:T(1,128)} %param.19) | copy-start | bytes 388
  4.3 9.9 %copy-start.16 = (s32[1,32]{1,0:T(1,128)S(1)}, s32[1,32]{1,0:T(1,128)}, u32[]{:S(2)}) copy-start(s32[1,32]{1,0:T(1,128)} %param.20) | copy-start | bytes 388
  4.3 51.5 %all-to-all-start = ((bf16[16,256,256]{2,1,0:T(8,128)(2,1)}), bf16[16,256,256]{2,1,0:T(8,128)(2,1)S(1)}, u32[]{:S(2)}, u32[]{:S(2)}) async-start(bf16[16,256,256]{2,1,0:T(8,128)(2,1)} %prepare.1), calls=%async_computation | async-start | bytes 4194304 | tf_op jit(solution)/shard_map/all_to_all | solution.py:469
  12.8 9.0 %collective-permute-start = (bf16[256,512]{1,0:T(8,128)(2,1)S(1)}, bf16[256,512]{1,0:T(8,128)(2,1)}, u32[]{:S(2)}, u32[]{:S(2)}) collective-permute-start(bf16[256,512]{1,0:T(8,128)(2,1)S(1)} %copy-done.22), channel_id=1, source_target_pairs={{0,1},{1,0},{2,3},{3,2},{4,5},{5,4},{6,7},{7,6},{8,9},{9,8},{10,11... | collective-permute-start | bytes 786440 | tf_op jit(solution)/shard_map/ppermute | solution.py:473
  12.9 10.6 %collective-permute-start.1 = (bf16[256,512]{1,0:T(8,128)(2,1)}, bf16[256,512]{1,0:T(8,128)(2,1)}, u32[]{:S(2)}, u32[]{:S(2)}) collective-permute-start(bf16[256,512]{1,0:T(8,128)(2,1)} %param.22), channel_id=1, source_target_pairs={{0,1},{1,0},{2,3},{3,2},{4,5},{5,4},{6,7},{7,6},{8,9},{9,8},{10,11... | collective-permute-start | bytes 786440 | tf_op jit(solution)/shard_map/ppermute | solution.py:473
  13.3 13.4 %collective-permute-start.2 = (bf16[1024,256]{1,0:T(8,128)(2,1)}, bf16[1024,256]{1,0:T(8,128)(2,1)}, u32[]{:S(2)}, u32[]{:S(2)}) collective-permute-start(bf16[1024,256]{1,0:T(8,128)(2,1)} %hist_ref.1), channel_id=1, source_target_pairs={{0,1},{1,0},{2,3},{3,2},{4,5},{5,4},{6,7},{7,6},{8,9},{9,8},{10,11... | collective-permute-start | bytes 1572872 | tf_op jit(solution)/shard_map/ppermute | solution.py:473
  14.2 1.0 copy-start.5
  15.2 1.0 copy-start.6
  18.9 1.0 copy-start.9
  19.8 1.0 copy-start.18
  23.5 2.3 %copy-start.21 = (bf16[512,512]{1,0:T(8,128)(2,1)S(1)}, bf16[512,512]{1,0:T(8,128)(2,1)}, u32[]{:S(2)}) copy-start(bf16[512,512]{1,0:T(8,128)(2,1)} %constant_dynamic-update-slice_fusion) | copy-start | bytes 1572868
  25.6 2.6 %copy-start.11 = (bf16[1024,256]{1,0:T(8,128)(2,1)S(1)}, bf16[1024,256]{1,0:T(8,128)(2,1)}, u32[]{:S(2)}) copy-start(bf16[1024,256]{1,0:T(8,128)(2,1)} %hist_ref.1) | copy-start | bytes 1572868
  25.8 3.6 %copy-start.3 = (bf16[512,512]{1,0:T(8,128)(2,1)}, bf16[512,512]{1,0:T(8,128)(2,1)S(1)}, u32[]{:S(2)}) copy-start(bf16[512,512]{1,0:T(8,128)(2,1)S(1)} %maximum_select_fusion.1.wo_ref) | copy-start | bytes 1572868
  26.8 29.1 %copy-start = (bf16[1,16,128,128]{3,2,1,0:T(8,128)(2,1)S(1)}, bf16[1,16,128,128]{3,2,1,0:T(8,128)(2,1)}, u32[]{:S(2)}) copy-start(bf16[1,16,128,128]{3,2,1,0:T(8,128)(2,1)} %param.14) | copy-start | bytes 1572868
  26.8 29.1 %copy-start.14 = (s32[1,16]{1,0:T(1,128)S(1)}, s32[1,16]{1,0:T(1,128)}, u32[]{:S(2)}) copy-start(s32[1,16]{1,0:T(1,128)} %param.15) | copy-start | bytes 196
  55.8 1.2 %copy-start.10 = (f32[8,128,256]{2,1,0:T(8,128)S(1)}, f32[8,128,256]{2,1,0:T(8,128)}, u32[]{:S(2)}) copy-start(f32[8,128,256]{2,1,0:T(8,128)} %copy-done.9) | copy-start | bytes 3145732
  57.1 1.1 copy-start.17
  57.1 1.2 %copy-start.19 = (f32[8,128,256]{2,1,0:T(8,128)S(1)}, f32[8,128,256]{2,1,0:T(8,128)}, u32[]{:S(2)}) copy-start(f32[8,128,256]{2,1,0:T(8,128)} %copy-done.18) | copy-start | bytes 3145732
  57.1 1.2 %copy-start.20 = (s32[1,16]{1,0:T(1,128)S(1)}, s32[1,16]{1,0:T(1,128)}, u32[]{:S(2)}) copy-start(s32[1,16]{1,0:T(1,128)} %param.17) | copy-start | bytes 196
  58.1 2.4 %copy-start.13 = (bf16[8,128,256]{2,1,0:T(8,128)(2,1)}, bf16[8,128,256]{2,1,0:T(8,128)(2,1)S(1)}, u32[]{:S(2)}) copy-start(bf16[8,128,256]{2,1,0:T(8,128)(2,1)S(1)} %remote_forward.2) | copy-start | bytes 1572868
  58.1 2.8 %collective-permute-start.3 = (bf16[1024,256]{1,0:T(8,128)(2,1)S(1)}, bf16[1024,256]{1,0:T(8,128)(2,1)}, u32[]{:S(2)}, u32[]{:S(2)}) collective-permute-start(bf16[1024,256]{1,0:T(8,128)(2,1)S(1)} %bitcast.58), channel_id=1, source_target_pairs={{0,1},{1,0},{2,3},{3,2},{4,5},{5,4},{6,7},{7,6},{8,9},{9,8},{10,11... | collective-permute-start | bytes 1572872 | tf_op jit(solution)/shard_map/ppermute | solution.py:473
  60.5 14.5 %collective-permute-start.4 = (bf16[3,1024,256]{2,1,0:T(8,128)(2,1)}, bf16[3,1024,256]{2,1,0:T(8,128)(2,1)}, u32[]{:S(2)}, u32[]{:S(2)}) collective-permute-start(bf16[3,1024,256]{2,1,0:T(8,128)(2,1)} %bitcast.15.sm_hbm), channel_id=1, source_target_pairs={{0,1},{1,0},{2,3},{3,2},{4,5},{5,4},{6,7},{7,6},{8,9},{9,8},{10,11... | collective-permute-start | bytes 4718600 | tf_op jit(solution)/shard_map/ppermute | solution.py:473
  64.7 10.3 %copy-start.4 = (bf16[512,512]{1,0:T(8,128)(2,1)S(1)}, bf16[512,512]{1,0:T(8,128)(2,1)}, u32[]{:S(2)}) copy-start(bf16[512,512]{1,0:T(8,128)(2,1)} %copy-done.3) | copy-start | bytes 1572868
  64.7 10.3 %copy-start.7 = (bf16[512,512]{1,0:T(8,128)(2,1)S(1)}, bf16[512,512]{1,0:T(8,128)(2,1)}, u32[]{:S(2)}) copy-start(bf16[512,512]{1,0:T(8,128)(2,1)} %maximum_select_fusion.wi_ref) | copy-start | bytes 1572868
  64.7 10.3 %copy-start.12 = (bf16[1024,256]{1,0:T(8,128)(2,1)S(1)}, bf16[1024,256]{1,0:T(8,128)(2,1)}, u32[]{:S(2)}) copy-start(bf16[1024,256]{1,0:T(8,128)(2,1)} %hist_ref.1) | copy-start | bytes 1572868
  64.8 45.3 %all-to-all-start.1 = ((bf16[16,128,256]{2,1,0:T(8,128)(2,1)}), bf16[16,128,256]{2,1,0:T(8,128)(2,1)S(1)}, u32[]{:S(2)}, u32[]{:S(2)}) async-start(bf16[16,128,256]{2,1,0:T(8,128)(2,1)} %middle.1), calls=%async_computation.1 | async-start | bytes 2097152 | tf_op jit(solution)/shard_map/all_to_all | solution.py:469
  75.0 8.3 %copy-start.2 = (bf16[1,32,128,128]{3,2,1,0:T(8,128)(2,1)S(1)}, bf16[1,32,128,128]{3,2,1,0:T(8,128)(2,1)}, u32[]{:S(2)}) copy-start(bf16[1,32,128,128]{3,2,1,0:T(8,128)(2,1)} %param.18) | copy-start | bytes 3145732
  75.0 8.3 %copy-start.8 = (bf16[512,512]{1,0:T(8,128)(2,1)S(1)}, bf16[512,512]{1,0:T(8,128)(2,1)}, u32[]{:S(2)}) copy-start(bf16[512,512]{1,0:T(8,128)(2,1)} %maximum_select_fusion.wi_ref) | copy-start | bytes 1572868
  79.8 12.4 %collective-permute-start.6 = (bf16[4,32,512]{2,1,0:T(8,128)(2,1)S(1)}, bf16[4,32,512]{2,1,0:T(8,128)(2,1)S(1)}, u32[]{:S(2)}, u32[]{:S(2)}) collective-permute-start(bf16[4,32,512]{2,1,0:T(8,128)(2,1)S(1)} %get-tuple-element.53), channel_id=1, source_target_pairs={{0,4},{2,6},{4,0},{6,2},{8,12},{10,14},{12,8},{14,10},{16,20},{18,... | collective-permute-start | bytes 393224 | tf_op jit(solution)/shard_map/ppermute | solution.py:443
  81.8 12.0 %collective-permute-start.5 = (bf16[4,32,512]{2,1,0:T(8,128)(2,1)S(1)}, bf16[4,32,512]{2,1,0:T(8,128)(2,1)S(1)}, u32[]{:S(2)}, u32[]{:S(2)}) collective-permute-start(bf16[4,32,512]{2,1,0:T(8,128)(2,1)S(1)} %get-tuple-element.54), channel_id=1, source_target_pairs={{0,6},{2,4},{4,2},{6,0},{8,14},{10,12},{12,10},{14,8},{16,22},{18,... | collective-permute-start | bytes 393224 | tf_op jit(solution)/shard_map/ppermute | solution.py:443
  83.2 11.5 %collective-permute-start.7 = (bf16[4,32,512]{2,1,0:T(8,128)(2,1)S(1)}, bf16[4,32,512]{2,1,0:T(8,128)(2,1)S(1)}, u32[]{:S(2)}, u32[]{:S(2)}) collective-permute-start(bf16[4,32,512]{2,1,0:T(8,128)(2,1)S(1)} %get-tuple-element.55), channel_id=1, source_target_pairs={{0,2},{2,0},{4,6},{6,4},{8,10},{10,8},{12,14},{14,12},{16,18},{18,... | collective-permute-start | bytes 393224 | tf_op jit(solution)/shard_map/ppermute | solution.py:443
  94.8 6.1 %collective-permute-start.8 = (bf16[4,32,512]{2,1,0:T(8,128)(2,1)S(1)}, bf16[4,32,512]{2,1,0:T(8,128)(2,1)S(1)}, u32[]{:S(2)}, u32[]{:S(2)}) collective-permute-start(bf16[4,32,512]{2,1,0:T(8,128)(2,1)S(1)} %add_convert_fusion.2), channel_id=1, source_target_pairs={{0,8},{2,10},{4,12},{6,14},{8,0},{10,2},{12,4},{14,6},{16,24},{18,... | collective-permute-start | bytes 393224 | tf_op jit(solution)/shard_map/ppermute | solution.py:443
  100.9 9.1 %collective-permute-start.9 = (bf16[4,32,512]{2,1,0:T(8,128)(2,1)S(1)}, bf16[4,32,512]{2,1,0:T(8,128)(2,1)S(1)}, u32[]{:S(2)}, u32[]{:S(2)}) collective-permute-start(bf16[4,32,512]{2,1,0:T(8,128)(2,1)S(1)} %add_convert_fusion.1), channel_id=1, source_target_pairs={{0,16},{2,18},{4,20},{6,22},{8,24},{10,26},{12,28},{14,30},{16,0},... | collective-permute-start | bytes 393224 | tf_op jit(solution)/shard_map/ppermute | solution.py:443
  110.0 6.0 %collective-permute-start.12 = (bf16[4,32,512]{2,1,0:T(8,128)(2,1)S(1)}, bf16[4,32,512]{2,1,0:T(8,128)(2,1)S(1)}, u32[]{:S(2)}, u32[]{:S(2)}) collective-permute-start(bf16[4,32,512]{2,1,0:T(8,128)(2,1)S(1)} %add_convert_fusion), channel_id=1, source_target_pairs={{0,6},{2,4},{4,2},{6,0},{8,14},{10,12},{12,10},{14,8},{16,22},{18,... | collective-permute-start | bytes 393224 | tf_op jit(solution)/shard_map/ppermute | solution.py:443
  112.5 5.0 %collective-permute-start.11 = (bf16[4,32,512]{2,1,0:T(8,128)(2,1)S(1)}, bf16[4,32,512]{2,1,0:T(8,128)(2,1)S(1)}, u32[]{:S(2)}, u32[]{:S(2)}) collective-permute-start(bf16[4,32,512]{2,1,0:T(8,128)(2,1)S(1)} %add_convert_fusion), channel_id=1, source_target_pairs={{0,4},{2,6},{4,0},{6,2},{8,12},{10,14},{12,8},{14,10},{16,20},{18,... | collective-permute-start | bytes 393224 | tf_op jit(solution)/shard_map/ppermute | solution.py:443
  113.1 5.0 %collective-permute-start.10 = (bf16[4,32,512]{2,1,0:T(8,128)(2,1)S(1)}, bf16[4,32,512]{2,1,0:T(8,128)(2,1)S(1)}, u32[]{:S(2)}, u32[]{:S(2)}) collective-permute-start(bf16[4,32,512]{2,1,0:T(8,128)(2,1)S(1)} %add_convert_fusion), channel_id=1, source_target_pairs={{0,2},{2,0},{4,6},{6,4},{8,10},{10,8},{12,14},{14,12},{16,18},{18,... | collective-permute-start | bytes 393224 | tf_op jit(solution)/shard_map/ppermute | solution.py:443
